TPU v7x, 128 devices: a whole 4x4x4 slice. The times are simulated.
128 devices in a mesh: dp: 8 (over x_hi, z), tensor: 16 (over x_lo, y, core).
Axes of the slice: x: 4 (x_hi: 2, x_lo: 2; x = x_hi * 2 + x_lo), y: 4, z: 4, core: 2. Of those that a mesh axis runs over, the one named last changes fastest.
Arguments:
- history: bfloat16 [17, 16384, 2048], P(None, ('dp', 'tensor')), may hold values from -6 to 6
- cotangent: bfloat16 [16384, 2048], P(('dp', 'tensor')), may hold values from -6 to 6
- lengths: int32 [8, 4], replicated, may hold values from 0 to 2048, as said below
- mix_gain: float32 [2048], replicated, may hold values from 0.5 to 1.5
- mix_first: float32 [2048, 68], replicated, may hold values from -0.125 to 0.125
- mix_second: float32 [68, 68], replicated, may hold values from -0.3 to 0.3
- mix_bias: float32 [68], replicated, may hold values from -1.8 to 1.8
- gain_query: float32 [2048], replicated, may hold values from 0.5 to 1.5
- gain_key: float32 [2048], replicated, may hold values from 0.5 to 1.5
- gain_value: float32 [2048], replicated, may hold values from 0.5 to 1.5
- gain_mlp: float32 [2048], replicated, may hold values from 0.5 to 1.5
- w_query: bfloat16 [2048, 2048], P(None, 'tensor'), may hold values from -0.125 to 0.125
- w_key: bfloat16 [2048, 2048], P(None, 'tensor'), may hold values from -0.125 to 0.125
- w_value: bfloat16 [2048, 2048], P(None, 'tensor'), may hold values from -0.125 to 0.125
- w_output: bfloat16 [2048, 2048], P('tensor'), may hold values from -1 to 1
- w_expand: bfloat16 [2048, 8192], P(None, 'tensor'), may hold values from -0.125 to 0.125
- w_reduce: bfloat16 [8192, 2048], P('tensor'), may hold values from -0.0625 to 0.0625
Outputs:
- output: bfloat16 [16384, 2048], P(('dp', 'tensor'))
- grad_history: bfloat16 [17, 16384, 2048], P(None, ('dp', 'tensor'))
- grad_mix_gain: float32 [2048], replicated
- grad_mix_first: float32 [2048, 68], replicated
- grad_mix_second: float32 [68, 68], replicated
- grad_mix_bias: float32 [68], replicated
- grad_gain_query: float32 [2048], replicated
- grad_gain_key: float32 [2048], replicated
- grad_gain_value: float32 [2048], replicated
- grad_gain_mlp: float32 [2048], replicated
- grad_w_query: float32 [2048, 2048], P('dp', 'tensor')
- grad_w_key: float32 [2048, 2048], P('dp', 'tensor')
- grad_w_value: float32 [2048, 2048], P('dp', 'tensor')
- grad_w_output: float32 [2048, 2048], P('tensor', 'dp')
- grad_w_expand: float32 [2048, 8192], P('dp', 'tensor')
- grad_w_reduce: float32 [8192, 2048], P('tensor', 'dp')
Inputs may be any that keep to these rules, and one draw needn't show every extreme that they name: Row g holds, in order, the lengths of the sequences packed into the 2048 tokens of data index g (0 marks an empty slot); each row sums to 2048, its longest entry is 1024 or more, and in some row one sequence fills all 2048 tokens.
All inputs are finite; a program needn't handle non-finite values.
Results may differ from a plain program's by a relative error of at most 0.019.
Values may be sent and summed in bfloat16 or wider, within the bound.
A program may use at most 320 MiB of HBM per device.

v0:
```python
import jax
import jax.numpy as jnp
from jax import lax
from jax.sharding import PartitionSpec as P

HEAD_DIM = 128
HISTORY = 17
STREAMS = 4


NORM_EPS = 1e-06
MASKED = -1e30
PRECISE = lax.Precision.HIGHEST


def swapped(x, axis, bit):
    return lax.ppermute(x, axis, [(i, i ^ 1 << bit) for i in range(lax.axis_size(axis))])


def rms_scale(values, gain_vector):
    inverse = lax.rsqrt(jnp.mean(values * values, axis=-1, keepdims=True) + NORM_EPS)
    return values * inverse * gain_vector


def matmul(left_side, right_side):
    return jnp.dot(left_side, right_side, precision=PRECISE)


def front_part(
    history_float, mix_gain, mix_first, mix_second, mix_bias, gain_query, gain_key, gain_value
):
    latest = rms_scale(history_float[HISTORY - 1], mix_gain)
    hidden = jax.nn.gelu(matmul(latest, mix_first), approximate=False)
    mixing = (matmul(hidden, mix_second) + mix_bias).reshape(
        history_float.shape[1], STREAMS, HISTORY
    )
    streams = jnp.einsum("tkj,jtd->ktd", mixing, history_float, precision=PRECISE)
    return (
        rms_scale(streams[0], gain_query),
        rms_scale(streams[1], gain_key),
        rms_scale(streams[2], gain_value),
        streams[3],
    )


def gelu_exact(values):
    return jax.nn.gelu(values, approximate=False)


def across_rows(left_side, right_side):
    return lax.dot_general(
        left_side, right_side, (((0,), (0,)), ((), ())), preferred_element_type=jnp.float32
    )


def across_cols(left_side, right_side):
    return lax.dot_general(
        left_side, right_side, (((1,), (1,)), ((), ())), preferred_element_type=jnp.float32
    )


def segment_of(places, doc_ends):
    return jnp.sum((places[:, None] >= doc_ends[None, :]).astype(jnp.int32), axis=1)


def gather_bits(piece, bit_list, join_dim, device_index):
    for bit_number in bit_list:
        partner = swapped(piece, "tensor", bit_number)
        upper = device_index // (1 << bit_number) % 2 == 1
        piece = jnp.where(
            upper,
            jnp.concatenate([partner, piece], axis=join_dim),
            jnp.concatenate([piece, partner], axis=join_dim),
        )
    return piece


def sum_bits(partial_value, bit_list, device_index, split_dim):
    for bit_number in reversed(bit_list):
        half_size = partial_value.shape[split_dim] // 2
        lower_half = lax.slice_in_dim(partial_value, 0, half_size, axis=split_dim)
        upper_half = lax.slice_in_dim(partial_value, half_size, 2 * half_size, axis=split_dim)
        upper = device_index // (1 << bit_number) % 2 == 1
        keep_half = jnp.where(upper, upper_half, lower_half)
        send_half = jnp.where(upper, lower_half, upper_half)
        partial_value = keep_half + swapped(
            send_half.astype(jnp.bfloat16), "tensor", bit_number
        ).astype(send_half.dtype)
    return partial_value


def make_scores(query_heads, key_heads, query_places, key_places, doc_ends):
    block_rows = min(512, query_heads.shape[0])
    scale_factor = HEAD_DIM ** (-0.5)
    query_segments = segment_of(query_places, doc_ends)
    key_segments = segment_of(key_places, doc_ends)

    def block_scores(block_index):
        scores = (
            jnp.einsum("qhd,khd->hqk", query_heads, key_heads, preferred_element_type=jnp.float32)
            * scale_factor
        )
        allowed = (query_places[:, None] >= key_places[None, :]) & (
            query_segments[:, None] == key_segments[None, :]
        )
        return (jnp.where(allowed[None], scores, MASKED), query_heads)

    return (block_scores, block_rows)


def on_device(
    history,
    cotangent,
    lengths,
    mix_gain,
    mix_first,
    mix_second,
    mix_bias,
    gain_query,
    gain_key,
    gain_value,
    gain_mlp,
    w_query,
    w_key,
    w_value,
    w_output,
    w_expand,
    w_reduce,
):
    shard_rows = history.shape[1]
    tensor_size = lax.axis_size("tensor")
    tok_group = shard_rows * tensor_size
    model_width = w_query.shape[0]
    tensor_index = lax.axis_index("tensor")
    low_bits = [0, 1]
    high_bits = list(range(2, tensor_size.bit_length() - 1))
    scale_factor = HEAD_DIM ** (-0.5)
    history_float = history.astype(jnp.float32)
    front_values, front_back = jax.vjp(
        front_part,
        history_float,
        mix_gain,
        mix_first,
        mix_second,
        mix_bias,
        gain_query,
        gain_key,
        gain_value,
    )
    query_norm, key_norm, value_norm, residual = front_values
    query_low = query_norm.astype(jnp.bfloat16)
    key_low = key_norm.astype(jnp.bfloat16)
    value_low = value_norm.astype(jnp.bfloat16)
    length_row = lax.dynamic_index_in_dim(lengths, lax.axis_index("dp"), 0, keepdims=False)
    doc_ends = jnp.cumsum(length_row)
    query_rows = gather_bits(query_low, high_bits, 0, tensor_index)
    key_rows = gather_bits(key_low, high_bits, 0, tensor_index)
    value_rows = gather_bits(value_low, high_bits, 0, tensor_index)
    cot_rows = gather_bits(cotangent, high_bits, 0, tensor_index)
    query_whole = gather_bits(w_query, low_bits, 1, tensor_index)
    key_whole = gather_bits(w_key, low_bits, 1, tensor_index)
    value_whole = gather_bits(w_value, low_bits, 1, tensor_index)
    output_whole = gather_bits(w_output, low_bits, 0, tensor_index)
    expand_whole = gather_bits(w_expand, low_bits, 1, tensor_index)
    reduce_whole = gather_bits(w_reduce, low_bits, 0, tensor_index)
    group_count = tensor_size // 4
    part_index = tensor_index % 4
    inner_rows = jnp.arange(shard_rows, dtype=jnp.int32)
    group_offsets = 4 * jnp.arange(group_count, dtype=jnp.int32)
    query_places = (
        (part_index + group_offsets)[:, None] * shard_rows + inner_rows[None, :]
    ).reshape(-1)
    key_places = (
        (jnp.arange(4, dtype=jnp.int32)[:, None, None] + group_offsets[None, :, None]) * shard_rows
        + inner_rows[None, None, :]
    ).reshape(-1)
    row_count = query_rows.shape[0]
    heads_here = query_whole.shape[1] // HEAD_DIM
    query_heads = (
        jnp.dot(query_rows, query_whole, preferred_element_type=jnp.float32)
        .astype(jnp.bfloat16)
        .reshape(row_count, heads_here, HEAD_DIM)
    )
    key_part = jnp.dot(key_rows, key_whole, preferred_element_type=jnp.float32).astype(jnp.bfloat16)
    value_part = jnp.dot(value_rows, value_whole, preferred_element_type=jnp.float32).astype(
        jnp.bfloat16
    )
    key_flat = gather_bits(key_part, low_bits, 0, tensor_index)
    value_flat = gather_bits(value_part, low_bits, 0, tensor_index)
    key_heads = key_flat.reshape(tok_group, heads_here, HEAD_DIM)
    value_heads = value_flat.reshape(tok_group, heads_here, HEAD_DIM)
    block_scores, block_rows = make_scores(
        query_heads, key_heads, query_places, key_places, doc_ends
    )
    block_count = row_count // block_rows

    def forward_block(block_index):
        masked, query_block = block_scores(block_index)
        top_score = jnp.max(masked, axis=-1, keepdims=True)
        exponent = jnp.exp(masked - top_score)
        row_total = jnp.sum(exponent, axis=-1, keepdims=True)
        weights_low = (exponent / row_total).astype(jnp.bfloat16)
        context_block = jnp.einsum(
            "hqk,khd->qhd", weights_low, value_heads, preferred_element_type=jnp.float32
        )
        return (context_block, top_score + jnp.log(row_total))

    context_blocks, log_totals = lax.map(forward_block, jnp.arange(block_count))
    context = context_blocks.reshape(row_count, heads_here * HEAD_DIM).astype(jnp.bfloat16)
    attended = sum_bits(
        jnp.dot(context, output_whole, preferred_element_type=jnp.float32),
        high_bits,
        tensor_index,
        0,
    )
    middle = residual + attended
    mlp_norm, norm_back = jax.vjp(rms_scale, middle, gain_mlp)
    mlp_low = mlp_norm.astype(jnp.bfloat16)
    mlp_gathered = gather_bits(mlp_low, high_bits, 0, tensor_index)
    expanded = jnp.dot(mlp_gathered, expand_whole, preferred_element_type=jnp.float32)
    activated, gelu_back = jax.vjp(gelu_exact, expanded)
    active_low = activated.astype(jnp.bfloat16)
    reduced = sum_bits(
        jnp.dot(active_low, reduce_whole, preferred_element_type=jnp.float32),
        high_bits,
        tensor_index,
        0,
    )
    output = (middle + reduced).astype(jnp.bfloat16)
    grad_w_reduce = across_rows(active_low, cot_rows)
    grad_active = across_cols(cot_rows, reduce_whole)
    (grad_expanded,) = gelu_back(grad_active)
    expand_low = grad_expanded.astype(jnp.bfloat16)
    grad_w_expand = across_rows(mlp_gathered, expand_low)
    grad_mlp_norm = sum_bits(across_cols(expand_low, expand_whole), high_bits, tensor_index, 0)
    grad_w_expand = sum_bits(grad_w_expand, low_bits, tensor_index, 1)
    grad_w_reduce = sum_bits(grad_w_reduce, low_bits, tensor_index, 0)
    grad_middle_norm, grad_gain_mlp = norm_back(grad_mlp_norm)
    grad_middle = cotangent.astype(jnp.float32) + grad_middle_norm
    middle_low = grad_middle.astype(jnp.bfloat16)
    middle_rows = gather_bits(middle_low, high_bits, 0, tensor_index)
    grad_w_output = across_rows(context, middle_rows)
    grad_context = (
        across_cols(middle_rows, output_whole)
        .astype(jnp.bfloat16)
        .reshape(row_count, heads_here, HEAD_DIM)
    )

    def backward_block(totals, block_index):
        grad_key_sum, grad_value_sum = totals
        masked, query_block = block_scores(block_index)
        weights_float = jnp.exp(masked - log_totals[block_index])
        weights_low = weights_float.astype(jnp.bfloat16)
        grad_weights = jnp.einsum(
            "qhd,khd->hqk", grad_context, value_heads, preferred_element_type=jnp.float32
        )
        row_delta = jnp.sum(grad_weights * weights_float, axis=-1, keepdims=True)
        grad_scores = (weights_float * (grad_weights - row_delta)).astype(jnp.bfloat16)
        grad_query_block = (
            jnp.einsum("hqk,khd->qhd", grad_scores, key_heads, preferred_element_type=jnp.float32)
            * scale_factor
        )
        grad_key_sum = (
            grad_key_sum
            + jnp.einsum(
                "hqk,qhd->khd", grad_scores, query_block, preferred_element_type=jnp.float32
            )
            * scale_factor
        )
        grad_value_sum = grad_value_sum + jnp.einsum(
            "hqk,qhd->khd", weights_low, grad_context, preferred_element_type=jnp.float32
        )
        return ((grad_key_sum, grad_value_sum), grad_query_block)

    zero_heads = jnp.zeros((tok_group, heads_here, HEAD_DIM), jnp.float32)
    (grad_key_sum, grad_value_sum), grad_query_blocks = lax.scan(
        backward_block, (zero_heads, zero_heads), jnp.arange(block_count)
    )
    grad_key_flat = grad_key_sum.reshape(tok_group, heads_here * HEAD_DIM)
    grad_value_flat = grad_value_sum.reshape(tok_group, heads_here * HEAD_DIM)
    grad_key_flat = sum_bits(grad_key_flat, low_bits, tensor_index, 0)
    grad_value_flat = sum_bits(grad_value_flat, low_bits, tensor_index, 0)
    grad_queries = grad_query_blocks.reshape(row_count, heads_here * HEAD_DIM).astype(jnp.bfloat16)
    grad_keys = grad_key_flat.astype(jnp.bfloat16)
    grad_values = grad_value_flat.astype(jnp.bfloat16)
    grad_w_query = across_rows(query_rows, grad_queries)
    grad_w_key = across_rows(key_rows, grad_keys)
    grad_w_value = across_rows(value_rows, grad_values)
    grad_w_query = sum_bits(grad_w_query, low_bits, tensor_index, 1)
    grad_w_key = sum_bits(grad_w_key, low_bits, tensor_index, 1)
    grad_w_value = sum_bits(grad_w_value, low_bits, tensor_index, 1)
    grad_w_output = sum_bits(grad_w_output, low_bits, tensor_index, 0)
    stream_partial = jnp.concatenate(
        [
            across_cols(grad_queries, query_whole),
            across_cols(grad_keys, key_whole),
            across_cols(grad_values, value_whole),
        ],
        axis=1,
    )
    grad_streams = sum_bits(stream_partial, high_bits, tensor_index, 0)
    front_grads = front_back(
        (
            grad_streams[:, :model_width],
            grad_streams[:, model_width : 2 * model_width],
            grad_streams[:, 2 * model_width :],
            grad_middle,
        )
    )
    grad_history = front_grads[0].astype(jnp.bfloat16)
    small_sums = lax.psum(
        (
            front_grads[1],
            front_grads[2],
            front_grads[3],
            front_grads[4],
            front_grads[5],
            front_grads[6],
            front_grads[7],
            grad_gain_mlp,
        ),
        ("dp", "tensor"),
    )
    sum_query, sum_key, sum_value, sum_output, sum_expand, sum_reduce = (
        lax.psum_scatter(
            grad_w_query.astype(jnp.bfloat16), "dp", scatter_dimension=0, tiled=True
        ).astype(jnp.float32),
        lax.psum_scatter(
            grad_w_key.astype(jnp.bfloat16), "dp", scatter_dimension=0, tiled=True
        ).astype(jnp.float32),
        lax.psum_scatter(
            grad_w_value.astype(jnp.bfloat16), "dp", scatter_dimension=0, tiled=True
        ).astype(jnp.float32),
        lax.psum_scatter(
            grad_w_output.astype(jnp.bfloat16), "dp", scatter_dimension=1, tiled=True
        ).astype(jnp.float32),
        lax.psum_scatter(
            grad_w_expand.astype(jnp.bfloat16), "dp", scatter_dimension=0, tiled=True
        ).astype(jnp.float32),
        lax.psum_scatter(
            grad_w_reduce.astype(jnp.bfloat16), "dp", scatter_dimension=1, tiled=True
        ).astype(jnp.float32),
    )
    return (
        output,
        grad_history,
        small_sums[0],
        small_sums[1],
        small_sums[2],
        small_sums[3],
        small_sums[4],
        small_sums[5],
        small_sums[6],
        small_sums[7],
        sum_query,
        sum_key,
        sum_value,
        sum_output,
        sum_expand,
        sum_reduce,
    )


def solution(mesh):
    placed = (
        P(None, ("dp", "tensor"), None),
        P(("dp", "tensor"), None),
        P(),
        P(),
        P(),
        P(),
        P(),
        P(),
        P(),
        P(),
        P(),
        P(None, "tensor"),
        P(None, "tensor"),
        P(None, "tensor"),
        P("tensor", None),
        P(None, "tensor"),
        P("tensor", None),
    )
    return jax.shard_map(
        on_device,
        mesh=mesh,
        in_specs=placed,
        out_specs=(
            P(("dp", "tensor"), None),
            P(None, ("dp", "tensor"), None),
            P(),
            P(),
            P(),
            P(),
            P(),
            P(),
            P(),
            P(),
            P("dp", "tensor"),
            P("dp", "tensor"),
            P("dp", "tensor"),
            P("tensor", "dp"),
            P("dp", "tensor"),
            P("tensor", "dp"),
        ),
        check_vma=False,
    )
```

profile of v0, /device:TPU:1, one launch (start us, length us, event | category | flops | bytes accessed | tf_op | source)
XLA Modules:
  0.0 1349.2 jit_solution(5649538605081657744)
XLA Ops:
  16.1 19.8 %fusion.22 = f32[4,128,2048]{2,0,1:T(4,128)S(1)} fusion(f32[128,4,17]{2,1,0:T(4,128)S(1)} %copy.62, bf16[17,128,2048]{2,1,0:T(8,128)(2,1)} %param.17), kind=kOutput, calls=%fused_computation.55 | convolution fusion | flops 213909504 | bytes 13142016 | tf_op jit(solution)/shard_map/jvp(tkj,jtd->ktd)/dot_general | solution.py:37
  51.3 16.1 %collective-permute-done.10 = bf16[128,2048]{1,0:T(8,128)(2,1)} collective-permute-done((bf16[128,2048]{1,0:T(8,128)(2,1)S(1)}, bf16[128,2048]{1,0:T(8,128)(2,1)}, u32[]{:S(2)}, u32[]{:S(2)}) %collective-permute-start.10) | collective-permute-done | bytes 524320 | tf_op jit(solution)/shard_map/ppermute | solution.py:17
  81.2 19.9 %collective-permute-done.6 = bf16[128,2048]{1,0:T(8,128)(2,1)S(1)} collective-permute-done((bf16[128,2048]{1,0:T(8,128)(2,1)S(1)}, bf16[128,2048]{1,0:T(8,128)(2,1)S(1)}, u32[]{:S(2)}, u32[]{:S(2)}) %collective-permute-start.6) | collective-permute-done | bytes 524320 | tf_op jit(solution)/shard_map/ppermute | solution.py:17
  102.9 5.0 convolution_convert_fusion.1
  110.7 13.2 collective-permute-done.3
  132.9 13.5 collective-permute-done.9
  151.4 17.4 %collective-permute-done.15 = bf16[1024,512]{0,1:T(8,128)(2,1)S(1)} collective-permute-done((bf16[1024,512]{0,1:T(8,128)(2,1)S(1)}, bf16[1024,512]{0,1:T(8,128)(2,1)S(1)}, u32[]{:S(2)}, u32[]{:S(2)}) %collective-permute-start.15) | collective-permute-done | bytes 1048608 | tf_op jit(solution)/shard_map/ppermute | solution.py:17
  168.8 8.6 fusion.112
  177.4 8.1 fusion.1
  185.5 28.3 %collective-permute-done.5 = bf16[1024,512]{0,1:T(8,128)(2,1)} collective-permute-done((bf16[1024,512]{0,1:T(8,128)(2,1)}, bf16[1024,512]{0,1:T(8,128)(2,1)}, u32[]{:S(2)}, u32[]{:S(2)}) %collective-permute-start.5) | collective-permute-done | bytes 1048608 | tf_op jit(solution)/shard_map/ppermute | solution.py:17
  213.9 8.3 fusion.30
  227.4 5.1 maximum_select_fusion.2
  233.7 16.4 %collective-permute-done.18 = bf16[256,2048]{1,0:T(8,128)(2,1)S(1)} collective-permute-done((bf16[256,2048]{1,0:T(8,128)(2,1)S(1)}, bf16[256,2048]{1,0:T(8,128)(2,1)S(1)}, u32[]{:S(2)}, u32[]{:S(2)}) %collective-permute-start.18) | collective-permute-done | bytes 1048608 | tf_op jit(solution)/shard_map/ppermute | solution.py:17
  254.3 80.8 %collective-permute-done.19 = bf16[128,2048]{1,0:T(8,128)(2,1)S(1)} collective-permute-done((bf16[128,2048]{1,0:T(8,128)(2,1)S(1)}, bf16[128,2048]{1,0:T(8,128)(2,1)S(1)}, u32[]{:S(2)}, u32[]{:S(2)}) %collective-permute-start.19) | collective-permute-done | bytes 524320 | tf_op jit(solution)/shard_map/ppermute | solution.py:17
  338.4 11.0 collective-permute-done.20
  351.9 3.7 maximum_select_fusion.3
  356.1 5.9 collective-permute-done.28
  366.0 5.8 collective-permute-done.21
  371.8 26.3 %multiply_convert_fusion.1 = (bf16[512,2048]{1,0:T(8,128)(2,1)}, f32[512,2048]{1,0:T(8,128)}, f32[512,2048]{1,0:T(8,128)}) fusion(bf16[2048,1024]{1,0:T(8,128)(2,1)} %copy-done.24, bf16[2048,1024]{1,0:T(8,128)(2,1)} %copy-done.80, pred[]{:T(512)S(6)} %eq.154, bf16[256,2048]{1,0:T(8,128)(2,1)} %copy-done.44, bf16[256,2048]{1,0:T(8,128)(2,1)} %collective-permute-done.21, ...), kind=kOutput, calls=%fused_computation.37 | convolution fusion | flops 4410310656 | bytes 20971522 | tf_op jit(solution)/shard_map/dot_general | solution.py:220
  398.1 52.9 %collective-permute-done.25 = bf16[1024,2048]{1,0:T(8,128)(2,1)} collective-permute-done((bf16[1024,2048]{1,0:T(8,128)(2,1)}, bf16[1024,2048]{1,0:T(8,128)(2,1)}, u32[]{:S(2)}, u32[]{:S(2)}) %collective-permute-start.25) | collective-permute-done | bytes 4194336 | tf_op jit(solution)/shard_map/ppermute | solution.py:17
  451.0 20.3 %add_convert_fusion.2 = bf16[512,2048]{1,0:T(8,128)(2,1)} fusion(f32[512,2048]{1,0:T(8,128)} %get-tuple-element.156, f32[512,2048]{1,0:T(8,128)} %get-tuple-element.171, bf16[1024,2048]{1,0:T(8,128)(2,1)} %maximum_select_fusion.3, bf16[1024,2048]{1,0:T(8,128)(2,1)} %collective-permute-done.25, pred[]{:T(512)S(6)} %eq.154, ...), kind=kOutput, calls=%fused_computation.36 | convolution fusion | flops 4356833280 | bytes 20971522 | tf_op jit(solution)/shard_map/dot_general | solution.py:57
  471.3 10.6 fusion.27
  482.2 10.2 fusion.26
  494.3 7.0 fusion.54
  501.3 34.4 %collective-permute-done.30 = bf16[256,2048]{1,0:T(8,128)(2,1)} collective-permute-done((bf16[256,2048]{1,0:T(8,128)(2,1)S(1)}, bf16[256,2048]{1,0:T(8,128)(2,1)}, u32[]{:S(2)}, u32[]{:S(2)}) %collective-permute-start.30) | collective-permute-done | bytes 1048608 | tf_op jit(solution)/shard_map/ppermute | solution.py:17
  543.8 4.5 collective-permute-done.31
  549.5 10.4 collective-permute-done.27
  566.5 4.8 collective-permute-done.32
  572.9 7.1 fusion.53
  580.0 5.8 copy-done.4
  589.7 4.3 convolution_convert_fusion
  595.0 3.7 fusion.19
  598.7 14.3 %multiply_reduce_fusion = (f32[4,512]{1,0:T(4,128)S(1)}, f32[4,512,2048]{2,1,0:T(8,128)}) fusion(f32[4,512,2048]{2,1,0:T(8,128)} %get-tuple-element.170, f32[4,512]{1,0:T(4,128)S(1)} %log_add_fusion, bf16[512,4,128]{0,2,1:T(8,128)(2,1)S(1)} %bitcast.140, bf16[1024,4,128]{0,2,1:T(8,128)(2,1)S(1)} %copy-done.29, bf16[1024,4,128]{0,2,1:T(8,128)(2,1)} %bitcast.5, ...), kind=kOutput, calls=%fused_computation.3 | convolution fusion | flops 1095759872 | bytes 36192256 | tf_op jit(solution)/shard_map/while/body/eval_jaxpr/qhd,khd->hqk/dot_general | solution.py:254
  613.1 15.9 %multiply_convert_fusion = bf16[4,512,2048]{2,1,0:T(8,128)(2,1)} fusion(f32[4,512,2048]{2,1,0:T(8,128)} %get-tuple-element.173, f32[4,512,2048]{2,1,0:T(8,128)} %get-tuple-element.170, f32[4,512]{1,0:T(4,128)S(1)} %get-tuple-element.172, f32[4,512]{1,0:T(4,128)S(1)} %log_add_fusion), kind=kLoop, calls=%fused_computation.2 | loop fusion | flops 16777216 | bytes 41959424 | tf_op jit(solution)/shard_map/while/body/eval_jaxpr/convert_element_type | solution.py:258
  629.0 6.3 fusion.29
  635.4 4.9 multiply_bitcast_fusion
  651.4 121.1 %collective-permute-done.46 = bf16[256,2048]{1,0:T(8,128)(2,1)S(1)} collective-permute-done((bf16[256,2048]{1,0:T(8,128)(2,1)S(1)}, bf16[256,2048]{1,0:T(8,128)(2,1)S(1)}, u32[]{:S(2)}, u32[]{:S(2)}) %collective-permute-start.46) | collective-permute-done | bytes 1048608 | tf_op jit(solution)/shard_map/ppermute | solution.py:17
  774.2 20.8 %collective-permute-done.36 = bf16[1024,512]{0,1:T(8,128)(2,1)S(1)} collective-permute-done((bf16[1024,512]{0,1:T(8,128)(2,1)S(1)}, bf16[1024,512]{0,1:T(8,128)(2,1)S(1)}, u32[]{:S(2)}, u32[]{:S(2)}) %collective-permute-start.36) | collective-permute-done | bytes 1048608 | tf_op jit(solution)/shard_map/ppermute | solution.py:17
  795.0 12.9 collective-permute-start.47
  809.3 8.2 collective-permute-done.34
  817.5 12.9 collective-permute-start.37
  833.0 7.0 collective-permute-done.40
  840.0 6.7 collective-permute-start.35
  848.4 4.9 convert_add_fusion.1
  862.3 3.7 fusion.63
  870.5 3.7 fusion.59
  882.8 4.6 copy-done.1
  897.2 16.3 %collective-permute-done.42 = bf16[2048,256]{1,0:T(8,128)(2,1)} collective-permute-done((bf16[2048,256]{1,0:T(8,128)(2,1)}, bf16[2048,256]{1,0:T(8,128)(2,1)}, u32[]{:S(2)}, u32[]{:S(2)}) %collective-permute-start.42) | collective-permute-done | bytes 1048608 | tf_op jit(solution)/shard_map/ppermute | solution.py:17
  917.7 11.7 convert_add_fusion
  931.4 5.2 select_convert_fusion.3
  936.7 6.7 add_convert_fusion.1
  943.4 18.8 %collective-permute-done.38 = bf16[256,6144]{1,0:T(8,128)(2,1)} collective-permute-done((bf16[256,6144]{1,0:T(8,128)(2,1)}, bf16[256,6144]{1,0:T(8,128)(2,1)}, u32[]{:S(2)}, u32[]{:S(2)}) %collective-permute-start.38) | collective-permute-done | bytes 3145760 | tf_op jit(solution)/shard_map/ppermute | solution.py:17
  962.2 7.4 convert_add_fusion.2
  976.9 29.3 %reduce-scatter.7.cloned.1.call-done = bf16[256,128]{1,0:T(8,128)(2,1)} async-done(((bf16[2048,128]{1,0:T(8,128)(2,1)}), bf16[256,128]{1,0:T(8,128)(2,1)}) %reduce-scatter.7.cloned.1.call-update) | async-done | bytes 65552 | tf_op jit(solution)/shard_map/reduce_scatter | solution.py:325
  1007.8 6.0 add_convert_fusion
  1014.0 65.8 %reduce-scatter.11.cloned.1.call-done = bf16[256,128]{1,0:T(8,128)(2,1)} async-done(((bf16[2048,128]{1,0:T(8,128)(2,1)}), bf16[256,128]{1,0:T(8,128)(2,1)}) %reduce-scatter.11.cloned.1.call-update) | async-done | bytes 65552 | tf_op jit(solution)/shard_map/reduce_scatter | solution.py:331
  1081.3 71.9 %reduce-scatter.9.cloned.1.call-done = bf16[256,128]{1,0:T(8,128)(2,1)} async-done(((bf16[2048,128]{1,0:T(8,128)(2,1)}), bf16[256,128]{1,0:T(8,128)(2,1)}) %reduce-scatter.9.cloned.1.call-update) | async-done | bytes 65552 | tf_op jit(solution)/shard_map/reduce_scatter | solution.py:328
  1154.8 3.9 convert_add_fusion.3
  1164.7 17.9 %fusion.113 = (f32[4,17]{1,0:T(4,128)S(1)}, f32[128,4,17]{2,1,0:T(4,128)S(1)}) fusion(bf16[17,128,2048]{2,1,0:T(8,128)(2,1)S(1)} %bitcast.136, f32[128,2048,4]{1,0,2:T(8,128)S(1)} %add_bitcast_fusion), kind=kOutput, calls=%fused_computation.270 | convolution fusion | flops 213918144 | bytes 13142288 | tf_op jit(solution)/shard_map/transpose(jvp(tkj,jtd->ktd))/dot_general | solution.py:37
  1190.6 25.6 %fusion = bf16[17,128,2048]{2,0,1:T(8,128)(2,1)} fusion(f32[1,128,2048]{2,0,1:T(1,128)S(1)} %broadcast_in_dim.111, f32[128,4,17]{2,1,0:T(4,128)S(1)} %copy-done.33, f32[128,2048,4]{1,0,2:T(8,128)} %copy-done.25), kind=kOutput, calls=%fused_computation.1 | convolution fusion | flops 222822400 | bytes 14190592 | tf_op jit(solution)/shard_map/transpose(jvp(tkj,jtd->ktd))/dot_general | solution.py:37
  1216.2 13.6 %copy.76 = bf16[17,128,2048]{2,1,0:T(8,128)(2,1)} copy(bf16[17,128,2048]{2,0,1:T(8,128)(2,1)} %fusion) | data formatting | bytes 17825792
  1230.1 69.4 %all-reduce.5 = (f32[2048]{0:T(1024)}, f32[68,68]{1,0:T(8,128)}, f32[68]{0:T(128)}, f32[2048]{0:T(1024)}, f32[2048]{0:T(1024)}, /*index=5*/f32[2048]{0:T(1024)}, f32[2048]{0:T(1024)}) all-reduce(f32[2048]{0:T(1024)S(1)} %get-tuple-element.133, f32[68,68]{1,0:T(8,128)S(1)} %fusion.72, ...), channel_id=1, replica_groups=mesh['dp'=8,'tensor'=16] {'dp','tensor'}, use_global_device_ids=true, to_apply=%region_17.18 | all-reduce | flops 14932 | bytes 119456 | tf_op jit(solution)/shard_map/psum | solution.py:311
  1301.3 8.9 reduce-scatter.17.cloned.1.call-done
  1312.0 27.4 %all-reduce.8.cloned.1.call-done = f32[2048,68]{0,1:T(8,128)} async-done(((f32[2048,68]{0,1:T(8,128)}), f32[2048,68]{0,1:T(8,128)}) %all-reduce.8.cloned.1.call-update) | async-done | bytes 557072 | tf_op jit(solution)/shard_map/psum | solution.py:311
  (424 shorter events, 188.5 us)
Async XLA Ops:
  8.0 967.4 %reduce-scatter.13.cloned.1.call-start = ((), (), s32[]{:S(2)}) async-start(), calls=%async_computation.10 | async-start | bytes 589824 | tf_op jit(solution)/shard_map/reduce_scatter | solution.py:334
  8.1 68.1 %collective-permute-start.8 = (bf16[2048,128]{1,0:T(8,128)(2,1)}, bf16[2048,128]{1,0:T(8,128)(2,1)}, u32[]{:S(2)}, u32[]{:S(2)}) collective-permute-start(bf16[2048,128]{1,0:T(8,128)(2,1)} %param.28), channel_id=1, source_target_pairs={{0,1},{1,0},{2,3},{3,2},{4,5},{5,4},{6,7},{7,6},{8,9},{9,8},{10,11... | collective-permute-start | bytes 1572872 | tf_op jit(solution)/shard_map/ppermute | solution.py:17
  9.6 37.6 %collective-permute-start.12 = (bf16[2048,128]{1,0:T(8,128)(2,1)}, bf16[2048,128]{1,0:T(8,128)(2,1)}, u32[]{:S(2)}, u32[]{:S(2)}) collective-permute-start(bf16[2048,128]{1,0:T(8,128)(2,1)} %param.29), channel_id=1, source_target_pairs={{0,1},{1,0},{2,3},{3,2},{4,5},{5,4},{6,7},{7,6},{8,9},{9,8},{10,11... | collective-permute-start | bytes 1572872 | tf_op jit(solution)/shard_map/ppermute | solution.py:17
  9.7 61.6 %collective-permute-start.2 = (bf16[2048,128]{1,0:T(8,128)(2,1)}, bf16[2048,128]{1,0:T(8,128)(2,1)}, u32[]{:S(2)}, u32[]{:S(2)}) collective-permute-start(bf16[2048,128]{1,0:T(8,128)(2,1)} %param.30), channel_id=1, source_target_pairs={{0,1},{1,0},{2,3},{3,2},{4,5},{5,4},{6,7},{7,6},{8,9},{9,8},{10,11... | collective-permute-start | bytes 1572872 | tf_op jit(solution)/shard_map/ppermute | solution.py:17
  40.5 37.9 %collective-permute-start = (bf16[128,2048]{1,0:T(8,128)(2,1)S(1)}, bf16[128,2048]{1,0:T(8,128)(2,1)}, u32[]{:S(2)}, u32[]{:S(2)}) collective-permute-start(bf16[128,2048]{1,0:T(8,128)(2,1)S(1)} %multiply_convert_fusion.5), channel_id=1, source_target_pairs={{0,4},{1,5},{2,6},{3,7},{4,0},{5,1},{6,2},{7,3},{8,12},{9,13},{10,... | collective-permute-start | bytes 1572872 | tf_op jit(solution)/shard_map/ppermute | solution.py:17
  44.9 22.5 %collective-permute-start.10 = (bf16[128,2048]{1,0:T(8,128)(2,1)S(1)}, bf16[128,2048]{1,0:T(8,128)(2,1)}, u32[]{:S(2)}, u32[]{:S(2)}) collective-permute-start(bf16[128,2048]{1,0:T(8,128)(2,1)S(1)} %multiply_convert_fusion.3), channel_id=1, source_target_pairs={{0,4},{1,5},{2,6},{3,7},{4,0},{5,1},{6,2},{7,3},{8,12},{9,13},{10,... | collective-permute-start | bytes 1572872 | tf_op jit(solution)/shard_map/ppermute | solution.py:17
  50.0 52.6 %collective-permute-start.13 = (bf16[2048,256]{1,0:T(8,128)(2,1)}, bf16[2048,256]{1,0:T(8,128)(2,1)}, u32[]{:S(2)}, u32[]{:S(2)}) collective-permute-start(bf16[2048,256]{1,0:T(8,128)(2,1)} %maximum_select_fusion.29), channel_id=1, source_target_pairs={{0,2},{1,3},{2,0},{3,1},{4,6},{5,7},{6,4},{7,5},{8,10},{9,11},{10,... | collective-permute-start | bytes 3145736 | tf_op jit(solution)/shard_map/ppermute | solution.py:17
  70.0 32.9 %collective-permute-start.11 = (bf16[256,2048]{1,0:T(8,128)(2,1)}, bf16[256,2048]{1,0:T(8,128)(2,1)}, u32[]{:S(2)}, u32[]{:S(2)}) collective-permute-start(bf16[256,2048]{1,0:T(8,128)(2,1)} %maximum_select_fusion.28), channel_id=1, source_target_pairs={{0,8},{1,9},{2,10},{3,11},{4,12},{5,13},{6,14},{7,15},{8,0},{9,1},... | collective-permute-start | bytes 3145736 | tf_op jit(solution)/shard_map/ppermute | solution.py:17
  71.3 29.7 %collective-permute-start.6 = (bf16[128,2048]{1,0:T(8,128)(2,1)S(1)}, bf16[128,2048]{1,0:T(8,128)(2,1)S(1)}, u32[]{:S(2)}, u32[]{:S(2)}) collective-permute-start(bf16[128,2048]{1,0:T(8,128)(2,1)S(1)} %multiply_convert_fusion.4), channel_id=1, source_target_pairs={{0,4},{1,5},{2,6},{3,7},{4,0},{5,1},{6,2},{7,3},{8,12},{9,13},{10,... | collective-permute-start | bytes 1572872 | tf_op jit(solution)/shard_map/ppermute | solution.py:17
  76.1 47.7 %collective-permute-start.3 = (bf16[2048,256]{1,0:T(8,128)(2,1)S(1)}, bf16[2048,256]{1,0:T(8,128)(2,1)S(1)}, u32[]{:S(2)}, u32[]{:S(2)}) collective-permute-start(bf16[2048,256]{1,0:T(8,128)(2,1)S(1)} %maximum_select_fusion.23), channel_id=1, source_target_pairs={{0,2},{1,3},{2,0},{3,1},{4,6},{5,7},{6,4},{7,5},{8,10},{9,11},{10,... | collective-permute-start | bytes 3145736 | tf_op jit(solution)/shard_map/ppermute | solution.py:17
  78.4 69.1 %copy-start.37 = (bf16[2048,256]{1,0:T(8,128)(2,1)}, bf16[2048,256]{1,0:T(8,128)(2,1)S(1)}, u32[]{:S(2)}) copy-start(bf16[2048,256]{1,0:T(8,128)(2,1)S(1)} %maximum_select_fusion.27) | copy-start | bytes 3145732
  78.5 67.9 %collective-permute-start.9 = (bf16[2048,256]{1,0:T(8,128)(2,1)S(1)}, bf16[2048,256]{1,0:T(8,128)(2,1)S(1)}, u32[]{:S(2)}, u32[]{:S(2)}) collective-permute-start(bf16[2048,256]{1,0:T(8,128)(2,1)S(1)} %maximum_select_fusion.27), channel_id=1, source_target_pairs={{0,2},{1,3},{2,0},{3,1},{4,6},{5,7},{6,4},{7,5},{8,10},{9,11},{10,... | collective-permute-start | bytes 3145736 | tf_op jit(solution)/shard_map/ppermute | solution.py:17
  101.0 24.2 %collective-permute-start.1 = (bf16[256,2048]{1,0:T(8,128)(2,1)S(1)}, bf16[256,2048]{1,0:T(8,128)(2,1)S(1)}, u32[]{:S(2)}, u32[]{:S(2)}) collective-permute-start(bf16[256,2048]{1,0:T(8,128)(2,1)S(1)} %maximum_select_fusion.22), channel_id=1, source_target_pairs={{0,8},{1,9},{2,10},{3,11},{4,12},{5,13},{6,14},{7,15},{8,0},{9,1},... | collective-permute-start | bytes 3145736 | tf_op jit(solution)/shard_map/ppermute | solution.py:17
  102.6 45.0 %collective-permute-start.7 = (bf16[256,2048]{1,0:T(8,128)(2,1)S(1)}, bf16[256,2048]{1,0:T(8,128)(2,1)S(1)}, u32[]{:S(2)}, u32[]{:S(2)}) collective-permute-start(bf16[256,2048]{1,0:T(8,128)(2,1)S(1)} %maximum_select_fusion.26), channel_id=1, source_target_pairs={{0,8},{1,9},{2,10},{3,11},{4,12},{5,13},{6,14},{7,15},{8,0},{9,1},... | collective-permute-start | bytes 3145736 | tf_op jit(solution)/shard_map/ppermute | solution.py:17
  107.9 21.9 %collective-permute-start.14 = (bf16[512,512]{0,1:T(8,128)(2,1)S(1)}, bf16[512,512]{0,1:T(8,128)(2,1)S(1)}, u32[]{:S(2)}, u32[]{:S(2)}) collective-permute-start(bf16[512,512]{0,1:T(8,128)(2,1)S(1)} %convolution_convert_fusion.1), channel_id=1, source_target_pairs={{0,1},{1,0},{2,3},{3,2},{4,5},{5,4},{6,7},{7,6},{8,9},{9,8},{10,11... | collective-permute-start | bytes 1572872 | tf_op jit(solution)/shard_map/ppermute | solution.py:17
  123.9 6.3 collective-permute-start.16
  125.2 102.2 %collective-permute-start.22 = (bf16[2048,512]{1,0:T(8,128)(2,1)}, bf16[2048,512]{1,0:T(8,128)(2,1)}, u32[]{:S(2)}, u32[]{:S(2)}) collective-permute-start(bf16[2048,512]{1,0:T(8,128)(2,1)} %param.32), channel_id=1, source_target_pairs={{0,1},{1,0},{2,3},{3,2},{4,5},{5,4},{6,7},{7,6},{8,9},{9,8},{10,11... | collective-permute-start | bytes 6291464 | tf_op jit(solution)/shard_map/ppermute | solution.py:17
  129.8 19.2 %collective-permute-start.4 = (bf16[512,512]{0,1:T(8,128)(2,1)S(1)}, bf16[512,512]{0,1:T(8,128)(2,1)S(1)}, u32[]{:S(2)}, u32[]{:S(2)}) collective-permute-start(bf16[512,512]{0,1:T(8,128)(2,1)S(1)} %convolution_convert_fusion.3), channel_id=1, source_target_pairs={{0,1},{1,0},{2,3},{3,2},{4,5},{5,4},{6,7},{7,6},{8,9},{9,8},{10,11... | collective-permute-start | bytes 1572872 | tf_op jit(solution)/shard_map/ppermute | solution.py:17
  130.2 38.6 %collective-permute-start.15 = (bf16[1024,512]{0,1:T(8,128)(2,1)S(1)}, bf16[1024,512]{0,1:T(8,128)(2,1)S(1)}, u32[]{:S(2)}, u32[]{:S(2)}) collective-permute-start(bf16[1024,512]{0,1:T(8,128)(2,1)S(1)} %maximum_select_fusion.30), channel_id=1, source_target_pairs={{0,2},{1,3},{2,0},{3,1},{4,6},{5,7},{6,4},{7,5},{8,10},{9,11},{10,... | collective-permute-start | bytes 3145736 | tf_op jit(solution)/shard_map/ppermute | solution.py:17
  146.4 75.9 %collective-permute-start.17 = (bf16[256,2048]{1,0:T(8,128)(2,1)}, bf16[256,2048]{1,0:T(8,128)(2,1)}, u32[]{:S(2)}, u32[]{:S(2)}) collective-permute-start(bf16[256,2048]{1,0:T(8,128)(2,1)} %maximum_select_fusion.32), channel_id=1, source_target_pairs={{0,2},{1,3},{2,0},{3,1},{4,6},{5,7},{6,4},{7,5},{8,10},{9,11},{10,... | collective-permute-start | bytes 3145736 | tf_op jit(solution)/shard_map/ppermute | solution.py:17
  150.2 63.7 %collective-permute-start.5 = (bf16[1024,512]{0,1:T(8,128)(2,1)}, bf16[1024,512]{0,1:T(8,128)(2,1)}, u32[]{:S(2)}, u32[]{:S(2)}) collective-permute-start(bf16[1024,512]{0,1:T(8,128)(2,1)} %maximum_select_fusion.24), channel_id=1, source_target_pairs={{0,2},{1,3},{2,0},{3,1},{4,6},{5,7},{6,4},{7,5},{8,10},{9,11},{10,... | collective-permute-start | bytes 3145736 | tf_op jit(solution)/shard_map/ppermute | solution.py:17
  226.1 23.9 %collective-permute-start.18 = (bf16[256,2048]{1,0:T(8,128)(2,1)S(1)}, bf16[256,2048]{1,0:T(8,128)(2,1)S(1)}, u32[]{:S(2)}, u32[]{:S(2)}) collective-permute-start(bf16[256,2048]{1,0:T(8,128)(2,1)S(1)} %select_convert_fusion.14), channel_id=1, source_target_pairs={{0,8},{1,9},{2,10},{3,11},{4,12},{5,13},{6,14},{7,15},{8,0},{9,1},... | collective-permute-start | bytes 3145736 | tf_op jit(solution)/shard_map/ppermute | solution.py:17
  232.5 131.4 %collective-permute-start.23 = (bf16[2048,1024]{1,0:T(8,128)(2,1)S(1)}, bf16[2048,1024]{1,0:T(8,128)(2,1)S(1)}, u32[]{:S(2)}, u32[]{:S(2)}) collective-permute-start(bf16[2048,1024]{1,0:T(8,128)(2,1)S(1)} %maximum_select_fusion.2), channel_id=1, source_target_pairs={{0,2},{1,3},{2,0},{3,1},{4,6},{5,7},{6,4},{7,5},{8,10},{9,11},{10,... | collective-permute-start | bytes 12582920 | tf_op jit(solution)/shard_map/ppermute | solution.py:17
  250.5 85.5 %copy-start.51 = (f32[2048]{0:T(1024)S(1)}, f32[2048]{0:T(1024)}, u32[]{:S(2)}) copy-start(f32[2048]{0:T(1024)} %param.27) | copy-start | bytes 24580
  250.6 84.5 %collective-permute-start.19 = (bf16[128,2048]{1,0:T(8,128)(2,1)S(1)}, bf16[128,2048]{1,0:T(8,128)(2,1)S(1)}, u32[]{:S(2)}, u32[]{:S(2)}) collective-permute-start(bf16[128,2048]{1,0:T(8,128)(2,1)S(1)} %select_convert_fusion.23), channel_id=1, source_target_pairs={{0,4},{1,5},{2,6},{3,7},{4,0},{5,1},{6,2},{7,3},{8,12},{9,13},{10,... | collective-permute-start | bytes 1572872 | tf_op jit(solution)/shard_map/ppermute | solution.py:17
  252.2 99.6 %collective-permute-start.24 = (bf16[512,2048]{1,0:T(8,128)(2,1)S(1)}, bf16[512,2048]{1,0:T(8,128)(2,1)S(1)}, u32[]{:S(2)}, u32[]{:S(2)}) collective-permute-start(bf16[512,2048]{1,0:T(8,128)(2,1)S(1)} %copy-done.31), channel_id=1, source_target_pairs={{0,1},{1,0},{2,3},{3,2},{4,5},{5,4},{6,7},{7,6},{8,9},{9,8},{10,11... | collective-permute-start | bytes 6291464 | tf_op jit(solution)/shard_map/ppermute | solution.py:17
  336.2 13.2 collective-permute-start.20
  349.7 22.1 %collective-permute-start.21 = (bf16[256,2048]{1,0:T(8,128)(2,1)S(1)}, bf16[256,2048]{1,0:T(8,128)(2,1)}, u32[]{:S(2)}, u32[]{:S(2)}) collective-permute-start(bf16[256,2048]{1,0:T(8,128)(2,1)S(1)} %maximum_select_fusion.33), channel_id=1, source_target_pairs={{0,8},{1,9},{2,10},{3,11},{4,12},{5,13},{6,14},{7,15},{8,0},{9,1},... | collective-permute-start | bytes 3145736 | tf_op jit(solution)/shard_map/ppermute | solution.py:17
  350.0 11.9 collective-permute-start.28
  355.6 95.4 %collective-permute-start.25 = (bf16[1024,2048]{1,0:T(8,128)(2,1)}, bf16[1024,2048]{1,0:T(8,128)(2,1)}, u32[]{:S(2)}, u32[]{:S(2)}) collective-permute-start(bf16[1024,2048]{1,0:T(8,128)(2,1)} %maximum_select_fusion.3), channel_id=1, source_target_pairs={{0,2},{1,3},{2,0},{3,1},{4,6},{5,7},{6,4},{7,5},{8,10},{9,11},{10,... | collective-permute-start | bytes 12582920 | tf_op jit(solution)/shard_map/ppermute | solution.py:17
  362.2 88.8 %copy-start.43 = (bf16[256,2048]{1,0:T(8,128)(2,1)}, bf16[256,2048]{1,0:T(8,128)(2,1)S(1)}, u32[]{:S(2)}) copy-start(bf16[256,2048]{1,0:T(8,128)(2,1)S(1)} %maximum_select_fusion.34) | copy-start | bytes 3145732
  362.2 35.9 %collective-permute-start.29 = (bf16[256,2048]{1,0:T(8,128)(2,1)S(1)}, bf16[256,2048]{1,0:T(8,128)(2,1)}, u32[]{:S(2)}, u32[]{:S(2)}) collective-permute-start(bf16[256,2048]{1,0:T(8,128)(2,1)S(1)} %maximum_select_fusion.34), channel_id=1, source_target_pairs={{0,8},{1,9},{2,10},{3,11},{4,12},{5,13},{6,14},{7,15},{8,0},{9,1},... | collective-permute-start | bytes 3145736 | tf_op jit(solution)/shard_map/ppermute | solution.py:17
  492.6 47.8 %collective-permute-start.26 = (bf16[256,2048]{1,0:T(8,128)(2,1)S(1)}, bf16[256,2048]{1,0:T(8,128)(2,1)}, u32[]{:S(2)}, u32[]{:S(2)}) collective-permute-start(bf16[256,2048]{1,0:T(8,128)(2,1)S(1)} %select_convert_fusion.13), channel_id=1, source_target_pairs={{0,8},{1,9},{2,10},{3,11},{4,12},{5,13},{6,14},{7,15},{8,0},{9,1},... | collective-permute-start | bytes 3145736 | tf_op jit(solution)/shard_map/ppermute | solution.py:17
  493.9 41.8 %collective-permute-start.30 = (bf16[256,2048]{1,0:T(8,128)(2,1)S(1)}, bf16[256,2048]{1,0:T(8,128)(2,1)}, u32[]{:S(2)}, u32[]{:S(2)}) collective-permute-start(bf16[256,2048]{1,0:T(8,128)(2,1)S(1)} %select_convert_fusion.12), channel_id=1, source_target_pairs={{0,8},{1,9},{2,10},{3,11},{4,12},{5,13},{6,14},{7,15},{8,0},{9,1},... | collective-permute-start | bytes 3145736 | tf_op jit(solution)/shard_map/ppermute | solution.py:17
  538.8 9.6 collective-permute-start.31
  542.3 17.6 %collective-permute-start.27 = (bf16[128,2048]{1,0:T(8,128)(2,1)S(1)}, bf16[128,2048]{1,0:T(8,128)(2,1)S(1)}, u32[]{:S(2)}, u32[]{:S(2)}) collective-permute-start(bf16[128,2048]{1,0:T(8,128)(2,1)S(1)} %select_convert_fusion.22), channel_id=1, source_target_pairs={{0,4},{1,5},{2,6},{3,7},{4,0},{5,1},{6,2},{7,3},{8,12},{9,13},{10,... | collective-permute-start | bytes 1572872 | tf_op jit(solution)/shard_map/ppermute | solution.py:17
  561.7 9.5 collective-permute-start.32
  565.6 281.5 %collective-permute-start.48 = (bf16[2048,1024]{1,0:T(8,128)(2,1)}, bf16[2048,1024]{1,0:T(8,128)(2,1)}, u32[]{:S(2)}, u32[]{:S(2)}) collective-permute-start(bf16[2048,1024]{1,0:T(8,128)(2,1)} %select_convert_fusion.1), channel_id=1, source_target_pairs={{0,2},{1,3},{2,0},{3,1},{4,6},{5,7},{6,4},{7,5},{8,10},{9,11},{10,... | collective-permute-start | bytes 12582920 | tf_op jit(solution)/shard_map/ppermute | solution.py:17
  571.6 18.2 %collective-permute-start.33 = (bf16[256,2048]{1,0:T(8,128)(2,1)S(1)}, bf16[256,2048]{1,0:T(8,128)(2,1)S(1)}, u32[]{:S(2)}, u32[]{:S(2)}) collective-permute-start(bf16[256,2048]{1,0:T(8,128)(2,1)S(1)} %maximum_select_fusion.35), channel_id=1, source_target_pairs={{0,8},{1,9},{2,10},{3,11},{4,12},{5,13},{6,14},{7,15},{8,0},{9,1},... | collective-permute-start | bytes 3145736 | tf_op jit(solution)/shard_map/ppermute | solution.py:17
  588.3 329.4 %collective-permute-start.50 = (bf16[1024,2048]{1,0:T(8,128)(2,1)}, bf16[1024,2048]{1,0:T(8,128)(2,1)}, u32[]{:S(2)}, u32[]{:S(2)}) collective-permute-start(bf16[1024,2048]{1,0:T(8,128)(2,1)} %select_convert_fusion), channel_id=1, source_target_pairs={{0,2},{1,3},{2,0},{3,1},{4,6},{5,7},{6,4},{7,5},{8,10},{9,11},{10,... | collective-permute-start | bytes 12582920 | tf_op jit(solution)/shard_map/ppermute | solution.py:17
  642.1 130.5 %collective-permute-start.46 = (bf16[256,2048]{1,0:T(8,128)(2,1)S(1)}, bf16[256,2048]{1,0:T(8,128)(2,1)S(1)}, u32[]{:S(2)}, u32[]{:S(2)}) collective-permute-start(bf16[256,2048]{1,0:T(8,128)(2,1)S(1)} %select_convert_fusion.6), channel_id=1, source_target_pairs={{0,2},{1,3},{2,0},{3,1},{4,6},{5,7},{6,4},{7,5},{8,10},{9,11},{10,... | collective-permute-start | bytes 3145736 | tf_op jit(solution)/shard_map/ppermute | solution.py:17
  643.4 151.7 %collective-permute-start.36 = (bf16[1024,512]{0,1:T(8,128)(2,1)S(1)}, bf16[1024,512]{0,1:T(8,128)(2,1)S(1)}, u32[]{:S(2)}, u32[]{:S(2)}) collective-permute-start(bf16[1024,512]{0,1:T(8,128)(2,1)S(1)} %bitcast.146), channel_id=1, source_target_pairs={{0,2},{1,3},{2,0},{3,1},{4,6},{5,7},{6,4},{7,5},{8,10},{9,11},{10,... | collective-permute-start | bytes 3145736 | tf_op jit(solution)/shard_map/ppermute | solution.py:17
  644.1 173.4 %collective-permute-start.34 = (bf16[1024,512]{0,1:T(8,128)(2,1)S(1)}, bf16[1024,512]{0,1:T(8,128)(2,1)S(1)}, u32[]{:S(2)}, u32[]{:S(2)}) collective-permute-start(bf16[1024,512]{0,1:T(8,128)(2,1)S(1)} %bitcast.145), channel_id=1, source_target_pairs={{0,2},{1,3},{2,0},{3,1},{4,6},{5,7},{6,4},{7,5},{8,10},{9,11},{10,... | collective-permute-start | bytes 3145736 | tf_op jit(solution)/shard_map/ppermute | solution.py:17
  772.6 67.4 %collective-permute-start.40 = (bf16[2048,256]{1,0:T(8,128)(2,1)S(1)}, bf16[2048,256]{1,0:T(8,128)(2,1)S(1)}, u32[]{:S(2)}, u32[]{:S(2)}) collective-permute-start(bf16[2048,256]{1,0:T(8,128)(2,1)S(1)} %select_convert_fusion.9), channel_id=1, source_target_pairs={{0,2},{1,3},{2,0},{3,1},{4,6},{5,7},{6,4},{7,5},{8,10},{9,11},{10,... | collective-permute-start | bytes 3145736 | tf_op jit(solution)/shard_map/ppermute | solution.py:17
  772.8 75.5 %slice-start.7 = ((s8[16777216]{0:T(1024)(128)(4,1)}), s8[4194304]{0:T(1024)(128)(4,1)S(1)}, s32[]{:S(2)}) async-start(s8[16777216]{0:T(1024)(128)(4,1)} %bitcast.137), calls=%async_computation.20 | async-start | bytes 8388608
  773.3 75.0 %slice-start.8 = ((s8[16777216]{0:T(1024)(128)(4,1)}), s8[4194304]{0:T(1024)(128)(4,1)S(1)}, s32[]{:S(2)}) async-start(s8[16777216]{0:T(1024)(128)(4,1)} %bitcast.137), calls=%async_computation.21 | async-start | bytes 8388608
  795.0 63.3 %collective-permute-start.47 = (bf16[128,2048]{1,0:T(8,128)(2,1)}, bf16[128,2048]{1,0:T(8,128)(2,1)}, u32[]{:S(2)}, u32[]{:S(2)}) collective-permute-start(bf16[128,2048]{1,0:T(8,128)(2,1)} %select_convert_fusion.15), channel_id=1, source_target_pairs={{0,1},{1,0},{2,3},{3,2},{4,5},{5,4},{6,7},{7,6},{8,9},{9,8},{10,11... | collective-permute-start | bytes 1572872 | tf_op jit(solution)/shard_map/ppermute | solution.py:17
  817.5 43.5 %collective-permute-start.37 = (bf16[512,512]{0,1:T(8,128)(2,1)}, bf16[512,512]{0,1:T(8,128)(2,1)}, u32[]{:S(2)}, u32[]{:S(2)}) collective-permute-start(bf16[512,512]{0,1:T(8,128)(2,1)} %select_convert_fusion.19), channel_id=1, source_target_pairs={{0,1},{1,0},{2,3},{3,2},{4,5},{5,4},{6,7},{7,6},{8,9},{9,8},{10,11... | collective-permute-start | bytes 1572872 | tf_op jit(solution)/shard_map/ppermute | solution.py:17
  840.0 27.3 %collective-permute-start.35 = (bf16[512,512]{0,1:T(8,128)(2,1)}, bf16[512,512]{0,1:T(8,128)(2,1)}, u32[]{:S(2)}, u32[]{:S(2)}) collective-permute-start(bf16[512,512]{0,1:T(8,128)(2,1)} %select_convert_fusion.20), channel_id=1, source_target_pairs={{0,1},{1,0},{2,3},{3,2},{4,5},{5,4},{6,7},{7,6},{8,9},{9,8},{10,11... | collective-permute-start | bytes 1572872 | tf_op jit(solution)/shard_map/ppermute | solution.py:17
  848.3 41.2 %collective-permute-start.41 = (bf16[2048,128]{1,0:T(8,128)(2,1)S(1)}, bf16[2048,128]{1,0:T(8,128)(2,1)}, u32[]{:S(2)}, u32[]{:S(2)}) collective-permute-start(bf16[2048,128]{1,0:T(8,128)(2,1)S(1)} %select_convert_fusion.18), channel_id=1, source_target_pairs={{0,1},{1,0},{2,3},{3,2},{4,5},{5,4},{6,7},{7,6},{8,9},{9,8},{10,11... | collective-permute-start | bytes 1572872 | tf_op jit(solution)/shard_map/ppermute | solution.py:17
  858.3 78.3 %collective-permute-start.49 = (bf16[2048,512]{1,0:T(8,128)(2,1)}, bf16[2048,512]{1,0:T(8,128)(2,1)}, u32[]{:S(2)}, u32[]{:S(2)}) collective-permute-start(bf16[2048,512]{1,0:T(8,128)(2,1)} %select_convert_fusion.4), channel_id=1, source_target_pairs={{0,1},{1,0},{2,3},{3,2},{4,5},{5,4},{6,7},{7,6},{8,9},{9,8},{10,11... | collective-permute-start | bytes 6291464 | tf_op jit(solution)/shard_map/ppermute | solution.py:17
  860.9 145.3 %reduce-scatter.7.cloned.1.call-start = ((), (), s32[]{:S(2)}) async-start(), calls=%async_computation.7 | async-start | bytes 589824 | tf_op jit(solution)/shard_map/reduce_scatter | solution.py:325
  866.2 26.7 %collective-permute-start.44 = (bf16[2048,256]{1,0:T(8,128)(2,1)S(1)}, bf16[2048,256]{1,0:T(8,128)(2,1)}, u32[]{:S(2)}, u32[]{:S(2)}) collective-permute-start(bf16[2048,256]{1,0:T(8,128)(2,1)S(1)} %select_convert_fusion.7), channel_id=1, source_target_pairs={{0,2},{1,3},{2,0},{3,1},{4,6},{5,7},{6,4},{7,5},{8,10},{9,11},{10,... | collective-permute-start | bytes 3145736 | tf_op jit(solution)/shard_map/ppermute | solution.py:17
  875.6 38.0 %collective-permute-start.42 = (bf16[2048,256]{1,0:T(8,128)(2,1)}, bf16[2048,256]{1,0:T(8,128)(2,1)}, u32[]{:S(2)}, u32[]{:S(2)}) collective-permute-start(bf16[2048,256]{1,0:T(8,128)(2,1)} %select_convert_fusion.8), channel_id=1, source_target_pairs={{0,2},{1,3},{2,0},{3,1},{4,6},{5,7},{6,4},{7,5},{8,10},{9,11},{10,... | collective-permute-start | bytes 3145736 | tf_op jit(solution)/shard_map/ppermute | solution.py:17
  889.5 72.7 %collective-permute-start.38 = (bf16[256,6144]{1,0:T(8,128)(2,1)}, bf16[256,6144]{1,0:T(8,128)(2,1)}, u32[]{:S(2)}, u32[]{:S(2)}) collective-permute-start(bf16[256,6144]{1,0:T(8,128)(2,1)} %select_convert_fusion.2), channel_id=1, source_target_pairs={{0,8},{1,9},{2,10},{3,11},{4,12},{5,13},{6,14},{7,15},{8,0},{9,1},... | collective-permute-start | bytes 9437192 | tf_op jit(solution)/shard_map/ppermute | solution.py:17
  892.9 186.9 %reduce-scatter.11.cloned.1.call-start = ((), (), s32[]{:S(2)}) async-start(), calls=%async_computation.9 | async-start | bytes 589824 | tf_op jit(solution)/shard_map/reduce_scatter | solution.py:331
  896.1 20.6 %collective-permute-start.45 = (bf16[2048,128]{1,0:T(8,128)(2,1)S(1)}, bf16[2048,128]{1,0:T(8,128)(2,1)S(1)}, u32[]{:S(2)}, u32[]{:S(2)}) collective-permute-start(bf16[2048,128]{1,0:T(8,128)(2,1)S(1)} %select_convert_fusion.16), channel_id=1, source_target_pairs={{0,1},{1,0},{2,3},{3,2},{4,5},{5,4},{6,7},{7,6},{8,9},{9,8},{10,11... | collective-permute-start | bytes 1572872 | tf_op jit(solution)/shard_map/ppermute | solution.py:17
  915.3 14.1 %collective-permute-start.43 = (bf16[2048,128]{1,0:T(8,128)(2,1)S(1)}, bf16[2048,128]{1,0:T(8,128)(2,1)}, u32[]{:S(2)}, u32[]{:S(2)}) collective-permute-start(bf16[2048,128]{1,0:T(8,128)(2,1)S(1)} %select_convert_fusion.17), channel_id=1, source_target_pairs={{0,1},{1,0},{2,3},{3,2},{4,5},{5,4},{6,7},{7,6},{8,9},{9,8},{10,11... | collective-permute-start | bytes 1572872 | tf_op jit(solution)/shard_map/ppermute | solution.py:17
  917.7 235.6 %reduce-scatter.9.cloned.1.call-start = ((), (), s32[]{:S(2)}) async-start(), calls=%async_computation.8 | async-start | bytes 589824 | tf_op jit(solution)/shard_map/reduce_scatter | solution.py:328
  931.4 368.1 %reduce-scatter.15.cloned.1.call-start = ((), (), s32[]{:S(2)}) async-start(), calls=%async_computation.11 | async-start | bytes 2359296 | tf_op jit(solution)/shard_map/reduce_scatter | solution.py:337
  936.6 71.1 %collective-permute-start.51 = (bf16[512,2048]{1,0:T(8,128)(2,1)}, bf16[512,2048]{1,0:T(8,128)(2,1)S(1)}, u32[]{:S(2)}, u32[]{:S(2)}) collective-permute-start(bf16[512,2048]{1,0:T(8,128)(2,1)} %select_convert_fusion.3), channel_id=1, source_target_pairs={{0,1},{1,0},{2,3},{3,2},{4,5},{5,4},{6,7},{7,6},{8,9},{9,8},{10,11... | collective-permute-start | bytes 6291464 | tf_op jit(solution)/shard_map/ppermute | solution.py:17
  943.3 366.9 %reduce-scatter.17.cloned.1.call-start = ((), (), s32[]{:S(2)}) async-start(), calls=%async_computation.12 | async-start | bytes 2359296 | tf_op jit(solution)/shard_map/reduce_scatter | solution.py:340
  973.8 181.0 %collective-permute-start.39 = (bf16[128,6144]{1,0:T(8,128)(2,1)}, bf16[128,6144]{1,0:T(8,128)(2,1)}, u32[]{:S(2)}, u32[]{:S(2)}) collective-permute-start(bf16[128,6144]{1,0:T(8,128)(2,1)} %select_convert_fusion.5), channel_id=1, source_target_pairs={{0,4},{1,5},{2,6},{3,7},{4,0},{5,1},{6,2},{7,3},{8,12},{9,13},{10,... | collective-permute-start | bytes 4718600 | tf_op jit(solution)/shard_map/ppermute | solution.py:17
  1013.8 325.6 %all-reduce.8.cloned.1.call-start = ((), (), s32[]{:S(2)}) async-start(), calls=%async_computation.6 | async-start | bytes 1179648 | tf_op jit(solution)/shard_map/psum | solution.py:311
  (100 other events, 1016.6 us)
Sparse Core Ops, SparseCore 0:
  861.0 71.6 reduce-scatter.12
  936.8 69.4 reduce-scatter.6
  1010.8 68.9 reduce-scatter.10
  1083.8 69.4 reduce-scatter.8
  1157.3 74.6 reduce-scatter.14
  1235.9 74.2 reduce-scatter.16
Sparse Core Ops, SparseCore 1:
  1190.6 148.7 all-reduce.7
where the time goes:
time: 1350 us
  waiting for transfers between devices  731 us (54%)
  matrix products  235 us (17%)
  other arithmetic  157 us (12%)
  starting transfers between devices  90.5 us (7%)
  blocking collectives  69.4 us (5%)
  local copies, waits for them, and re-layouts  49.2 us (4%)
  between operations  17.8 us (1%)
    ppermute x52, waiting for transfers between devices, swapped(): lax.ppermute(x, axis, [(i, i ^ 1 << bit) for i in range(lax.axis_size(axi...  528 us
    ppermute x52, starting transfers between devices, swapped(): lax.ppermute(x, axis, [(i, i ^ 1 << bit) for i in range(lax.axis_size(axi...  90.1 us
    reduce_scatter x1, waiting for transfers between devices, on_device(): lax.psum_scatter(grad_w_key.astype(jnp.bfloat16), 'dp', scatter_dimension...  71.9 us
    psum x1, blocking collectives, on_device(): lax.psum((front_grads[1], front_grads[2], front_grads[3], front_grads[4],...  69.4 us
    reduce_scatter x1, waiting for transfers between devices, on_device(): lax.psum_scatter(grad_w_value.astype(jnp.bfloat16), 'dp', scatter_dimensi...  65.8 us
    dot_general x3, matrix products, front_part(): jnp.einsum('tkj,jtd->ktd', mixing, history_float, precision=PRECISE)  63.3 us
    unnamed x212, local copies, waits for them, and re-layouts  44.7 us
    dot_general x6, matrix products, across_cols(): lax.dot_general(left_side, right_side, (((1,), (1,)), ((), ())), preferre...  43.8 us
  transfers between devices with their start and end apart: 59, of which 27 were waited for; matrix products, arithmetic and copies ran while one was open for 27% of the time, Pallas kernels for 0%

commit v1 on v0

v1 whole, which is shorter than its diff:
```python
import functools

import jax
import jax.numpy as jnp
from jax import lax
from jax.experimental import pallas as pl
from jax.experimental.pallas import tpu as pltpu
from jax.sharding import PartitionSpec as P

HEAD_DIM = 128
HISTORY = 17
STREAMS = 4
MIX = HISTORY * STREAMS
D = 2048
ROWS = 128
FF_SHARD = 512
NORM_EPS = 1e-06
MASKED = -1e30
PRECISE = lax.Precision.HIGHEST
MESH = pl.DeviceIdType.MESH
BF = jnp.bfloat16
F32 = jnp.float32
VMEM = pltpu.VMEM
ANY = pl.ANY
MIB = 2**20

Y1, Y2, Y3 = 2, 4, 6
SIB, XN, DIAG = 1, 8, 9
A_MASKS = (0, SIB, XN, DIAG)
LO, HI = pl.ds(0, 64), pl.ds(64, 64)


def flip(value, mask):
    for bit in (1, 2, 4, 8):
        if mask & bit:
            value = value + bit - 2 * bit * lax.rem(lax.div(value, bit), 2)
    return value


def dev(t_mask, dp_mask=0):
    return (flip(lax.axis_index("dp"), dp_mask), flip(lax.axis_index("tensor"), t_mask))


def enter(partners):
    barrier = pltpu.get_barrier_semaphore()
    for partner in partners:
        pl.semaphore_signal(barrier, inc=1, device_id=dev(*partner), device_id_type=MESH)
    pl.semaphore_wait(barrier, len(partners))


def rcopy(src, dst, send, recv, target):
    return pltpu.make_async_remote_copy(
        src_ref=src, dst_ref=dst, send_sem=send, recv_sem=recv, device_id=dev(*target), device_id_type=MESH
    )


def nt(a, b):
    return lax.dot_general(a, b, (((1,), (1,)), ((), ())), preferred_element_type=F32)


def tn(a, b):
    return lax.dot_general(a, b, (((0,), (0,)), ((), ())), preferred_element_type=F32)


def nn(a, b):
    return jnp.dot(a, b, preferred_element_type=F32)


class Gather:
    def __init__(self, own, rows, send, recv):
        def c(i, src, dst, target):
            return rcopy(src, dst, send.at[i], recv.at[i], (target,))

        self.copies = [
            c(0, own.at[LO], rows.at[1, LO], Y1),
            c(1, own.at[HI], rows.at[3, HI], Y3),
            c(2, own.at[HI], rows.at[1, HI], Y1),
            c(3, own.at[LO], rows.at[3, LO], Y3),
            c(4, rows.at[1, LO], rows.at[2, LO], Y3),
            c(5, rows.at[3, HI], rows.at[2, HI], Y1),
        ]

    def start(self):
        for i in range(4):
            self.copies[i].start()

    def forward(self):
        self.copies[0].wait_recv()
        self.copies[4].start()
        self.copies[1].wait_recv()
        self.copies[5].start()

    def arrived(self, slot):
        for i in {1: (2,), 3: (3,), 2: (4, 5)}[slot]:
            self.copies[i].wait_recv()

    def finish(self):
        for c in self.copies:
            c.wait_send()


class Scatter:
    def __init__(self, out, passed, got, send, recv):
        def c(i, src, dst, target):
            return rcopy(src, dst, send.at[i], recv.at[i], (target,))

        self.out, self.passed, self.got = out, passed, got
        self.copies = [
            c(0, out.at[0, LO], passed.at[LO], Y1),
            c(1, out.at[0, HI], passed.at[HI], Y3),
            c(2, out.at[1, LO], got.at[0, LO], Y1),
            c(3, out.at[2, HI], got.at[1, HI], Y3),
            c(4, out.at[2, LO], got.at[1, LO], Y3),
            c(5, out.at[1, HI], got.at[0, HI], Y1),
        ]

    def opposite(self, part):
        self.out[0] = part.astype(BF)
        self.copies[0].start()
        self.copies[1].start()

    def first(self, part):
        self.out[1, LO] = part[0:64].astype(BF)
        self.copies[2].start()

    def second(self, part):
        self.out[2, HI] = part[64:128].astype(BF)
        self.copies[3].start()

    def relay(self, first_ref, second_ref):
        self.copies[0].wait_recv()
        self.out[2, LO] = (second_ref[LO] + self.passed[LO].astype(F32)).astype(BF)
        self.copies[4].start()
        self.copies[1].wait_recv()
        self.out[1, HI] = (first_ref[HI] + self.passed[HI].astype(F32)).astype(BF)
        self.copies[5].start()

    def total(self):
        for i in (2, 3, 4, 5):
            self.copies[i].wait_recv()
        return self.got[0].astype(F32) + self.got[1].astype(F32)

    def finish(self):
        for c in self.copies:
            c.wait_send()


def gelu_parts(x):
    cdf = 0.5 * (1.0 + lax.erf(x * (0.5**0.5)))
    return x * cdf, cdf + x * jnp.exp(-0.5 * x * x) * 0.3989422804014327


def front_kernel(
    hist, latest, mix_gain, mix_first, mix_second, mix_bias, gains, x_out, n_out, inv_out, resid_out, mix_out, pre_out, mix
):
    @pl.when(pl.program_id(0) == 0)
    def _():
        last = latest[0].astype(F32)
        inverse = lax.rsqrt(jnp.mean(last * last, axis=-1, keepdims=True) + NORM_EPS)
        pre = jnp.dot(last * inverse * mix_gain[...], mix_first[...], precision=PRECISE, preferred_element_type=F32)
        pre_out[...] = pre
        hidden = gelu_parts(pre)[0]
        mixing = jnp.dot(hidden, mix_second[...], precision=PRECISE, preferred_element_type=F32) + mix_bias[...]
        mix[...] = mixing
        mix_out[...] = mixing

    rows = hist.shape[1]
    here = mix[pl.ds(pl.multiple_of(pl.program_id(0) * rows, rows), rows), :]
    spread = [jnp.broadcast_to(here[:, i : i + 1], (rows, 128)) for i in range(MIX)]
    squares = [jnp.zeros((rows, 128), F32) for _ in range(3)]
    sums = []
    width = 256
    for c in range(D // width):
        tiles = [[None] * (width // 128) for _ in range(STREAMS)]
        for j in range(HISTORY):
            h = hist[j, :, c * width : (c + 1) * width].astype(F32)
            for lane in range(width // 128):
                piece = h[:, lane * 128 : (lane + 1) * 128]
                for k in range(STREAMS):
                    term = spread[k * HISTORY + j] * piece
                    tiles[k][lane] = term if j == 0 else tiles[k][lane] + term
        for lane in range(width // 128):
            at = slice(c * width + lane * 128, c * width + (lane + 1) * 128)
            resid_out[:, at] = tiles[3][lane]
            for k in range(3):
                squares[k] = squares[k] + tiles[k][lane] * tiles[k][lane]
        sums.append(tiles)
    for k in range(3):
        inverse = lax.rsqrt(jnp.sum(squares[k], axis=-1, keepdims=True) * (1.0 / D) + NORM_EPS)
        inv_out[k] = jnp.broadcast_to(inverse, (rows, 128))
        for c in range(D // width):
            for lane in range(width // 128):
                at = slice(c * width + lane * 128, c * width + (lane + 1) * 128)
                normal = sums[c][k][lane] * inverse
                n_out[k, :, at] = normal.astype(BF)
                x_out[k, :, at] = (normal * gains[k : k + 1, at]).astype(BF)


def front(history, mix_gain, mix_first, mix_second, mix_bias, gains):
    rows = 16
    return pl.pallas_call(
        front_kernel,
        grid=(ROWS // rows,),
        in_specs=[
            pl.BlockSpec((HISTORY, rows, D), lambda i: (0, i, 0)),
            pl.BlockSpec((1, ROWS, D), lambda i: (HISTORY - 1, 0, 0)),
            pl.BlockSpec((1, D), lambda i: (0, 0)),
            pl.BlockSpec((D, MIX), lambda i: (0, 0)),
            pl.BlockSpec((MIX, MIX), lambda i: (0, 0)),
            pl.BlockSpec((1, MIX), lambda i: (0, 0)),
            pl.BlockSpec((3, D), lambda i: (0, 0)),
        ],
        out_specs=[
            pl.BlockSpec((3, rows, D), lambda i: (0, i, 0)),
            pl.BlockSpec((3, rows, D), lambda i: (0, i, 0)),
            pl.BlockSpec((3, rows, 128), lambda i: (0, i, 0)),
            pl.BlockSpec((rows, D), lambda i: (i, 0)),
            pl.BlockSpec((ROWS, MIX), lambda i: (0, 0)),
            pl.BlockSpec((ROWS, MIX), lambda i: (0, 0)),
        ],
        out_shape=[
            jax.ShapeDtypeStruct((3, ROWS, D), BF),
            jax.ShapeDtypeStruct((3, ROWS, D), BF),
            jax.ShapeDtypeStruct((3, ROWS, 128), F32),
            jax.ShapeDtypeStruct((ROWS, D), F32),
            jax.ShapeDtypeStruct((ROWS, MIX), F32),
            jax.ShapeDtypeStruct((ROWS, MIX), F32),
        ],
        scratch_shapes=[VMEM((ROWS, MIX), F32)],
        compiler_params=pltpu.CompilerParams(vmem_limit_bytes=48 * MIB),
        name="front",
    )(history, history, mix_gain[None], mix_first, mix_second, mix_bias[None], gains)


def qkv_kernel(
    x, w_query, w_key, w_value, w_output, w_expand,
    heads, rows_out, w_out, wo_all, we_two,
    rows, weights, proj, g_send, g_recv, w_send, w_recv, f_send, f_recv, h_send, h_recv, local,
):
    enter([(Y1,), (Y3,), (SIB,), (XN,), (XN, 4), (DIAG,)])
    t = lax.axis_index("tensor")
    sources = [w_query, w_key, w_value, w_output, w_expand]
    slots = [lambda r, i=i: weights.at[i, r] for i in range(3)]
    slots += [lambda r: wo_all.at[r], lambda r: we_two.at[r - 1]]
    to_sib, to_x, onward = [], [], []
    for i, src in enumerate(sources):
        half = src.shape[0] // 2
        lo, hi = pl.ds(0, half), pl.ds(half, half)
        to_x.append(
            (
                rcopy(src.at[lo], slots[i](2).at[lo], w_send.at[i, 0], w_recv.at[i, 0], (XN,)),
                rcopy(src.at[hi], slots[i](2).at[hi], w_send.at[i, 1], w_recv.at[i, 1], (XN, 4)),
            )
        )
        to_sib.append(rcopy(src, slots[i](1), w_send.at[i, 2], w_recv.at[i, 2], (SIB,)))
        if i < 4:
            onward.append(rcopy(slots[i](2), slots[i](3), f_send.at[i], f_recv.at[i], (SIB,)))
    keep = [pltpu.make_async_copy(sources[i], slots[i](0), local.at[i]) for i in range(4)]
    gathers = [Gather(x.at[a], rows.at[a], g_send.at[a], g_recv.at[a]) for a in range(3)]
    for a in range(3):
        to_x[a][0].start()
        to_x[a][1].start()
        gathers[a].start()
        to_sib[a].start()
        keep[a].start()
    for i in (3, 4):
        to_x[i][0].start()
        to_x[i][1].start()
        to_sib[i].start()
    keep[3].start()
    for a in range(3):
        for c in to_x[a]:
            c.wait_recv()
        onward[a].start()
        gathers[a].forward()
    sends = []

    def project(a, s):
        block = x[a] if s == 0 else rows[a, s]
        for p in range(2):
            pair = jnp.concatenate([weights[a, 2 * p], weights[a, 2 * p + 1]], axis=1)
            y = nn(block, pair).astype(BF)
            proj[a, s, 2 * p] = y[:, :128]
            proj[a, s, 2 * p + 1] = y[:, 128:]
        place = flip(t, 2 * s)
        for r in range(4):
            src, dst = proj.at[a, s, r], heads.at[a, place]
            if r == 0:
                c = pltpu.make_async_copy(src, dst, h_send.at[a, s, 0])
            else:
                c = rcopy(src, dst, h_send.at[a, s, r], h_recv.at[a, s, r], (A_MASKS[r],))
            c.start()
            sends.append((r, c))

    for a in range(3):
        keep[a].wait()
        to_sib[a].wait_recv()
        onward[a].wait_recv()
        project(a, 0)
    store = []
    for a in range(3):
        c = pltpu.make_async_copy(weights.at[a], w_out.at[a], local.at[4 + a])
        c.start()
        store.append(c)
        c = pltpu.make_async_copy(x.at[a], rows_out.at[a, 0], local.at[7 + a])
        c.start()
        store.append(c)
    for a in range(3):
        for s in (1, 3):
            gathers[a].arrived(s)
            project(a, s)
    for c in to_x[3]:
        c.wait_recv()
    onward[3].start()
    for a in range(3):
        gathers[a].arrived(2)
        project(a, 2)
        c = pltpu.make_async_copy(rows.at[a, pl.ds(1, 3)], rows_out.at[a, pl.ds(1, 3)], local.at[10 + a])
        c.start()
        store.append(c)
    for g in gathers:
        g.finish()
    for r, c in sends:
        if r == 0:
            c.wait()
        else:
            c.wait_send()
    for r, c in sends:
        if r:
            c.wait_recv()
    for i in range(5):
        for c in to_x[i]:
            c.wait_send()
            if i > 3:
                c.wait_recv()
        to_sib[i].wait_send()
        if i > 2:
            to_sib[i].wait_recv()
    for i in range(4):
        onward[i].wait_send()
    onward[3].wait_recv()
    keep[3].wait()
    for c in store:
        c.wait()


def qkv(x, w_query, w_key, w_value, w_output, w_expand):
    dma = pltpu.SemaphoreType.DMA
    return pl.pallas_call(
        qkv_kernel,
        in_specs=[pl.BlockSpec(memory_space=VMEM)] + [pl.BlockSpec(memory_space=ANY)] * 5,
        out_specs=[pl.BlockSpec(memory_space=ANY)] * 5,
        out_shape=[
            jax.ShapeDtypeStruct((3, 16, ROWS, HEAD_DIM), BF),
            jax.ShapeDtypeStruct((3, 4, ROWS, D), BF),
            jax.ShapeDtypeStruct((3, 4, D, HEAD_DIM), BF),
            jax.ShapeDtypeStruct((4, HEAD_DIM, D), BF),
            jax.ShapeDtypeStruct((2, D, FF_SHARD), BF),
        ],
        scratch_shapes=[
            VMEM((3, 4, ROWS, D), BF),
            VMEM((3, 4, D, HEAD_DIM), BF),
            VMEM((3, 4, 4, ROWS, HEAD_DIM), BF),
            dma((3, 6)), dma((3, 6)), dma((5, 3)), dma((5, 3)), dma((4,)), dma((4,)), dma((3, 4, 4)), dma((3, 4, 4)), dma((13,)),
        ],
        compiler_params=pltpu.CompilerParams(collective_id=1, has_side_effects=True, vmem_limit_bytes=48 * MIB),
        cost_estimate=pl.CostEstimate(flops=6 * 512 * 2048 * 512, bytes_accessed=30 * MIB, transcendentals=0),
        name="qkv",
    )(x, w_query, w_key, w_value, w_output, w_expand)


def attend_kernel(q, k, v, first, ctx):
    tokens, step = q.shape[0], 256
    scale = HEAD_DIM ** (-0.5)
    for i in range(tokens // step):
        length = (i + 1) * step
        at = slice(i * step, length)
        scores = nt(q[at], k[:length]) * scale
        key_place = lax.broadcasted_iota(jnp.int32, (step, length), 1)
        query_place = lax.broadcasted_iota(jnp.int32, (step, 1), 0) + i * step
        allowed = (key_place >= first[at]) & (key_place <= query_place)
        scores = jnp.where(allowed, scores, MASKED)
        top = jnp.max(scores, axis=-1, keepdims=True)
        e = jnp.exp(scores - top)
        low = (e * (1.0 / jnp.sum(e, axis=-1, keepdims=True))).astype(BF)
        ctx[at] = nn(low, v[:length]).astype(BF)


def attend(q, k, v, first_column):
    full = pl.BlockSpec(memory_space=VMEM)
    return pl.pallas_call(
        attend_kernel,
        in_specs=[full] * 4,
        out_specs=full,
        out_shape=jax.ShapeDtypeStruct(q.shape, BF),
        compiler_params=pltpu.CompilerParams(vmem_limit_bytes=48 * MIB),
        cost_estimate=pl.CostEstimate(flops=4 * 2048 * 1024 * 128, bytes_accessed=4 * MIB, transcendentals=2048 * 1024),
        name="attend",
    )(q, k, v, first_column)


def attend_back_kernel(q, k, v, gc, first, dq, dk, dv, dk_sum, dv_sum):
    tokens, step = q.shape[0], 256
    scale = HEAD_DIM ** (-0.5)
    k_turned = k[...].astype(F32).T.astype(BF)
    for i in range(tokens // step):
        length = (i + 1) * step
        at = slice(i * step, length)
        scores = nt(k[:length], q[at]) * scale
        key_place = lax.broadcasted_iota(jnp.int32, (length, step), 0)
        query_place = lax.broadcasted_iota(jnp.int32, (1, step), 1) + i * step
        allowed = (key_place >= first[:, at]) & (key_place <= query_place)
        scores = jnp.where(allowed, scores, MASKED)
        top = jnp.max(scores, axis=0, keepdims=True)
        e = jnp.exp(scores - top)
        probs = e * (1.0 / jnp.sum(e, axis=0, keepdims=True))
        grad_probs = nt(v[:length], gc[at])
        delta = jnp.sum(grad_probs * probs, axis=0, keepdims=True)
        grad_scores = (probs * (grad_probs - delta)).astype(BF)
        low = probs.astype(BF)
        dq[at] = (nn(k_turned[:, :length], grad_scores) * scale).T.astype(BF)
        key_part = nn(grad_scores, q[at])
        value_part = nn(low, gc[at])
        if i:
            dk_sum[: i * step] += key_part[: i * step]
            dv_sum[: i * step] += value_part[: i * step]
        dk_sum[at] = key_part[i * step :]
        dv_sum[at] = value_part[i * step :]
    dk[...] = (dk_sum[...] * scale).astype(BF)
    dv[...] = dv_sum[...].astype(BF)


def attend_back(q, k, v, grad_context, first_row):
    full = pl.BlockSpec(memory_space=VMEM)
    return pl.pallas_call(
        attend_back_kernel,
        in_specs=[full] * 5,
        out_specs=[full] * 3,
        out_shape=[jax.ShapeDtypeStruct(q.shape, BF)] * 3,
        scratch_shapes=[VMEM(q.shape, F32)] * 2,
        compiler_params=pltpu.CompilerParams(vmem_limit_bytes=48 * MIB),
        cost_estimate=pl.CostEstimate(flops=10 * 2048 * 1024 * 128, bytes_accessed=8 * MIB, transcendentals=2048 * 1024),
        name="attend_back",
    )(q, k, v, grad_context, first_row)


def moved(x, mask):
    return x if mask == 0 else lax.ppermute(x, "tensor", [(i, i ^ mask) for i in range(16)])


def y_gather_plain(x):
    return jnp.stack([moved(x, 2 * s) for s in range(4)])


def y_sum_plain(parts):
    return sum(moved(parts[s].astype(BF), 2 * s).astype(F32) if s else parts[0] for s in range(4))


def to_rows_plain(heads):
    t = lax.axis_index("tensor")
    out = []
    for r in range(4):
        piece = jnp.stack([heads[(t ^ A_MASKS[r]) ^ (2 * s)] for s in range(4)])
        out.append(moved(piece, A_MASKS[r]))
    return jnp.stack(out, 1)


def to_heads_plain(rows):
    t = lax.axis_index("tensor")
    out = jnp.zeros((16, 128, 128), rows.dtype)
    for r in range(4):
        got = moved(rows[:, r], A_MASKS[r])
        for s in range(4):
            out = out.at[(t ^ A_MASKS[r]) ^ (2 * s)].set(got[s])
    return out


def mlp_plain(ctx, wo_all, resid, gain_mlp, cot, w_expand, we_two, w_reduce):
    ctx_rows = to_rows_plain(ctx)
    we = jnp.stack([w_expand, we_two[0], we_two[1], moved(we_two[1], SIB)])
    wr = jnp.stack([moved(w_reduce, m) for m in A_MASKS])
    cot_rows = y_gather_plain(cot)
    attended = y_sum_plain(jnp.einsum("srtd,rdo->sto", ctx_rows, wo_all, preferred_element_type=F32))
    middle = resid + attended
    inverse = lax.rsqrt(jnp.mean(middle * middle, -1, keepdims=True) + NORM_EPS)
    normal = middle * inverse
    mlp_rows = y_gather_plain((normal * gain_mlp).astype(BF))
    expanded = jnp.einsum("std,rdf->srtf", mlp_rows, we, preferred_element_type=F32)
    act, slope = gelu_parts(expanded)
    act = act.astype(BF)
    reduced = jnp.einsum("srtf,rfd->std", act, wr, preferred_element_type=F32)
    grad_active = jnp.einsum("std,rfd->srtf", cot_rows, wr, preferred_element_type=F32)
    gexp = (grad_active * slope).astype(BF)
    grad_wr = jnp.einsum("srtf,std->rfd", act, cot_rows, preferred_element_type=F32).astype(BF)
    grad_we = jnp.einsum("std,srtf->rdf", mlp_rows, gexp, preferred_element_type=F32).astype(BF)
    gmlp = y_sum_plain(jnp.einsum("srtf,rdf->std", gexp, we, preferred_element_type=F32))
    grad_gain = jnp.sum(gmlp * normal, 0, keepdims=True)
    scaled = gmlp * gain_mlp
    grad_middle = cot.astype(F32) + inverse * (scaled - normal * jnp.mean(scaled * normal, -1, keepdims=True))
    return ctx_rows, middle, reduced, grad_we, grad_wr, grad_gain, grad_middle


def out_back_plain(grad_middle, middle, reduced, ctx_rows, wo_all):
    gmid_rows = y_gather_plain(grad_middle.astype(BF))
    output = (middle + y_sum_plain(reduced)).astype(BF)
    gctx = jnp.einsum("std,rhd->srth", gmid_rows, wo_all, preferred_element_type=F32).astype(BF)
    grad_wo = jnp.einsum("srth,std->rhd", ctx_rows, gmid_rows, preferred_element_type=F32).astype(BF)
    return output, to_heads_plain(gctx), grad_wo


def streams_back_plain(grads, rows, w_all):
    dw, gs = [], []
    for a in range(3):
        g = to_rows_plain(grads[a])
        dw.append(jnp.einsum("std,srth->rdh", rows[a], g, preferred_element_type=F32).astype(BF))
        gs.append(y_sum_plain(jnp.einsum("srth,rdh->std", g, w_all[a], preferred_element_type=F32)))
    return jnp.stack(gs), jnp.stack(dw)


def weight_sum_plain(dw, split):
    own = y = sum(moved(dw[r], A_MASKS[r]).astype(F32) for r in range(4))
    return lax.psum_scatter(own, "dp", scatter_dimension=split, tiled=True)


def front_back_plain(history, gs, grad_middle, n, inv, mix, pre, mix_gain, mix_first, mix_second, gains):
    grads_gain, ds = [], []
    for k in range(3):
        normal = n[k].astype(F32)
        grads_gain.append(jnp.sum(gs[k] * normal, 0))
        scaled = gs[k] * gains[k]
        ds.append(inv[k][:, :1] * (scaled - normal * jnp.mean(scaled * normal, -1, keepdims=True)))
    ds = jnp.stack(ds + [grad_middle])
    h = history.astype(F32)
    gmix = jnp.einsum("ktd,jtd->tkj", ds, h, precision=PRECISE).reshape(ROWS, MIX)
    hidden, slope = gelu_parts(pre)
    last = h[HISTORY - 1]
    inverse = lax.rsqrt(jnp.mean(last * last, -1, keepdims=True) + NORM_EPS)
    normal = last * inverse
    latest = normal * mix_gain
    g_bias = gmix.sum(0)
    g_second = jnp.dot(hidden.T, gmix, precision=PRECISE)
    dpre = jnp.dot(gmix, mix_second.T, precision=PRECISE) * slope
    g_first = jnp.dot(latest.T, dpre, precision=PRECISE)
    dl = jnp.dot(dpre, mix_first.T, precision=PRECISE)
    g_gain = jnp.sum(dl * normal, 0)
    scaled = dl * mix_gain
    extra = inverse * (scaled - normal * jnp.mean(scaled * normal, -1, keepdims=True))
    gh = jnp.einsum("tkj,ktd->jtd", mix.reshape(ROWS, STREAMS, HISTORY), ds, precision=PRECISE)
    gh = gh.at[HISTORY - 1].add(extra).astype(BF)
    return gh, g_gain, g_first, g_second, g_bias, grads_gain[0], grads_gain[1], grads_gain[2]


def on_device(
    history, cotangent, lengths, mix_gain, mix_first, mix_second, mix_bias,
    gain_query, gain_key, gain_value, gain_mlp, w_query, w_key, w_value, w_output, w_expand, w_reduce,
):
    gains = jnp.stack([gain_query, gain_key, gain_value])
    row = lax.dynamic_index_in_dim(lengths, lax.axis_index("dp"), 0, keepdims=False)
    places = jnp.arange(2048, dtype=jnp.int32)
    first = jnp.zeros_like(places)
    end = jnp.int32(0)
    for i in range(lengths.shape[1]):
        end = end + row[i]
        first = jnp.where(places >= end, end, first)
    x, n, inv, resid, mix, pre = front(history, mix_gain, mix_first, mix_second, mix_bias, gains)
    heads, rows, w_all, wo_all, we_two = qkv(x, w_query, w_key, w_value, w_output, w_expand)
    q, k, v = [heads[a].reshape(2048, HEAD_DIM) for a in range(3)]
    ctx = attend(q, k, v, first[:, None]).reshape(16, ROWS, HEAD_DIM)
    ctx_rows, middle, reduced, grad_we, grad_wr, g_gain_mlp, grad_middle = mlp_plain(
        ctx, wo_all, resid, gain_mlp, cotangent, w_expand, we_two, w_reduce)
    output, gctx, grad_wo = out_back_plain(grad_middle, middle, reduced, ctx_rows, wo_all)
    dq, dk, dv = attend_back(q, k, v, gctx.reshape(2048, HEAD_DIM), first[None])
    gs, dw = streams_back_plain([z.reshape(16, ROWS, HEAD_DIM) for z in (dq, dk, dv)], rows, w_all)
    small = front_back_plain(history, gs, grad_middle, n, inv, mix, pre, mix_gain, mix_first, mix_second, gains)
    summed = lax.psum(small[1:] + (g_gain_mlp[0],), ("dp", "tensor"))
    return (output, small[0], *summed,
        weight_sum_plain(dw[0], 0), weight_sum_plain(dw[1], 0), weight_sum_plain(dw[2], 0),
        weight_sum_plain(grad_wo, 1), weight_sum_plain(grad_we, 0), weight_sum_plain(grad_wr, 1))


def solution(mesh):
    rows, cols, both = P("tensor", None), P(None, "tensor"), ("dp", "tensor")
    return jax.shard_map(
        on_device,
        mesh=mesh,
        in_specs=(P(None, both, None), P(both, None)) + (P(),) * 9 + (cols, cols, cols, rows, cols, rows),
        out_specs=(P(both, None), P(None, both, None)) + (P(),) * 8
        + (P("dp", "tensor"),) * 3 + (P("tensor", "dp"), P("dp", "tensor"), P("tensor", "dp")),
        check_vma=False,
    )
```

time: 1350 us -> 979 us (0.73)
  waiting for transfers between devices: 731 us -> 448 us
  matrix products: 235 us -> 115 us
  Pallas kernels: 0 us -> 97.9 us
  other arithmetic: 157 us -> 65.5 us
  local copies, waits for them, and re-layouts: 49.2 us -> 75.8 us
    reduce_scatter x6, waiting for transfers between devices: 176 us -> 0.01 us  [weight_sum_plain(): return lax.psum_scatter(own, 'dp', scatter_dimension=split, tiled=True)]
    dot_general x33 -> x21, matrix products: 235 us -> 115 us  [the longest x1 24.8 us: front_back_plain(): jnp.einsum('tkj,ktd->jtd', mix.reshape(ROWS, STREAMS, HISTORY), ds, preci...]
    pallas_call x0 -> x4, Pallas kernels: none -> 97.9 us  [the longest x1 69.3 us: qkv(): pl.pallas_call(qkv_kernel, in_specs=[pl.BlockSpec(memory_space=VMEM)] + [...]
    ppermute x52 -> x64, waiting for transfers between devices: 528 us -> 448 us  [moved(): lax.ppermute(x, 'tensor', [(i, i ^ mask) for i in range(16)])]
    convert_element_type x43 -> x3, other arithmetic: 70.6 us -> 15.8 us  [the longest x1 14.1 us: front_back_plain(): gh = gh.at[HISTORY - 1].add(extra).astype(BF)]
    psum x1, waiting for transfers between devices: 27.4 us -> 0.01 us  [on_device(): summed = lax.psum(small[1:] + (g_gain_mlp[0],), ('dp', 'tensor'))]
    select_n x18 -> x2, other arithmetic: 24.8 us -> 2.6 us  [on_device(): first = jnp.where(places >= end, end, first)]
    scatter-add x0 -> x1, local copies, waits for them, and re-layouts: none -> 20.6 us  [front_back_plain(): gh = gh.at[HISTORY - 1].add(extra).astype(BF)]
  transfers between devices with their start and end apart: 59 -> 71, of which waited for: 27 -> 35; matrix products, arithmetic and copies ran while one was open for 27% -> 21% of each run, Pallas kernels for 0% -> 0%
where the time goes in v1:
time: 979 us; the launch traced here: 971 us
  waiting for transfers between devices  448 us (46%)
  matrix products  115 us (12%)
  Pallas kernels  97.9 us (10%)
  starting transfers between devices  78.9 us (8%)
  local copies, waits for them, and re-layouts  75.8 us (8%)
  blocking collectives  69.6 us (7%)
  other arithmetic  65.5 us (7%)
  between operations  19.9 us (2%)
    ppermute x64, waiting for transfers between devices, moved(): lax.ppermute(x, 'tensor', [(i, i ^ mask) for i in range(16)])  448 us
    ppermute x64, starting transfers between devices, moved(): lax.ppermute(x, 'tensor', [(i, i ^ mask) for i in range(16)])  78.6 us
    psum x1, blocking collectives, on_device(): summed = lax.psum(small[1:] + (g_gain_mlp[0],), ('dp', 'tensor'))  69.6 us
    pallas_call x1, Pallas kernels, qkv(): pl.pallas_call(qkv_kernel, in_specs=[pl.BlockSpec(memory_space=VMEM)] + [...  69.3 us
    unnamed x201, local copies, waits for them, and re-layouts  39.8 us
    dot_general x1, matrix products, front_back_plain(): jnp.einsum('tkj,ktd->jtd', mix.reshape(ROWS, STREAMS, HISTORY), ds, preci...  24.8 us
    add x6, other arithmetic, weight_sum_plain(): own = y = sum((moved(dw[r], A_MASKS[r]).astype(F32) for r in range(4)))  22.3 us
    scatter-add x1, local copies, waits for them, and re-layouts, front_back_plain(): gh = gh.at[HISTORY - 1].add(extra).astype(BF)  20.6 us
  transfers between devices with their start and end apart: 71, of which 35 were waited for; matrix products, arithmetic and copies ran while one was open for 21% of the time, Pallas kernels for 0%

profile of v1, /device:TPU:1, one launch (start us, length us, event | category | flops | bytes accessed | tf_op | source)
XLA Modules:
  0.0 970.9 jit_solution(5101598680704346)
XLA Ops:
  18.2 11.4 %front.1 = (bf16[3,128,2048]{2,1,0:T(8,128)(2,1)S(1)}, bf16[3,128,2048]{2,1,0:T(8,128)(2,1)S(1)}, f32[3,128,128]{2,1,0:T(8,128)S(1)}, f32[128,2048]{1,0:T(8,128)...) custom-call(bf16[17,128,2048]{2,1,0:T(8,128)(2,1)} %latest.1, bf16[17,128,2048]{2,1,0:T(8,128)(2,1)} %latest.1, ...), custom_call_target="tpu_custom_call" | custom-call | tf_op jit(solution)/shard_map/front/pallas_call | solution.py:201
  30.5 69.3 %qkv.1 = (bf16[3,16,128,128]{3,2,1,0:T(8,128)(2,1)S(1)}, bf16[3,4,128,2048]{3,2,1,0:T(8,128)(2,1)}, bf16[3,4,2048,128]{3,2,1,0:T(8,128)(2,1)}, bf16[4,128,2048]{2,1,0:T(8,128)(2,1)}, bf16[2,2048,512]{2,1,0:T(8,128)(2,1)}) custom-call(bf16[3,128,2048]{2,1,0:T(8,128)(2,1)S(1)} %get-tuple-element.235.x, bf16[2048,128]{1,0:T(8,128)(2,1)S(1)} %copy-done.12, ...), custom_call_target="tpu_custom_call" | custom-call | flops 3221225472 | bytes 31457280 | tf_op jit(solution)/shard_map/qkv/pallas_call | solution.py:349
  103.0 6.6 attend.1
  112.4 3.0 collective-permute-done.1
  115.4 3.4 collective-permute-done.2
  124.5 12.5 %collective-permute-done.3 = bf16[128,2048]{1,0:T(8,128)(2,1)S(1)} collective-permute-done((bf16[128,2048]{1,0:T(8,128)(2,1)S(1)}, bf16[128,2048]{1,0:T(8,128)(2,1)S(1)}, u32[]{:S(2)}, u32[]{:S(2)}) %collective-permute-start.3) | collective-permute-done | bytes 524320 | tf_op jit(solution)/shard_map/ppermute | solution.py:448
  137.0 12.0 %collective-permute-done.4 = bf16[128,2048]{1,0:T(8,128)(2,1)S(1)} collective-permute-done((bf16[128,2048]{1,0:T(8,128)(2,1)S(1)}, bf16[128,2048]{1,0:T(8,128)(2,1)S(1)}, u32[]{:S(2)}, u32[]{:S(2)}) %collective-permute-start.4) | collective-permute-done | bytes 524320 | tf_op jit(solution)/shard_map/ppermute | solution.py:448
  153.6 9.9 %collective-permute-done.8 = bf16[128,2048]{1,0:T(8,128)(2,1)S(1)} collective-permute-done((bf16[128,2048]{1,0:T(8,128)(2,1)S(1)}, bf16[128,2048]{1,0:T(8,128)(2,1)S(1)}, u32[]{:S(2)}, u32[]{:S(2)}) %collective-permute-start.8) | collective-permute-done | bytes 524320 | tf_op jit(solution)/shard_map/ppermute | solution.py:448
  165.6 8.7 collective-permute-done.7
  176.0 11.2 %collective-permute-done.9 = bf16[128,2048]{1,0:T(8,128)(2,1)S(1)} collective-permute-done((bf16[128,2048]{1,0:T(8,128)(2,1)S(1)}, bf16[128,2048]{1,0:T(8,128)(2,1)S(1)}, u32[]{:S(2)}, u32[]{:S(2)}) %collective-permute-start.9) | collective-permute-done | bytes 524320 | tf_op jit(solution)/shard_map/ppermute | solution.py:448
  187.7 6.6 fusion.4
  194.4 18.3 %collective-permute-done.18 = bf16[128,2048]{1,0:T(8,128)(2,1)S(1)} collective-permute-done((bf16[128,2048]{1,0:T(8,128)(2,1)S(1)}, bf16[128,2048]{1,0:T(8,128)(2,1)S(1)}, u32[]{:S(2)}, u32[]{:S(2)}) %collective-permute-start.18) | collective-permute-done | bytes 524320 | tf_op jit(solution)/shard_map/ppermute | solution.py:448
  212.7 32.7 %collective-permute-done.11 = bf16[512,2048]{1,0:T(8,128)(2,1)S(1)} collective-permute-done((bf16[512,2048]{1,0:T(8,128)(2,1)S(1)}, bf16[512,2048]{1,0:T(8,128)(2,1)S(1)}, u32[]{:S(2)}, u32[]{:S(2)}) %collective-permute-start.11) | collective-permute-done | bytes 2097184 | tf_op jit(solution)/shard_map/ppermute | solution.py:448
  246.7 10.4 %fusion.10 = bf16[4,4,128,512]{2,3,0,1:T(8,128)(2,1)} fusion(f32[4,512,4,128]{3,1,2,0:T(8,128)} %fusion.4, bf16[1,512,2048]{2,1,0:T(8,128)(2,1)S(1)} %bitcast.572, bf16[1,512,2048]{2,1,0:T(8,128)(2,1)} %bitcast.574, bf16[1,512,2048]{2,1,0:T(8,128)(2,1)S(1)} %bitcast.570, bf16[1,512,2048]{2,1,0:T(8,128)(2,1)S(1)} %bitcast.567, ...), kind=kOutput, calls=%fused_computation.15 | convolution fusion | flops 4347396096 | bytes 16777216 | tf_op jit(solution)/shard_map/std,rfd->srtf/dot_general | solution.py:492
  257.1 6.2 fusion.171
  267.0 9.4 fusion.172
  280.0 8.6 collective-permute-done.20
  289.1 9.5 collective-permute-done.13
  298.6 14.0 %collective-permute-done.15 = bf16[128,2048]{1,0:T(8,128)(2,1)S(1)} collective-permute-done((bf16[128,2048]{1,0:T(8,128)(2,1)S(1)}, bf16[128,2048]{1,0:T(8,128)(2,1)S(1)}, u32[]{:S(2)}, u32[]{:S(2)}) %collective-permute-start.15) | collective-permute-done | bytes 524320 | tf_op jit(solution)/shard_map/ppermute | solution.py:448
  320.5 19.2 %collective-permute-done.24 = bf16[128,2048]{1,0:T(8,128)(2,1)S(1)} collective-permute-done((bf16[128,2048]{1,0:T(8,128)(2,1)S(1)}, bf16[128,2048]{1,0:T(8,128)(2,1)S(1)}, u32[]{:S(2)}, u32[]{:S(2)}) %collective-permute-start.24) | collective-permute-done | bytes 524320 | tf_op jit(solution)/shard_map/ppermute | solution.py:448
  356.0 10.6 %attend_back.1 = (bf16[2048,128]{1,0:T(8,128)(2,1)S(1)}, bf16[2048,128]{1,0:T(8,128)(2,1)S(1)}, bf16[2048,128]{1,0:T(8,128)(2,1)S(1)}) custom-call(bf16[2048,128]{1,0:T(8,128)(2,1)S(1)} %bitcast.527, bf16[2048,128]{1,0:T(8,128)(2,1)S(1)} %bitcast.525, bf16[2048,128]{1,0:T(8,128)(2,1)S(1)} %bitcast.523, bf16[2048,128]{1,0:T(8,128)(2,1)S(1)} %bitcast.519, ...), custom_call_target="tpu_custom_call" | custom-call | flops 2684354560 | bytes 8388608 | tf_op jit(solution)/shard_map/attend_back/pallas_call | solution.py:435
  372.7 3.6 collective-permute-done.29
  376.3 3.1 collective-permute-done.30
  384.3 2.7 fusion.27
  387.0 8.3 collective-permute-done.48
  395.3 11.0 %collective-permute-done.47 = bf16[2048,128]{0,1:T(8,128)(2,1)S(1)} collective-permute-done((bf16[2048,128]{0,1:T(8,128)(2,1)S(1)}, bf16[2048,128]{0,1:T(8,128)(2,1)S(1)}, u32[]{:S(2)}, u32[]{:S(2)}) %collective-permute-start.47) | collective-permute-done | bytes 524320 | tf_op jit(solution)/shard_map/ppermute | solution.py:448
  411.5 8.8 fusion.2
  425.5 11.9 %collective-permute-done.50 = bf16[2048,128]{0,1:T(8,128)(2,1)S(1)} collective-permute-done((bf16[2048,128]{0,1:T(8,128)(2,1)S(1)}, bf16[2048,128]{0,1:T(8,128)(2,1)S(1)}, u32[]{:S(2)}, u32[]{:S(2)}) %collective-permute-start.50) | collective-permute-done | bytes 524320 | tf_op jit(solution)/shard_map/ppermute | solution.py:448
  437.4 2.3 fusion.110
  440.2 4.2 collective-permute-done.42
  444.5 3.2 fusion.28
  449.8 2.8 slice_bitcast_fusion.6
  454.6 8.3 collective-permute-done.54
  462.9 12.4 %collective-permute-done.53 = bf16[2048,128]{0,1:T(8,128)(2,1)S(1)} collective-permute-done((bf16[2048,128]{0,1:T(8,128)(2,1)S(1)}, bf16[2048,128]{0,1:T(8,128)(2,1)S(1)}, u32[]{:S(2)}, u32[]{:S(2)}) %collective-permute-start.53) | collective-permute-done | bytes 524320 | tf_op jit(solution)/shard_map/ppermute | solution.py:448
  478.2 46.6 %collective-permute-done.60 = bf16[2048,512]{0,1:T(8,128)(2,1)} collective-permute-done((bf16[2048,512]{0,1:T(8,128)(2,1)}, bf16[2048,512]{0,1:T(8,128)(2,1)}, u32[]{:S(2)}, u32[]{:S(2)}) %collective-permute-start.60) | collective-permute-done | bytes 2097184 | tf_op jit(solution)/shard_map/ppermute | solution.py:448
  524.8 47.5 %collective-permute-done.59 = bf16[2048,512]{0,1:T(8,128)(2,1)} collective-permute-done((bf16[2048,512]{0,1:T(8,128)(2,1)}, bf16[2048,512]{0,1:T(8,128)(2,1)}, u32[]{:S(2)}, u32[]{:S(2)}) %collective-permute-start.59) | collective-permute-done | bytes 2097184 | tf_op jit(solution)/shard_map/ppermute | solution.py:448
  572.3 7.1 fusion.14
  579.5 7.0 bitcast_convert_fusion
  586.6 2.9 slice_bitcast_fusion.2
  589.5 2.4 copy-done.18
  591.9 3.1 fusion.173
  598.4 2.3 fusion.175
  604.3 3.8 collective-permute-done.37
  610.6 10.3 %collective-permute-done.38 = bf16[128,2048]{1,0:T(8,128)(2,1)S(1)} collective-permute-done((bf16[128,2048]{1,0:T(8,128)(2,1)S(1)}, bf16[128,2048]{1,0:T(8,128)(2,1)S(1)}, u32[]{:S(2)}, u32[]{:S(2)}) %collective-permute-start.38) | collective-permute-done | bytes 524320 | tf_op jit(solution)/shard_map/ppermute | solution.py:448
  621.7 8.9 collective-permute-done.43
  635.2 10.3 %collective-permute-start.61 = (bf16[512,2048]{1,0:T(8,128)(2,1)}, bf16[512,2048]{1,0:T(8,128)(2,1)}, u32[]{:S(2)}, u32[]{:S(2)}) collective-permute-start(bf16[512,2048]{1,0:T(8,128)(2,1)} %get-tuple-element.323), channel_id=1, source_target_pairs={{0,1},{1,0},{2,3},{3,2},{4,5},{5,4},{6,7},{7,6},{8,9},{9,8},{10,11... | collective-permute-start | bytes 6291464 | tf_op jit(solution)/shard_map/ppermute | solution.py:448
  646.6 6.5 collective-permute-done.31
  653.1 2.5 collective-permute-start.55
  655.6 10.5 %collective-permute-start.57 = (bf16[128,2048]{1,0:T(8,128)(2,1)}, bf16[128,2048]{1,0:T(8,128)(2,1)}, u32[]{:S(2)}, u32[]{:S(2)}) collective-permute-start(bf16[128,2048]{1,0:T(8,128)(2,1)} %get-tuple-element.332), channel_id=1, source_target_pairs={{0,9},{1,8},{2,11},{3,10},{4,13},{5,12},{6,15},{7,14},{8,1},{9,0},... | collective-permute-start | bytes 1572872 | tf_op jit(solution)/shard_map/ppermute | solution.py:448
  672.8 18.2 %fusion.176 = (f32[4,17]{1,0:T(4,128)S(1)}, f32[128,4,17]{2,1,0:T(4,128)S(1)}) fusion(bf16[17,128,2048]{2,1,0:T(8,128)(2,1)S(1)} %bitcast.534, f32[4,128,2048]{2,1,0:T(8,128)S(1)} %pad_maximum_fusion), kind=kOutput, calls=%fused_computation.428 | convolution fusion | flops 213918144 | bytes 13142288 | tf_op jit(solution)/shard_map/ktd,jtd->tkj/dot_general | solution.py:534
  692.2 2.8 fusion.66
  695.1 32.3 %collective-permute-done.57 = bf16[128,2048]{1,0:T(8,128)(2,1)} collective-permute-done((bf16[128,2048]{1,0:T(8,128)(2,1)}, bf16[128,2048]{1,0:T(8,128)(2,1)}, u32[]{:S(2)}, u32[]{:S(2)}) %collective-permute-start.57) | collective-permute-done | bytes 524320 | tf_op jit(solution)/shard_map/ppermute | solution.py:448
  727.4 16.9 %collective-permute-done.56 = bf16[128,2048]{1,0:T(8,128)(2,1)} collective-permute-done((bf16[128,2048]{1,0:T(8,128)(2,1)}, bf16[128,2048]{1,0:T(8,128)(2,1)}, u32[]{:S(2)}, u32[]{:S(2)}) %collective-permute-start.56) | collective-permute-done | bytes 524320 | tf_op jit(solution)/shard_map/ppermute | solution.py:448
  744.3 2.9 fusion.106
  747.2 46.7 %collective-permute-done.62 = bf16[512,2048]{1,0:T(8,128)(2,1)} collective-permute-done((bf16[512,2048]{1,0:T(8,128)(2,1)S(1)}, bf16[512,2048]{1,0:T(8,128)(2,1)}, u32[]{:S(2)}, u32[]{:S(2)}) %collective-permute-start.62) | collective-permute-done | bytes 2097184 | tf_op jit(solution)/shard_map/ppermute | solution.py:448
  794.0 7.3 fusion.12
  801.5 24.8 %fusion.20 = f32[128,2048,17]{1,2,0:T(8,128)S(1)} fusion(f32[128,4,17]{2,1,0:T(4,128)S(1)} %reshape.790, f32[4,128,2048]{2,1,0:T(8,128)} %copy-done.17), kind=kOutput, calls=%fused_computation.34 | convolution fusion | flops 213909504 | bytes 22054912 | tf_op jit(solution)/shard_map/tkj,ktd->jtd/dot_general | solution.py:548
  827.1 2.7 fusion.65
  829.8 2.2 fusion.64
  831.9 3.2 copy-done.16
  836.3 20.6 %scatter-add.4 = f32[17,128,2048]{2,0,1:T(8,128)} dynamic-update-slice(f32[17,128,2048]{2,0,1:T(8,128)} %bitcast.532, f32[1,128,2048]{2,0,1:T(1,128)S(1)} %copy.94, s32[]{:T(128)} %constant.391.clone.1, s32[]{:T(128)} %constant.388.clone.1, s32[]{:T(128)} %constant.388.clone.1) | dynamic-update-slice | bytes 2097156 | tf_op jit(solution)/shard_map/scatter-add | solution.py:549
  856.8 14.1 %convert_element_type.342 = bf16[17,128,2048]{2,0,1:T(8,128)(2,1)} convert(f32[17,128,2048]{2,0,1:T(8,128)} %scatter-add.4) | non-fusion elementwise | flops 4456448 | bytes 26738688 | tf_op jit(solution)/shard_map/convert_element_type | solution.py:549
  871.0 13.4 %copy.99 = bf16[17,128,2048]{2,1,0:T(8,128)(2,1)} copy(bf16[17,128,2048]{2,0,1:T(8,128)(2,1)} %convert_element_type.342) | data formatting | bytes 17825792
  884.6 69.6 %all-reduce = (f32[2048]{0:T(1024)}, f32[68,68]{1,0:T(8,128)}, f32[68]{0:T(128)}, f32[2048]{0:T(1024)}, f32[2048]{0:T(1024)}, /*index=5*/f32[2048]{0:T(1024)}, f32[2048]{0:T(1024)}) all-reduce(f32[2048]{0:T(1024)S(1)} %get-tuple-element.280, f32[68,68]{1,0:T(8,128)S(1)} %fusion.121, ...), channel_id=1, replica_groups=mesh['dp'=8,'tensor'=16] {'dp','tensor'}, use_global_device_ids=true, to_apply=%region_24.25 | all-reduce | flops 14932 | bytes 119456 | tf_op jit(solution)/shard_map/psum | solution.py:575
  (409 shorter events, 125.8 us)
Async XLA Ops:
  8.0 946.2 %reduce-scatter.7.cloned.1.call-start = ((), (), s32[]{:S(2)}) async-start(), calls=%async_computation.7 | async-start | bytes 1179648 | tf_op jit(solution)/shard_map/reduce_scatter | solution.py:522
  110.7 8.1 collective-permute-start.2
  112.3 41.1 %collective-permute-start.16 = (bf16[128,2048]{1,0:T(8,128)(2,1)S(1)}, bf16[128,2048]{1,0:T(8,128)(2,1)S(1)}, u32[]{:S(2)}, u32[]{:S(2)}) collective-permute-start(bf16[128,2048]{1,0:T(8,128)(2,1)S(1)} %copy-done.27), channel_id=1, source_target_pairs={{0,2},{1,3},{2,0},{3,1},{4,6},{5,7},{6,4},{7,5},{8,10},{9,11},{10,... | collective-permute-start | bytes 1572872 | tf_op jit(solution)/shard_map/ppermute | solution.py:448
  120.2 16.8 %collective-permute-start.3 = (bf16[128,2048]{1,0:T(8,128)(2,1)S(1)}, bf16[128,2048]{1,0:T(8,128)(2,1)S(1)}, u32[]{:S(2)}, u32[]{:S(2)}) collective-permute-start(bf16[128,2048]{1,0:T(8,128)(2,1)S(1)} %get-tuple-element.358), channel_id=1, source_target_pairs={{0,2},{1,3},{2,0},{3,1},{4,6},{5,7},{6,4},{7,5},{8,10},{9,11},{10,... | collective-permute-start | bytes 1572872 | tf_op jit(solution)/shard_map/ppermute | solution.py:448
  120.3 16.7 %collective-permute-start.5 = (bf16[128,2048]{1,0:T(8,128)(2,1)S(1)}, bf16[128,2048]{1,0:T(8,128)(2,1)S(1)}, u32[]{:S(2)}, u32[]{:S(2)}) collective-permute-start(bf16[128,2048]{1,0:T(8,128)(2,1)S(1)} %get-tuple-element.359), channel_id=1, source_target_pairs={{0,6},{1,7},{2,4},{3,5},{4,2},{5,3},{6,0},{7,1},{8,14},{9,15},{10,... | collective-permute-start | bytes 1572872 | tf_op jit(solution)/shard_map/ppermute | solution.py:448
  122.1 26.9 %collective-permute-start.4 = (bf16[128,2048]{1,0:T(8,128)(2,1)S(1)}, bf16[128,2048]{1,0:T(8,128)(2,1)S(1)}, u32[]{:S(2)}, u32[]{:S(2)}) collective-permute-start(bf16[128,2048]{1,0:T(8,128)(2,1)S(1)} %get-tuple-element.360), channel_id=1, source_target_pairs={{0,4},{1,5},{2,6},{3,7},{4,0},{5,1},{6,2},{7,3},{8,12},{9,13},{10,... | collective-permute-start | bytes 1572872 | tf_op jit(solution)/shard_map/ppermute | solution.py:448
  123.8 63.9 %collective-permute-start.6 = (bf16[2048,512]{1,0:T(8,128)(2,1)S(1)}, bf16[2048,512]{1,0:T(8,128)(2,1)S(1)}, u32[]{:S(2)}, u32[]{:S(2)}) collective-permute-start(bf16[2048,512]{1,0:T(8,128)(2,1)S(1)} %slice_bitcast_fusion.8), channel_id=1, source_target_pairs={{0,1},{1,0},{2,3},{3,2},{4,5},{5,4},{6,7},{7,6},{8,9},{9,8},{10,11... | collective-permute-start | bytes 6291464 | tf_op jit(solution)/shard_map/ppermute | solution.py:448
  149.6 13.9 %collective-permute-start.8 = (bf16[128,2048]{1,0:T(8,128)(2,1)S(1)}, bf16[128,2048]{1,0:T(8,128)(2,1)S(1)}, u32[]{:S(2)}, u32[]{:S(2)}) collective-permute-start(bf16[128,2048]{1,0:T(8,128)(2,1)S(1)} %multiply_convert_fusion), channel_id=1, source_target_pairs={{0,4},{1,5},{2,6},{3,7},{4,0},{5,1},{6,2},{7,3},{8,12},{9,13},{10,... | collective-permute-start | bytes 1572872 | tf_op jit(solution)/shard_map/ppermute | solution.py:448
  150.5 23.8 %collective-permute-start.7 = (bf16[128,2048]{1,0:T(8,128)(2,1)S(1)}, bf16[128,2048]{1,0:T(8,128)(2,1)S(1)}, u32[]{:S(2)}, u32[]{:S(2)}) collective-permute-start(bf16[128,2048]{1,0:T(8,128)(2,1)S(1)} %multiply_convert_fusion), channel_id=1, source_target_pairs={{0,2},{1,3},{2,0},{3,1},{4,6},{5,7},{6,4},{7,5},{8,10},{9,11},{10,... | collective-permute-start | bytes 1572872 | tf_op jit(solution)/shard_map/ppermute | solution.py:448
  152.0 60.7 %collective-permute-start.10 = (bf16[512,2048]{1,0:T(8,128)(2,1)S(1)}, bf16[512,2048]{1,0:T(8,128)(2,1)S(1)}, u32[]{:S(2)}, u32[]{:S(2)}) collective-permute-start(bf16[512,2048]{1,0:T(8,128)(2,1)S(1)} %copy-done.71), channel_id=1, source_target_pairs={{0,1},{1,0},{2,3},{3,2},{4,5},{5,4},{6,7},{7,6},{8,9},{9,8},{10,11... | collective-permute-start | bytes 6291464 | tf_op jit(solution)/shard_map/ppermute | solution.py:448
  153.4 59.3 %collective-permute-start.12 = (bf16[512,2048]{1,0:T(8,128)(2,1)S(1)}, bf16[512,2048]{1,0:T(8,128)(2,1)S(1)}, u32[]{:S(2)}, u32[]{:S(2)}) collective-permute-start(bf16[512,2048]{1,0:T(8,128)(2,1)S(1)} %copy-done.71), channel_id=1, source_target_pairs={{0,9},{1,8},{2,11},{3,10},{4,13},{5,12},{6,15},{7,14},{8,1},{9,0},... | collective-permute-start | bytes 6291464 | tf_op jit(solution)/shard_map/ppermute | solution.py:448
  163.6 81.8 %collective-permute-start.11 = (bf16[512,2048]{1,0:T(8,128)(2,1)S(1)}, bf16[512,2048]{1,0:T(8,128)(2,1)S(1)}, u32[]{:S(2)}, u32[]{:S(2)}) collective-permute-start(bf16[512,2048]{1,0:T(8,128)(2,1)S(1)} %copy-done.71), channel_id=1, source_target_pairs={{0,8},{1,9},{2,10},{3,11},{4,12},{5,13},{6,14},{7,15},{8,0},{9,1},... | collective-permute-start | bytes 6291464 | tf_op jit(solution)/shard_map/ppermute | solution.py:448
  174.3 12.9 %collective-permute-start.9 = (bf16[128,2048]{1,0:T(8,128)(2,1)S(1)}, bf16[128,2048]{1,0:T(8,128)(2,1)S(1)}, u32[]{:S(2)}, u32[]{:S(2)}) collective-permute-start(bf16[128,2048]{1,0:T(8,128)(2,1)S(1)} %multiply_convert_fusion), channel_id=1, source_target_pairs={{0,6},{1,7},{2,4},{3,5},{4,2},{5,3},{6,0},{7,1},{8,14},{9,15},{10,... | collective-permute-start | bytes 1572872 | tf_op jit(solution)/shard_map/ppermute | solution.py:448
  187.2 25.4 %collective-permute-start.18 = (bf16[128,2048]{1,0:T(8,128)(2,1)S(1)}, bf16[128,2048]{1,0:T(8,128)(2,1)S(1)}, u32[]{:S(2)}, u32[]{:S(2)}) collective-permute-start(bf16[128,2048]{1,0:T(8,128)(2,1)S(1)} %copy-done.27), channel_id=1, source_target_pairs={{0,6},{1,7},{2,4},{3,5},{4,2},{5,3},{6,0},{7,1},{8,14},{9,15},{10,... | collective-permute-start | bytes 1572872 | tf_op jit(solution)/shard_map/ppermute | solution.py:448
  187.7 25.0 %collective-permute-start.17 = (bf16[128,2048]{1,0:T(8,128)(2,1)S(1)}, bf16[128,2048]{1,0:T(8,128)(2,1)S(1)}, u32[]{:S(2)}, u32[]{:S(2)}) collective-permute-start(bf16[128,2048]{1,0:T(8,128)(2,1)S(1)} %copy-done.27), channel_id=1, source_target_pairs={{0,4},{1,5},{2,6},{3,7},{4,0},{5,1},{6,2},{7,3},{8,12},{9,13},{10,... | collective-permute-start | bytes 1572872 | tf_op jit(solution)/shard_map/ppermute | solution.py:448
  263.5 15.1 %collective-permute-start.19 = (bf16[128,2048]{1,0:T(8,128)(2,1)S(1)}, bf16[128,2048]{1,0:T(8,128)(2,1)S(1)}, u32[]{:S(2)}, u32[]{:S(2)}) collective-permute-start(bf16[128,2048]{1,0:T(8,128)(2,1)S(1)} %get-tuple-element.352), channel_id=1, source_target_pairs={{0,2},{1,3},{2,0},{3,1},{4,6},{5,7},{6,4},{7,5},{8,10},{9,11},{10,... | collective-permute-start | bytes 1572872 | tf_op jit(solution)/shard_map/ppermute | solution.py:448
  263.6 16.4 %collective-permute-start.21 = (bf16[128,2048]{1,0:T(8,128)(2,1)S(1)}, bf16[128,2048]{1,0:T(8,128)(2,1)S(1)}, u32[]{:S(2)}, u32[]{:S(2)}) collective-permute-start(bf16[128,2048]{1,0:T(8,128)(2,1)S(1)} %get-tuple-element.353), channel_id=1, source_target_pairs={{0,6},{1,7},{2,4},{3,5},{4,2},{5,3},{6,0},{7,1},{8,14},{9,15},{10,... | collective-permute-start | bytes 1572872 | tf_op jit(solution)/shard_map/ppermute | solution.py:448
  265.5 23.1 %collective-permute-start.20 = (bf16[128,2048]{1,0:T(8,128)(2,1)S(1)}, bf16[128,2048]{1,0:T(8,128)(2,1)S(1)}, u32[]{:S(2)}, u32[]{:S(2)}) collective-permute-start(bf16[128,2048]{1,0:T(8,128)(2,1)S(1)} %get-tuple-element.354), channel_id=1, source_target_pairs={{0,4},{1,5},{2,6},{3,7},{4,0},{5,1},{6,2},{7,3},{8,12},{9,13},{10,... | collective-permute-start | bytes 1572872 | tf_op jit(solution)/shard_map/ppermute | solution.py:448
  276.6 22.0 %collective-permute-start.13 = (bf16[128,2048]{1,0:T(8,128)(2,1)S(1)}, bf16[128,2048]{1,0:T(8,128)(2,1)S(1)}, u32[]{:S(2)}, u32[]{:S(2)}) collective-permute-start(bf16[128,2048]{1,0:T(8,128)(2,1)S(1)} %get-tuple-element.355), channel_id=1, source_target_pairs={{0,2},{1,3},{2,0},{3,1},{4,6},{5,7},{6,4},{7,5},{8,10},{9,11},{10,... | collective-permute-start | bytes 1572872 | tf_op jit(solution)/shard_map/ppermute | solution.py:448
  276.8 35.7 %collective-permute-start.15 = (bf16[128,2048]{1,0:T(8,128)(2,1)S(1)}, bf16[128,2048]{1,0:T(8,128)(2,1)S(1)}, u32[]{:S(2)}, u32[]{:S(2)}) collective-permute-start(bf16[128,2048]{1,0:T(8,128)(2,1)S(1)} %get-tuple-element.356), channel_id=1, source_target_pairs={{0,6},{1,7},{2,4},{3,5},{4,2},{5,3},{6,0},{7,1},{8,14},{9,15},{10,... | collective-permute-start | bytes 1572872 | tf_op jit(solution)/shard_map/ppermute | solution.py:448
  278.6 33.9 %collective-permute-start.14 = (bf16[128,2048]{1,0:T(8,128)(2,1)S(1)}, bf16[128,2048]{1,0:T(8,128)(2,1)S(1)}, u32[]{:S(2)}, u32[]{:S(2)}) collective-permute-start(bf16[128,2048]{1,0:T(8,128)(2,1)S(1)} %get-tuple-element.357), channel_id=1, source_target_pairs={{0,4},{1,5},{2,6},{3,7},{4,0},{5,1},{6,2},{7,3},{8,12},{9,13},{10,... | collective-permute-start | bytes 1572872 | tf_op jit(solution)/shard_map/ppermute | solution.py:448
  314.1 25.6 %collective-permute-start.24 = (bf16[128,2048]{1,0:T(8,128)(2,1)S(1)}, bf16[128,2048]{1,0:T(8,128)(2,1)S(1)}, u32[]{:S(2)}, u32[]{:S(2)}) collective-permute-start(bf16[128,2048]{1,0:T(8,128)(2,1)S(1)} %get-tuple-element.329), channel_id=1, source_target_pairs={{0,6},{1,7},{2,4},{3,5},{4,2},{5,3},{6,0},{7,1},{8,14},{9,15},{10,... | collective-permute-start | bytes 1572872 | tf_op jit(solution)/shard_map/ppermute | solution.py:448
  315.3 24.3 %collective-permute-start.23 = (bf16[128,2048]{1,0:T(8,128)(2,1)S(1)}, bf16[128,2048]{1,0:T(8,128)(2,1)S(1)}, u32[]{:S(2)}, u32[]{:S(2)}) collective-permute-start(bf16[128,2048]{1,0:T(8,128)(2,1)S(1)} %get-tuple-element.329), channel_id=1, source_target_pairs={{0,4},{1,5},{2,6},{3,7},{4,0},{5,1},{6,2},{7,3},{8,12},{9,13},{10,... | collective-permute-start | bytes 1572872 | tf_op jit(solution)/shard_map/ppermute | solution.py:448
  315.7 24.2 %collective-permute-start.22 = (bf16[128,2048]{1,0:T(8,128)(2,1)S(1)}, bf16[128,2048]{1,0:T(8,128)(2,1)S(1)}, u32[]{:S(2)}, u32[]{:S(2)}) collective-permute-start(bf16[128,2048]{1,0:T(8,128)(2,1)S(1)} %get-tuple-element.329), channel_id=1, source_target_pairs={{0,2},{1,3},{2,0},{3,1},{4,6},{5,7},{6,4},{7,5},{8,10},{9,11},{10,... | collective-permute-start | bytes 1572872 | tf_op jit(solution)/shard_map/ppermute | solution.py:448
  341.9 11.4 %collective-permute-start.27 = (bf16[4,128,128]{2,1,0:T(8,128)(2,1)S(1)}, bf16[4,128,128]{2,1,0:T(8,128)(2,1)S(1)}, u32[]{:S(2)}, u32[]{:S(2)}) collective-permute-start(bf16[4,128,128]{2,1,0:T(8,128)(2,1)S(1)} %get-tuple-element.416), channel_id=1, source_target_pairs={{0,9},{1,8},{2,11},{3,10},{4,13},{5,12},{6,15},{7,14},{8,1},{9,0},... | collective-permute-start | bytes 393224 | tf_op jit(solution)/shard_map/ppermute | solution.py:448
  343.3 7.3 collective-permute-start.26
  367.9 15.0 %collective-permute-start.36 = (bf16[4,128,128]{2,1,0:T(8,128)(2,1)S(1)}, bf16[4,128,128]{2,1,0:T(8,128)(2,1)S(1)}, u32[]{:S(2)}, u32[]{:S(2)}) collective-permute-start(bf16[4,128,128]{2,1,0:T(8,128)(2,1)S(1)} %pad_maximum_fusion.16), channel_id=1, source_target_pairs={{0,9},{1,8},{2,11},{3,10},{4,13},{5,12},{6,15},{7,14},{8,1},{9,0},... | collective-permute-start | bytes 393224 | tf_op jit(solution)/shard_map/ppermute | solution.py:448
  369.0 7.3 collective-permute-start.29
  370.5 8.9 collective-permute-start.30
  371.7 11.7 %collective-permute-start.35 = (bf16[4,128,128]{2,1,0:T(8,128)(2,1)S(1)}, bf16[4,128,128]{2,1,0:T(8,128)(2,1)S(1)}, u32[]{:S(2)}, u32[]{:S(2)}) collective-permute-start(bf16[4,128,128]{2,1,0:T(8,128)(2,1)S(1)} %pad_maximum_fusion.15), channel_id=1, source_target_pairs={{0,8},{1,9},{2,10},{3,11},{4,12},{5,13},{6,14},{7,15},{8,0},{9,1},... | collective-permute-start | bytes 393224 | tf_op jit(solution)/shard_map/ppermute | solution.py:448
  381.1 14.2 %collective-permute-start.48 = (bf16[2048,128]{0,1:T(8,128)(2,1)S(1)}, bf16[2048,128]{0,1:T(8,128)(2,1)S(1)}, u32[]{:S(2)}, u32[]{:S(2)}) collective-permute-start(bf16[2048,128]{0,1:T(8,128)(2,1)S(1)} %get-tuple-element.341), channel_id=1, source_target_pairs={{0,9},{1,8},{2,11},{3,10},{4,13},{5,12},{6,15},{7,14},{8,1},{9,0},... | collective-permute-start | bytes 1572872 | tf_op jit(solution)/shard_map/ppermute | solution.py:448
  382.0 24.3 %collective-permute-start.47 = (bf16[2048,128]{0,1:T(8,128)(2,1)S(1)}, bf16[2048,128]{0,1:T(8,128)(2,1)S(1)}, u32[]{:S(2)}, u32[]{:S(2)}) collective-permute-start(bf16[2048,128]{0,1:T(8,128)(2,1)S(1)} %get-tuple-element.342), channel_id=1, source_target_pairs={{0,8},{1,9},{2,10},{3,11},{4,12},{5,13},{6,14},{7,15},{8,0},{9,1},... | collective-permute-start | bytes 1572872 | tf_op jit(solution)/shard_map/ppermute | solution.py:448
  407.6 548.3 %reduce-scatter.9.cloned.1.call-start = ((), (), s32[]{:S(2)}) async-start(), calls=%async_computation.8 | async-start | bytes 1179648 | tf_op jit(solution)/shard_map/reduce_scatter | solution.py:522
  409.1 14.5 %collective-permute-start.49 = (bf16[2048,128]{0,1:T(8,128)(2,1)S(1)}, bf16[2048,128]{0,1:T(8,128)(2,1)S(1)}, u32[]{:S(2)}, u32[]{:S(2)}) collective-permute-start(bf16[2048,128]{0,1:T(8,128)(2,1)S(1)} %get-tuple-element.337), channel_id=1, source_target_pairs={{0,1},{1,0},{2,3},{3,2},{4,5},{5,4},{6,7},{7,6},{8,9},{9,8},{10,11... | collective-permute-start | bytes 1572872 | tf_op jit(solution)/shard_map/ppermute | solution.py:448
  409.9 15.6 %collective-permute-start.51 = (bf16[2048,128]{0,1:T(8,128)(2,1)S(1)}, bf16[2048,128]{0,1:T(8,128)(2,1)S(1)}, u32[]{:S(2)}, u32[]{:S(2)}) collective-permute-start(bf16[2048,128]{0,1:T(8,128)(2,1)S(1)} %get-tuple-element.338), channel_id=1, source_target_pairs={{0,9},{1,8},{2,11},{3,10},{4,13},{5,12},{6,15},{7,14},{8,1},{9,0},... | collective-permute-start | bytes 1572872 | tf_op jit(solution)/shard_map/ppermute | solution.py:448
  410.6 26.9 %collective-permute-start.50 = (bf16[2048,128]{0,1:T(8,128)(2,1)S(1)}, bf16[2048,128]{0,1:T(8,128)(2,1)S(1)}, u32[]{:S(2)}, u32[]{:S(2)}) collective-permute-start(bf16[2048,128]{0,1:T(8,128)(2,1)S(1)} %get-tuple-element.339), channel_id=1, source_target_pairs={{0,8},{1,9},{2,10},{3,11},{4,12},{5,13},{6,14},{7,15},{8,0},{9,1},... | collective-permute-start | bytes 1572872 | tf_op jit(solution)/shard_map/ppermute | solution.py:448
  421.0 18.8 %collective-permute-start.40 = (bf16[4,128,128]{2,1,0:T(8,128)(2,1)}, bf16[4,128,128]{2,1,0:T(8,128)(2,1)S(1)}, u32[]{:S(2)}, u32[]{:S(2)}) collective-permute-start(bf16[4,128,128]{2,1,0:T(8,128)(2,1)} %pad_maximum_fusion.17), channel_id=1, source_target_pairs={{0,1},{1,0},{2,3},{3,2},{4,5},{5,4},{6,7},{7,6},{8,9},{9,8},{10,11... | collective-permute-start | bytes 393224 | tf_op jit(solution)/shard_map/ppermute | solution.py:448
  422.4 17.8 %collective-permute-start.41 = (bf16[4,128,128]{2,1,0:T(8,128)(2,1)}, bf16[4,128,128]{2,1,0:T(8,128)(2,1)}, u32[]{:S(2)}, u32[]{:S(2)}) collective-permute-start(bf16[4,128,128]{2,1,0:T(8,128)(2,1)} %pad_maximum_fusion.18), channel_id=1, source_target_pairs={{0,8},{1,9},{2,10},{3,11},{4,12},{5,13},{6,14},{7,15},{8,0},{9,1},... | collective-permute-start | bytes 393224 | tf_op jit(solution)/shard_map/ppermute | solution.py:448
  423.7 20.8 %collective-permute-start.42 = (bf16[4,128,128]{2,1,0:T(8,128)(2,1)}, bf16[4,128,128]{2,1,0:T(8,128)(2,1)}, u32[]{:S(2)}, u32[]{:S(2)}) collective-permute-start(bf16[4,128,128]{2,1,0:T(8,128)(2,1)} %pad_maximum_fusion.19), channel_id=1, source_target_pairs={{0,9},{1,8},{2,11},{3,10},{4,13},{5,12},{6,15},{7,14},{8,1},{9,0},... | collective-permute-start | bytes 393224 | tf_op jit(solution)/shard_map/ppermute | solution.py:448
  439.8 517.8 %reduce-scatter.11.cloned.1.call-start = ((), (), s32[]{:S(2)}) async-start(), calls=%async_computation.9 | async-start | bytes 1179648 | tf_op jit(solution)/shard_map/reduce_scatter | solution.py:522
  447.9 15.0 %collective-permute-start.54 = (bf16[2048,128]{0,1:T(8,128)(2,1)S(1)}, bf16[2048,128]{0,1:T(8,128)(2,1)S(1)}, u32[]{:S(2)}, u32[]{:S(2)}) collective-permute-start(bf16[2048,128]{0,1:T(8,128)(2,1)S(1)} %get-tuple-element.335), channel_id=1, source_target_pairs={{0,9},{1,8},{2,11},{3,10},{4,13},{5,12},{6,15},{7,14},{8,1},{9,0},... | collective-permute-start | bytes 1572872 | tf_op jit(solution)/shard_map/ppermute | solution.py:448
  448.4 26.9 %collective-permute-start.53 = (bf16[2048,128]{0,1:T(8,128)(2,1)S(1)}, bf16[2048,128]{0,1:T(8,128)(2,1)S(1)}, u32[]{:S(2)}, u32[]{:S(2)}) collective-permute-start(bf16[2048,128]{0,1:T(8,128)(2,1)S(1)} %get-tuple-element.336), channel_id=1, source_target_pairs={{0,8},{1,9},{2,10},{3,11},{4,12},{5,13},{6,14},{7,15},{8,0},{9,1},... | collective-permute-start | bytes 1572872 | tf_op jit(solution)/shard_map/ppermute | solution.py:448
  452.6 25.6 %collective-permute-start.58 = (bf16[2048,512]{0,1:T(8,128)(2,1)}, bf16[2048,512]{0,1:T(8,128)(2,1)}, u32[]{:S(2)}, u32[]{:S(2)}) collective-permute-start(bf16[2048,512]{0,1:T(8,128)(2,1)} %get-tuple-element.326), channel_id=1, source_target_pairs={{0,1},{1,0},{2,3},{3,2},{4,5},{5,4},{6,7},{7,6},{8,9},{9,8},{10,11... | collective-permute-start | bytes 6291464 | tf_op jit(solution)/shard_map/ppermute | solution.py:448
  453.0 71.8 %collective-permute-start.60 = (bf16[2048,512]{0,1:T(8,128)(2,1)}, bf16[2048,512]{0,1:T(8,128)(2,1)}, u32[]{:S(2)}, u32[]{:S(2)}) collective-permute-start(bf16[2048,512]{0,1:T(8,128)(2,1)} %get-tuple-element.327), channel_id=1, source_target_pairs={{0,9},{1,8},{2,11},{3,10},{4,13},{5,12},{6,15},{7,14},{8,1},{9,0},... | collective-permute-start | bytes 6291464 | tf_op jit(solution)/shard_map/ppermute | solution.py:448
  453.3 119.0 %collective-permute-start.59 = (bf16[2048,512]{0,1:T(8,128)(2,1)}, bf16[2048,512]{0,1:T(8,128)(2,1)}, u32[]{:S(2)}, u32[]{:S(2)}) collective-permute-start(bf16[2048,512]{0,1:T(8,128)(2,1)} %get-tuple-element.328), channel_id=1, source_target_pairs={{0,8},{1,9},{2,10},{3,11},{4,12},{5,13},{6,14},{7,15},{8,0},{9,1},... | collective-permute-start | bytes 6291464 | tf_op jit(solution)/shard_map/ppermute | solution.py:448
  476.6 482.6 %reduce-scatter.15.cloned.1.call-start = ((), (), s32[]{:S(2)}) async-start(), calls=%async_computation.11 | async-start | bytes 4718592 | tf_op jit(solution)/shard_map/reduce_scatter | solution.py:522
  579.5 381.8 %all-reduce.3.cloned.1.call-start = ((), (), s32[]{:S(2)}) async-start(), calls=%async_computation.6 | async-start | bytes 1179648 | tf_op jit(solution)/shard_map/psum | solution.py:575
  595.1 13.0 %collective-permute-start.37 = (bf16[128,2048]{1,0:T(8,128)(2,1)S(1)}, bf16[128,2048]{1,0:T(8,128)(2,1)S(1)}, u32[]{:S(2)}, u32[]{:S(2)}) collective-permute-start(bf16[128,2048]{1,0:T(8,128)(2,1)S(1)} %get-tuple-element.349), channel_id=1, source_target_pairs={{0,2},{1,3},{2,0},{3,1},{4,6},{5,7},{6,4},{7,5},{8,10},{9,11},{10,... | collective-permute-start | bytes 1572872 | tf_op jit(solution)/shard_map/ppermute | solution.py:448
  595.2 14.7 %collective-permute-start.39 = (bf16[128,2048]{1,0:T(8,128)(2,1)S(1)}, bf16[128,2048]{1,0:T(8,128)(2,1)S(1)}, u32[]{:S(2)}, u32[]{:S(2)}) collective-permute-start(bf16[128,2048]{1,0:T(8,128)(2,1)S(1)} %get-tuple-element.350), channel_id=1, source_target_pairs={{0,6},{1,7},{2,4},{3,5},{4,2},{5,3},{6,0},{7,1},{8,14},{9,15},{10,... | collective-permute-start | bytes 1572872 | tf_op jit(solution)/shard_map/ppermute | solution.py:448
  597.0 23.9 %collective-permute-start.38 = (bf16[128,2048]{1,0:T(8,128)(2,1)S(1)}, bf16[128,2048]{1,0:T(8,128)(2,1)S(1)}, u32[]{:S(2)}, u32[]{:S(2)}) collective-permute-start(bf16[128,2048]{1,0:T(8,128)(2,1)S(1)} %get-tuple-element.351), channel_id=1, source_target_pairs={{0,4},{1,5},{2,6},{3,7},{4,0},{5,1},{6,2},{7,3},{8,12},{9,13},{10,... | collective-permute-start | bytes 1572872 | tf_op jit(solution)/shard_map/ppermute | solution.py:448
  600.9 29.7 %collective-permute-start.43 = (bf16[128,2048]{1,0:T(8,128)(2,1)S(1)}, bf16[128,2048]{1,0:T(8,128)(2,1)S(1)}, u32[]{:S(2)}, u32[]{:S(2)}) collective-permute-start(bf16[128,2048]{1,0:T(8,128)(2,1)S(1)} %get-tuple-element.343), channel_id=1, source_target_pairs={{0,2},{1,3},{2,0},{3,1},{4,6},{5,7},{6,4},{7,5},{8,10},{9,11},{10,... | collective-permute-start | bytes 1572872 | tf_op jit(solution)/shard_map/ppermute | solution.py:448
  602.4 32.8 %collective-permute-start.45 = (bf16[128,2048]{1,0:T(8,128)(2,1)S(1)}, bf16[128,2048]{1,0:T(8,128)(2,1)S(1)}, u32[]{:S(2)}, u32[]{:S(2)}) collective-permute-start(bf16[128,2048]{1,0:T(8,128)(2,1)S(1)} %get-tuple-element.344), channel_id=1, source_target_pairs={{0,6},{1,7},{2,4},{3,5},{4,2},{5,3},{6,0},{7,1},{8,14},{9,15},{10,... | collective-permute-start | bytes 1572872 | tf_op jit(solution)/shard_map/ppermute | solution.py:448
  608.1 37.4 %collective-permute-start.44 = (bf16[128,2048]{1,0:T(8,128)(2,1)S(1)}, bf16[128,2048]{1,0:T(8,128)(2,1)S(1)}, u32[]{:S(2)}, u32[]{:S(2)}) collective-permute-start(bf16[128,2048]{1,0:T(8,128)(2,1)S(1)} %get-tuple-element.345), channel_id=1, source_target_pairs={{0,4},{1,5},{2,6},{3,7},{4,0},{5,1},{6,2},{7,3},{8,12},{9,13},{10,... | collective-permute-start | bytes 1572872 | tf_op jit(solution)/shard_map/ppermute | solution.py:448
  609.9 43.3 %collective-permute-start.31 = (bf16[128,2048]{1,0:T(8,128)(2,1)S(1)}, bf16[128,2048]{1,0:T(8,128)(2,1)S(1)}, u32[]{:S(2)}, u32[]{:S(2)}) collective-permute-start(bf16[128,2048]{1,0:T(8,128)(2,1)S(1)} %get-tuple-element.346), channel_id=1, source_target_pairs={{0,2},{1,3},{2,0},{3,1},{4,6},{5,7},{6,4},{7,5},{8,10},{9,11},{10,... | collective-permute-start | bytes 1572872 | tf_op jit(solution)/shard_map/ppermute | solution.py:448
  620.9 34.7 %collective-permute-start.33 = (bf16[128,2048]{1,0:T(8,128)(2,1)S(1)}, bf16[128,2048]{1,0:T(8,128)(2,1)S(1)}, u32[]{:S(2)}, u32[]{:S(2)}) collective-permute-start(bf16[128,2048]{1,0:T(8,128)(2,1)S(1)} %get-tuple-element.347), channel_id=1, source_target_pairs={{0,6},{1,7},{2,4},{3,5},{4,2},{5,3},{6,0},{7,1},{8,14},{9,15},{10,... | collective-permute-start | bytes 1572872 | tf_op jit(solution)/shard_map/ppermute | solution.py:448
  630.6 35.4 %collective-permute-start.32 = (bf16[128,2048]{1,0:T(8,128)(2,1)S(1)}, bf16[128,2048]{1,0:T(8,128)(2,1)S(1)}, u32[]{:S(2)}, u32[]{:S(2)}) collective-permute-start(bf16[128,2048]{1,0:T(8,128)(2,1)S(1)} %get-tuple-element.348), channel_id=1, source_target_pairs={{0,4},{1,5},{2,6},{3,7},{4,0},{5,1},{6,2},{7,3},{8,12},{9,13},{10,... | collective-permute-start | bytes 1572872 | tf_op jit(solution)/shard_map/ppermute | solution.py:448
  635.2 112.0 %collective-permute-start.61 = (bf16[512,2048]{1,0:T(8,128)(2,1)}, bf16[512,2048]{1,0:T(8,128)(2,1)}, u32[]{:S(2)}, u32[]{:S(2)}) collective-permute-start(bf16[512,2048]{1,0:T(8,128)(2,1)} %get-tuple-element.323), channel_id=1, source_target_pairs={{0,1},{1,0},{2,3},{3,2},{4,5},{5,4},{6,7},{7,6},{8,9},{9,8},{10,11... | collective-permute-start | bytes 6291464 | tf_op jit(solution)/shard_map/ppermute | solution.py:448
  645.6 101.7 %collective-permute-start.63 = (bf16[512,2048]{1,0:T(8,128)(2,1)}, bf16[512,2048]{1,0:T(8,128)(2,1)}, u32[]{:S(2)}, u32[]{:S(2)}) collective-permute-start(bf16[512,2048]{1,0:T(8,128)(2,1)} %get-tuple-element.324), channel_id=1, source_target_pairs={{0,9},{1,8},{2,11},{3,10},{4,13},{5,12},{6,15},{7,14},{8,1},{9,0},... | collective-permute-start | bytes 6291464 | tf_op jit(solution)/shard_map/ppermute | solution.py:448
  653.1 38.3 %collective-permute-start.55 = (bf16[128,2048]{1,0:T(8,128)(2,1)}, bf16[128,2048]{1,0:T(8,128)(2,1)}, u32[]{:S(2)}, u32[]{:S(2)}) collective-permute-start(bf16[128,2048]{1,0:T(8,128)(2,1)} %get-tuple-element.331), channel_id=1, source_target_pairs={{0,1},{1,0},{2,3},{3,2},{4,5},{5,4},{6,7},{7,6},{8,9},{9,8},{10,11... | collective-permute-start | bytes 1572872 | tf_op jit(solution)/shard_map/ppermute | solution.py:448
  655.6 71.8 %collective-permute-start.57 = (bf16[128,2048]{1,0:T(8,128)(2,1)}, bf16[128,2048]{1,0:T(8,128)(2,1)}, u32[]{:S(2)}, u32[]{:S(2)}) collective-permute-start(bf16[128,2048]{1,0:T(8,128)(2,1)} %get-tuple-element.332), channel_id=1, source_target_pairs={{0,9},{1,8},{2,11},{3,10},{4,13},{5,12},{6,15},{7,14},{8,1},{9,0},... | collective-permute-start | bytes 1572872 | tf_op jit(solution)/shard_map/ppermute | solution.py:448
  666.1 78.2 %collective-permute-start.56 = (bf16[128,2048]{1,0:T(8,128)(2,1)}, bf16[128,2048]{1,0:T(8,128)(2,1)}, u32[]{:S(2)}, u32[]{:S(2)}) collective-permute-start(bf16[128,2048]{1,0:T(8,128)(2,1)} %get-tuple-element.333), channel_id=1, source_target_pairs={{0,8},{1,9},{2,10},{3,11},{4,12},{5,13},{6,14},{7,15},{8,0},{9,1},... | collective-permute-start | bytes 1572872 | tf_op jit(solution)/shard_map/ppermute | solution.py:448
  691.4 102.5 %collective-permute-start.62 = (bf16[512,2048]{1,0:T(8,128)(2,1)S(1)}, bf16[512,2048]{1,0:T(8,128)(2,1)}, u32[]{:S(2)}, u32[]{:S(2)}) collective-permute-start(bf16[512,2048]{1,0:T(8,128)(2,1)S(1)} %copy-done.23), channel_id=1, source_target_pairs={{0,8},{1,9},{2,10},{3,11},{4,12},{5,13},{6,14},{7,15},{8,0},{9,1},... | collective-permute-start | bytes 6291464 | tf_op jit(solution)/shard_map/ppermute | solution.py:448
  695.0 266.2 %reduce-scatter.13.cloned.1.call-start = ((), (), s32[]{:S(2)}) async-start(), calls=%async_computation.10 | async-start | bytes 1179648 | tf_op jit(solution)/shard_map/reduce_scatter | solution.py:522
  747.2 214.1 %reduce-scatter.17.cloned.1.call-start = ((), (), s32[]{:S(2)}) async-start(), calls=%async_computation.12 | async-start | bytes 4718592 | tf_op jit(solution)/shard_map/reduce_scatter | solution.py:522
  (104 other events, 1811.6 us)
Sparse Core Ops, SparseCore 0:
  407.8 73.4 reduce-scatter.6
  484.8 73.3 reduce-scatter.8
  562.2 69.9 reduce-scatter.10
  635.9 115.5 reduce-scatter.14
  755.9 70.8 reduce-scatter.12
  831.0 84.3 reduce-scatter.16
Sparse Core Ops, SparseCore 1:
  695.1 167.4 all-reduce.2

commit v2 on v1

--- a/solution.py
+++ b/solution.py
@@ -386,24 +386,13 @@
         ctx[at] = nn(low, v[:length]).astype(BF)
 
 
-def attend(q, k, v, first_column):
-    full = pl.BlockSpec(memory_space=VMEM)
-    return pl.pallas_call(
-        attend_kernel,
-        in_specs=[full] * 4,
-        out_specs=full,
-        out_shape=jax.ShapeDtypeStruct(q.shape, BF),
-        compiler_params=pltpu.CompilerParams(vmem_limit_bytes=48 * MIB),
-        cost_estimate=pl.CostEstimate(flops=4 * 2048 * 1024 * 128, bytes_accessed=4 * MIB, transcendentals=2048 * 1024),
-        name="attend",
-    )(q, k, v, first_column)
-
-
-def attend_back_kernel(q, k, v, gc, first, dq, dk, dv, dk_sum, dv_sum):
+def attend_back_kernel(q, k, v, gc, first, dq, dk, dv, dk_sum, dv_sum, hooks):
     tokens, step = q.shape[0], 256
     scale = HEAD_DIM ** (-0.5)
     k_turned = k[...].astype(F32).T.astype(BF)
     for i in range(tokens // step):
+        if i in hooks:
+            hooks[i]()
         length = (i + 1) * step
         at = slice(i * step, length)
         scores = nt(k[:length], q[at]) * scale
@@ -430,124 +419,798 @@
     dv[...] = dv_sum[...].astype(BF)
 
 
-def attend_back(q, k, v, grad_context, first_row):
-    full = pl.BlockSpec(memory_space=VMEM)
+def mlp_kernel(
+    q, k, v, first_place, wo_all, resid, gain, cot, w_expand, we_two, w_reduce,
+    ctx_rows, middle_out, reduced_out, keep_out, sib_out, grad_gain, grad_middle, grad_low,
+    ctx, we, wr, mlp_rows, cot_rows, act, gexp, turned, parts, stage, sc_out, sc_pass, sc_got,
+    g_send, g_recv, s_send, s_recv, w_send, w_recv, c_send, c_recv, d_send, d_recv, local,
+):
+    enter([(Y1,), (Y3,), (SIB,), (XN,), (XN, 4), (DIAG,)])
+    t = lax.axis_index("tensor")
+    cot_gather = Gather(cot, cot_rows, g_send.at[0], g_recv.at[0])
+    cot_gather.start()
+    half = FF_SHARD // 2
+    lo, hi = pl.ds(0, half), pl.ds(half, half)
+    loads = [
+        pltpu.make_async_copy(w_expand, we.at[0], local.at[0]),
+        pltpu.make_async_copy(we_two, we.at[pl.ds(1, 2)], local.at[1]),
+        pltpu.make_async_copy(w_reduce, wr.at[0], local.at[2]),
+    ]
+    for c in loads:
+        c.start()
+    sib = [
+        rcopy(we_two.at[1], we.at[3], w_send.at[0], w_recv.at[0], (SIB,)),
+        rcopy(w_reduce, wr.at[1], w_send.at[1], w_recv.at[1], (SIB,)),
+        rcopy(wr.at[2], wr.at[3], w_send.at[2], w_recv.at[2], (SIB,)),
+    ]
+    across = [
+        rcopy(w_reduce.at[lo], wr.at[2, lo], w_send.at[3], w_recv.at[3], (XN,)),
+        rcopy(w_reduce.at[hi], wr.at[2, hi], w_send.at[4], w_recv.at[4], (XN, 4)),
+    ]
+    sib[0].start()
+    sib[1].start()
+    cot_gather.forward()
+    attend_kernel(q, k, v, first_place, ctx)
+    back = {}
+    for s in (2, 1, 3, 0):
+        for r in range(4):
+            place = pl.multiple_of(flip(t, A_MASKS[r] + 2 * s) * ROWS, ROWS)
+            src, dst = ctx.at[pl.ds(place, ROWS)], ctx_rows.at[s, r]
+            if r:
+                back[s, r] = rcopy(src, dst, c_send.at[s, r], c_recv.at[s, r], (A_MASKS[r],))
+            else:
+                back[s, r] = pltpu.make_async_copy(src, dst, c_send.at[s, r])
+            back[s, r].start()
+    for c in across:
+        c.start()
+
+    def rows_of(s):
+        for r in range(4):
+            back[s, r].wait_recv() if r else back[s, r].wait()
+        return jnp.concatenate([ctx_rows[s, r] for r in range(4)], axis=1)
+
+    weight = wo_all[...].reshape(4 * HEAD_DIM, D)
+
+    def scatter(index, part_of):
+        sc = Scatter(sc_out.at[index], sc_pass.at[index], sc_got.at[index], s_send.at[index], s_recv.at[index])
+        part_of(2, parts.at[0])
+        sc.opposite(parts[0])
+        part_of(1, parts.at[1])
+        sc.first(parts[1])
+        part_of(3, parts.at[2])
+        sc.second(parts[2])
+        sc.relay(parts.at[1], parts.at[2])
+        part_of(0, parts.at[0])
+        return sc
+
+    def attended(s, into):
+        into[...] = nn(rows_of(s), weight)
+
+    sc = scatter(0, attended)
+    for c in across:
+        c.wait_recv()
+    sib[2].start()
+    middle = resid[...] + parts[0] + sc.total()
+    middle_out[...] = middle
+    inverse = lax.rsqrt(jnp.mean(middle * middle, axis=-1, keepdims=True) + NORM_EPS)
+    mlp_rows[0] = (middle * inverse * gain[...]).astype(BF)
+    mlp_gather = Gather(mlp_rows.at[0], mlp_rows, g_send.at[1], g_recv.at[1])
+    mlp_gather.start()
+    for c in loads:
+        c.wait()
+    for c in sib:
+        c.wait_recv()
+    cot_rows[0] = cot[...]
+
+    def block(s):
+        @pl.loop(0, 4)
+        def _(r):
+            expanded = nn(mlp_rows[s], we[r])
+            grad_active = nt(cot_rows[s], wr[r])
+            value, slope = gelu_parts(expanded)
+            act[s, r] = value.astype(BF)
+            gexp[s, r] = (grad_active * slope).astype(BF)
+
+    block(0)
+    mlp_gather.forward()
+    for s in (1, 3, 2):
+        cot_gather.arrived(s)
+        mlp_gather.arrived(s)
+        block(s)
+
+    def grad_mlp(s, into):
+        into[...] = jnp.zeros((ROWS, D), F32)
+
+        @pl.loop(0, 4)
+        def _(r):
+            into[...] += nt(gexp[s, r], we[r])
+
+    sc2 = scatter(1, grad_mlp)
+    turned[...] = mlp_rows[...].reshape(512, D).T
+    cot_all = cot_rows[...].reshape(512, D)
+    sends = {}
+    for n, r in enumerate((1, 3, 0, 2)):
+        buffer = stage.at[n % 2]
+        if n > 1:
+            sends[n - 2].wait_send()
+        grad_e = nn(turned[...], gexp[:, r].reshape(512, FF_SHARD)).astype(BF)
+        for d in range(8):
+            for c in range(2):
+                buffer[d, c * 256 : (c + 1) * 256] = grad_e[d * 256 : (d + 1) * 256, c * 256 : (c + 1) * 256]
+        grad_r = tn(act[:, r].reshape(512, FF_SHARD), cot_all).astype(BF)
+        for d in range(8):
+            buffer[d, 512:] = grad_r[:, d * 256 : (d + 1) * 256]
+        if n < 2:
+            c = rcopy(buffer, sib_out.at[n], d_send.at[n], d_recv.at[n], (SIB,))
+        else:
+            c = pltpu.make_async_copy(buffer, keep_out.at[n - 2], d_send.at[n])
+        c.start()
+        sends[n] = c
+    for s in range(4):
+        reduced = nn(act[s, 0], wr[0])
+        for r in range(1, 4):
+            reduced += nn(act[s, r], wr[r])
+        reduced_out[s] = reduced.astype(BF)
+    got = parts[0] + sc2.total()
+    middle = middle_out[...]
+    inverse = lax.rsqrt(jnp.mean(middle * middle, axis=-1, keepdims=True) + NORM_EPS)
+    normal = middle * inverse
+    grad_gain[...] = jnp.sum(got * normal, axis=0, keepdims=True)
+    scaled = got * gain[...]
+    grad = cot[...].astype(F32) + inverse * (scaled - normal * jnp.mean(scaled * normal, axis=-1, keepdims=True))
+    grad_middle[...] = grad
+    grad_low[...] = grad.astype(BF)
+    sc.finish()
+    sc2.finish()
+    cot_gather.finish()
+    mlp_gather.finish()
+    for c in sib + across:
+        c.wait_send()
+    for (s, r), c in back.items():
+        if r:
+            c.wait_send()
+    for n in range(2):
+        sends[n].wait_recv()
+    for n in (2, 3):
+        sends[n].wait()
+
+
+def mlp(q, k, v, first_column, wo_all, resid, gain_mlp, cot, w_expand, we_two, w_reduce):
+    dma = pltpu.SemaphoreType.DMA
+    vm, hbm = pl.BlockSpec(memory_space=VMEM), pl.BlockSpec(memory_space=ANY)
     return pl.pallas_call(
-        attend_back_kernel,
-        in_specs=[full] * 5,
-        out_specs=[full] * 3,
-        out_shape=[jax.ShapeDtypeStruct(q.shape, BF)] * 3,
-        scratch_shapes=[VMEM(q.shape, F32)] * 2,
-        compiler_params=pltpu.CompilerParams(vmem_limit_bytes=48 * MIB),
-        cost_estimate=pl.CostEstimate(flops=10 * 2048 * 1024 * 128, bytes_accessed=8 * MIB, transcendentals=2048 * 1024),
-        name="attend_back",
-    )(q, k, v, grad_context, first_row)
-
-
-def moved(x, mask):
-    return x if mask == 0 else lax.ppermute(x, "tensor", [(i, i ^ mask) for i in range(16)])
-
-
-def y_gather_plain(x):
-    return jnp.stack([moved(x, 2 * s) for s in range(4)])
-
-
-def y_sum_plain(parts):
-    return sum(moved(parts[s].astype(BF), 2 * s).astype(F32) if s else parts[0] for s in range(4))
-
-
-def to_rows_plain(heads):
+        mlp_kernel,
+        in_specs=[vm] * 8 + [hbm] * 3,
+        out_specs=[vm, vm, vm, hbm, hbm, vm, vm, vm],
+        out_shape=[
+            jax.ShapeDtypeStruct((4, 4, ROWS, HEAD_DIM), BF),
+            jax.ShapeDtypeStruct((ROWS, D), F32),
+            jax.ShapeDtypeStruct((4, ROWS, D), BF),
+            jax.ShapeDtypeStruct((2, 8, 1024, 256), BF),
+            jax.ShapeDtypeStruct((2, 8, 1024, 256), BF),
+            jax.ShapeDtypeStruct((1, D), F32),
+            jax.ShapeDtypeStruct((ROWS, D), F32),
+            jax.ShapeDtypeStruct((ROWS, D), BF),
+        ],
+        scratch_shapes=[
+            VMEM((2048, HEAD_DIM), BF),
+            VMEM((4, D, FF_SHARD), BF),
+            VMEM((4, FF_SHARD, D), BF),
+            VMEM((4, ROWS, D), BF),
+            VMEM((4, ROWS, D), BF),
+            VMEM((4, 4, ROWS, FF_SHARD), BF),
+            VMEM((4, 4, ROWS, FF_SHARD), BF),
+            VMEM((D, 512), BF),
+            VMEM((3, ROWS, D), F32),
+            VMEM((2, 8, 1024, 256), BF),
+            VMEM((2, 3, ROWS, D), BF),
+            VMEM((2, ROWS, D), BF),
+            VMEM((2, 2, ROWS, D), BF),
+            dma((2, 6)), dma((2, 6)), dma((2, 6)), dma((2, 6)), dma((5,)), dma((5,)), dma((4, 4)), dma((4, 4)),
+            dma((4,)), dma((4,)), dma((3,)),
+        ],
+        compiler_params=pltpu.CompilerParams(collective_id=2, has_side_effects=True, vmem_limit_bytes=60 * MIB),
+        cost_estimate=pl.CostEstimate(flops=30 * 10**9, bytes_accessed=50 * MIB, transcendentals=0),
+        name="mlp",
+    )(q, k, v, first_column, wo_all, resid, gain_mlp[None], cot, w_expand, we_two, w_reduce)
+
+
+class Ring:
+    def __init__(self, part, out, passed, got, send, recv, near, far, size):
+        half = size // 2
+        lo, hi = pl.ds(0, half), pl.ds(half, half)
+
+        def c(i, src, dst, target):
+            return rcopy(src, dst, send.at[i], recv.at[i], target)
+
+        self.part, self.out, self.passed, self.got, self.lo, self.hi = part, out, passed, got, lo, hi
+        self.copies = [
+            c(0, out.at[0, lo], passed.at[lo], near),
+            c(1, out.at[0, hi], passed.at[hi], far),
+            c(2, out.at[1, lo], got.at[0, lo], near),
+            c(3, out.at[2, hi], got.at[1, hi], far),
+            c(4, out.at[2, lo], got.at[1, lo], far),
+            c(5, out.at[1, hi], got.at[0, hi], near),
+        ]
+
+    def begin(self):
+        for i, (slot, s, half) in enumerate(((0, 2, self.lo), (0, 2, self.hi), (1, 1, self.lo), (2, 3, self.hi))):
+            self.out[slot, half] = self.part(s, half).astype(BF)
+            self.copies[i].start()
+
+    def send(self, slot, s, half, value, i):
+        self.out[slot, half] = value.astype(BF)
+        self.copies[i].start()
+
+    def relay(self):
+        for i, slot, s, half in ((0, 2, 3, self.lo), (1, 1, 1, self.hi)):
+            self.copies[i].wait_recv()
+            self.out[slot, half] = (self.part(s, half) + self.passed[half].astype(F32)).astype(BF)
+            self.copies[4 + i].start()
+
+    def arrive(self):
+        for i in (2, 3, 4, 5):
+            self.copies[i].wait_recv()
+
+    def total(self, index):
+        return self.part(0, index) + self.got[0, index].astype(F32) + self.got[1, index].astype(F32)
+
+    def finish(self):
+        for c in self.copies:
+            c.wait_send()
+
+
+X_RING = ((XN,), (XN, 4))
+Z_RING = ((0, 1), (0, 3))
+
+
+class GridSum:
+    @staticmethod
+    def scratch(rows):
+        half, dma = rows // 2, pltpu.SemaphoreType.DMA
+        return [
+            VMEM((2, 8, rows, 256), BF),
+            VMEM((2, 8, rows, 256), BF),
+            VMEM((2, 3, 4, half, 256), BF),
+            VMEM((2, 4, half, 256), BF),
+            VMEM((2, 2, 4, half, 256), BF),
+            VMEM((2, 4, half, 256), F32),
+            VMEM((2, 3, half, 256), BF),
+            VMEM((2, half, 256), BF),
+            VMEM((2, 2, half, 256), BF),
+            dma((4, 6)),
+            dma((4, 6)),
+            dma((4,)),
+        ]
+
+    def __init__(self, pieces, scratch):
+        (self.a, self.b, out1, pass1, got1, self.mid, out2, pass2, got2, send, recv, load) = scratch
+        rows = self.a.shape[2]
+        self.half = half = rows // 2
+        self.loads, start = [], 0
+        for i, (kept, given) in enumerate(pieces):
+            at = pl.ds(start, kept.shape[2])
+            start += kept.shape[2]
+            self.loads += [
+                pltpu.make_async_copy(kept, self.a.at[:, :, at], load.at[2 * i]),
+                pltpu.make_async_copy(given, self.b.at[:, :, at], load.at[2 * i + 1]),
+            ]
+        dp = lax.axis_index("dp")
+        place = {(sx, sz): flip(dp, (4 if sx in (2, 3) else 0) + sz) for sx in range(4) for sz in range(4)}
+
+        def block(sx, sz, path):
+            shard = 0 if sx in (0, 2) else 1
+            at = slice(path * half, (path + 1) * half)
+            d = place[sx, sz]
+            return self.a[shard, d, at].astype(F32) + self.b[shard, d, at].astype(F32)
+
+        def span(ds):
+            return range(ds.start, ds.start + ds.size)
+
+        def over_x(s, half_):
+            return jnp.stack([block(s, z, 0) for z in span(half_)])
+
+        def over_z(s, half_):
+            return jnp.stack([block(x, s, 1) for x in span(half_)])
+
+        rings = (X_RING, Z_RING)
+        self.first, self.second = [], []
+        for path, part in enumerate((over_x, over_z)):
+            near, far = rings[path]
+            self.first.append(
+                Ring(part, out1.at[path], pass1.at[path], got1.at[path], send.at[path], recv.at[path], near, far, 4)
+            )
+            near, far = rings[1 - path]
+            mid = self.mid.at[path]
+
+            def later(s, half_, mid=mid):
+                return mid[s, half_]
+
+            self.second.append(
+                Ring(
+                    later, out2.at[path], pass2.at[path], got2.at[path], send.at[2 + path], recv.at[2 + path], near, far, half
+                )
+            )
+
+    def load(self):
+        for c in self.loads:
+            c.start()
+
+    def begin(self):
+        for c in self.loads:
+            c.wait()
+        for ring in self.first:
+            ring.begin()
+
+    def relay(self):
+        for ring in self.first:
+            ring.relay()
+
+    def turn(self):
+        for path in range(2):
+            ring = self.first[path]
+            ring.arrive()
+            for s in (2, 1, 3, 0):
+                self.mid[path, s] = ring.total(pl.ds(s, 1))[0]
+            self.second[path].begin()
+
+    def relay2(self):
+        for ring in self.second:
+            ring.relay()
+
+    def result(self):
+        parts = []
+        for ring in self.second:
+            ring.arrive()
+            parts.append(ring.total(pl.ds(0, self.half)))
+        return jnp.concatenate(parts, axis=0)
+
+    def finish(self):
+        for ring in self.first + self.second:
+            ring.finish()
+
+
+def back_kernel(
+    q, k, v, first_place, grad_low, wo_all, ctx_rows, reduced, middle, keep_in, sib_in,
+    output, grads, summed, keep_out, sib_out,
+    rows, proj, gc, dk_sum, dv_sum, stage, sc_out, sc_pass, sc_got,
+    g_send, g_recv, s_send, s_recv, c_send, c_recv, d_send, d_recv, *grid_scratch,
+):
+    enter([(Y1,), (Y3,), (SIB,), (DIAG,), *X_RING, *Z_RING])
     t = lax.axis_index("tensor")
-    out = []
-    for r in range(4):
-        piece = jnp.stack([heads[(t ^ A_MASKS[r]) ^ (2 * s)] for s in range(4)])
-        out.append(moved(piece, A_MASKS[r]))
-    return jnp.stack(out, 1)
-
-
-def to_heads_plain(rows):
+    gather = Gather(grad_low, rows, g_send, g_recv)
+    gather.start()
+    part = pl.ds(0, 512)
+    grid = GridSum([(keep_in.at[:, :, part], sib_in.at[:, :, part])], grid_scratch)
+    grid.load()
+    ring = Ring(
+        lambda s, half: reduced[s, half].astype(F32), sc_out, sc_pass, sc_got, s_send, s_recv, (Y1,), (Y3,), ROWS
+    )
+    rows[0] = grad_low[...]
+    weight = wo_all[...].reshape(4 * HEAD_DIM, D)
+    moves = []
+
+    def project(s):
+        y = nt(rows[s], weight).astype(BF)
+        place = pl.multiple_of(flip(t, 2 * s) * ROWS, ROWS)
+        for r in range(4):
+            proj[s, r] = y[:, r * HEAD_DIM : (r + 1) * HEAD_DIM]
+            src, dst = proj.at[s, r], gc.at[pl.ds(place, ROWS)]
+            if r:
+                c = rcopy(src, dst, c_send.at[s, r], c_recv.at[s, r], (A_MASKS[r],))
+            else:
+                c = pltpu.make_async_copy(src, dst, c_send.at[s, r])
+            c.start()
+            moves.append((r, c))
+
+    project(0)
+    gather.forward()
+    ring.begin()
+    grid.begin()
+    for s in (1, 3, 2):
+        gather.arrived(s)
+        project(s)
+    ring.relay()
+    grid.relay()
+    all_rows = rows[...].reshape(4 * ROWS, D)
+    sends = []
+    for n, r in enumerate((1, 3, 0, 2)):
+        lhs = jnp.concatenate([ctx_rows[s, r] for s in range(4)], axis=0)
+        grad_o = tn(lhs, all_rows).astype(BF)
+        for d in range(8):
+            stage[n, d] = grad_o[:, d * 256 : (d + 1) * 256]
+        if n < 2:
+            c = rcopy(stage.at[n], sib_out.at[n], d_send.at[n], d_recv.at[n], (SIB,))
+        else:
+            c = pltpu.make_async_copy(stage.at[n], keep_out.at[n - 2], d_send.at[n])
+        c.start()
+        sends.append(c)
+    for r, c in moves:
+        c.wait_recv() if r else c.wait()
+    hooks = {4: grid.turn, 7: grid.relay2}
+    attend_back_kernel(q, k, v, gc, first_place, grads.at[0], grads.at[1], grads.at[2], dk_sum, dv_sum, hooks)
+    summed[...] = grid.result()
+    grid.finish()
+    ring.arrive()
+    output[...] = (middle[...] + ring.total(pl.ds(0, ROWS))).astype(BF)
+    gather.finish()
+    ring.finish()
+    for r, c in moves:
+        if r:
+            c.wait_send()
+    for n, c in enumerate(sends):
+        c.wait()
+
+
+def back(q, k, v, first_row, grad_low, wo_all, ctx_rows, reduced, middle, keep, sib):
+    dma = pltpu.SemaphoreType.DMA
+    vm, hbm = pl.BlockSpec(memory_space=VMEM), pl.BlockSpec(memory_space=ANY)
+    return pl.pallas_call(
+        back_kernel,
+        in_specs=[vm] * 9 + [hbm] * 2,
+        out_specs=[vm, vm, vm, hbm, hbm],
+        out_shape=[
+            jax.ShapeDtypeStruct((ROWS, D), BF),
+            jax.ShapeDtypeStruct((3, 2048, HEAD_DIM), BF),
+            jax.ShapeDtypeStruct((512, 256), F32),
+            jax.ShapeDtypeStruct((2, 8, ROWS, 256), BF),
+            jax.ShapeDtypeStruct((2, 8, ROWS, 256), BF),
+        ],
+        scratch_shapes=[
+            VMEM((4, ROWS, D), BF),
+            VMEM((4, 4, ROWS, HEAD_DIM), BF),
+            VMEM((2048, HEAD_DIM), BF),
+            VMEM((2048, HEAD_DIM), F32),
+            VMEM((2048, HEAD_DIM), F32),
+            VMEM((4, 8, ROWS, 256), BF),
+            VMEM((3, ROWS, D), BF),
+            VMEM((ROWS, D), BF),
+            VMEM((2, ROWS, D), BF),
+            dma((6,)), dma((6,)), dma((6,)), dma((6,)), dma((4, 4)), dma((4, 4)), dma((4,)), dma((4,)),
+            *GridSum.scratch(512),
+        ],
+        compiler_params=pltpu.CompilerParams(collective_id=3, has_side_effects=True, vmem_limit_bytes=60 * MIB),
+        cost_estimate=pl.CostEstimate(flops=8 * 10**9, bytes_accessed=20 * MIB, transcendentals=0),
+        name="back",
+    )(q, k, v, first_row, grad_low, wo_all, ctx_rows, reduced, middle, keep, sib)
+
+
+def streams_kernel(
+    grads, rows_in, w_in, keep_in, sib_in,
+    out, summed, keep_out, sib_out,
+    rows, weights, g, turned, parts, stage, sc_out, sc_pass, sc_got,
+    s_send, s_recv, c_send, c_recv, d_send, d_recv, local, *grid_scratch,
+):
+    enter([(Y1,), (Y3,), (SIB,), (DIAG,), *X_RING, *Z_RING])
     t = lax.axis_index("tensor")
-    out = jnp.zeros((16, 128, 128), rows.dtype)
-    for r in range(4):
-        got = moved(rows[:, r], A_MASKS[r])
-        for s in range(4):
-            out = out.at[(t ^ A_MASKS[r]) ^ (2 * s)].set(got[s])
-    return out
-
-
-def mlp_plain(ctx, wo_all, resid, gain_mlp, cot, w_expand, we_two, w_reduce):
-    ctx_rows = to_rows_plain(ctx)
-    we = jnp.stack([w_expand, we_two[0], we_two[1], moved(we_two[1], SIB)])
-    wr = jnp.stack([moved(w_reduce, m) for m in A_MASKS])
-    cot_rows = y_gather_plain(cot)
-    attended = y_sum_plain(jnp.einsum("srtd,rdo->sto", ctx_rows, wo_all, preferred_element_type=F32))
-    middle = resid + attended
-    inverse = lax.rsqrt(jnp.mean(middle * middle, -1, keepdims=True) + NORM_EPS)
-    normal = middle * inverse
-    mlp_rows = y_gather_plain((normal * gain_mlp).astype(BF))
-    expanded = jnp.einsum("std,rdf->srtf", mlp_rows, we, preferred_element_type=F32)
-    act, slope = gelu_parts(expanded)
-    act = act.astype(BF)
-    reduced = jnp.einsum("srtf,rfd->std", act, wr, preferred_element_type=F32)
-    grad_active = jnp.einsum("std,rfd->srtf", cot_rows, wr, preferred_element_type=F32)
-    gexp = (grad_active * slope).astype(BF)
-    grad_wr = jnp.einsum("srtf,std->rfd", act, cot_rows, preferred_element_type=F32).astype(BF)
-    grad_we = jnp.einsum("std,srtf->rdf", mlp_rows, gexp, preferred_element_type=F32).astype(BF)
-    gmlp = y_sum_plain(jnp.einsum("srtf,rdf->std", gexp, we, preferred_element_type=F32))
-    grad_gain = jnp.sum(gmlp * normal, 0, keepdims=True)
-    scaled = gmlp * gain_mlp
-    grad_middle = cot.astype(F32) + inverse * (scaled - normal * jnp.mean(scaled * normal, -1, keepdims=True))
-    return ctx_rows, middle, reduced, grad_we, grad_wr, grad_gain, grad_middle
-
-
-def out_back_plain(grad_middle, middle, reduced, ctx_rows, wo_all):
-    gmid_rows = y_gather_plain(grad_middle.astype(BF))
-    output = (middle + y_sum_plain(reduced)).astype(BF)
-    gctx = jnp.einsum("std,rhd->srth", gmid_rows, wo_all, preferred_element_type=F32).astype(BF)
-    grad_wo = jnp.einsum("srth,std->rhd", ctx_rows, gmid_rows, preferred_element_type=F32).astype(BF)
-    return output, to_heads_plain(gctx), grad_wo
-
-
-def streams_back_plain(grads, rows, w_all):
-    dw, gs = [], []
+    part = pl.ds(512, 512)
+    grid = GridSum([(keep_in.at[:, :, part], sib_in.at[:, :, part])], grid_scratch)
+    moves = {}
     for a in range(3):
-        g = to_rows_plain(grads[a])
-        dw.append(jnp.einsum("std,srth->rdh", rows[a], g, preferred_element_type=F32).astype(BF))
-        gs.append(y_sum_plain(jnp.einsum("srth,rdh->std", g, w_all[a], preferred_element_type=F32)))
-    return jnp.stack(gs), jnp.stack(dw)
-
-
-def weight_sum_plain(dw, split):
-    own = y = sum(moved(dw[r], A_MASKS[r]).astype(F32) for r in range(4))
-    return lax.psum_scatter(own, "dp", scatter_dimension=split, tiled=True)
-
-
-def front_back_plain(history, gs, grad_middle, n, inv, mix, pre, mix_gain, mix_first, mix_second, gains):
-    grads_gain, ds = [], []
+        for s in (2, 1, 3, 0):
+            for r in range(4):
+                place = pl.multiple_of(flip(t, A_MASKS[r] + 2 * s) * ROWS, ROWS)
+                src, dst = grads.at[a, pl.ds(place, ROWS)], g.at[a, s, r]
+                if r:
+                    c = rcopy(src, dst, c_send.at[a, s, r], c_recv.at[a, s, r], (A_MASKS[r],))
+                else:
+                    c = pltpu.make_async_copy(src, dst, c_send.at[a, s, r])
+                c.start()
+                moves[a, s, r] = c
+    loads = []
+    for a in range(3):
+        c = pltpu.make_async_copy(w_in.at[a], weights.at[a], local.at[a])
+        c.start()
+        loads.append(c)
+    for a in range(3):
+        loads.append(pltpu.make_async_copy(rows_in.at[a], rows, local.at[3 + a]))
+    loads[3].start()
+    grid.load()
+    rings = []
+    for a in range(3):
+        loads[a].wait()
+        weight = jnp.concatenate([weights[a, r] for r in range(4)], axis=1)
+        ring = Ring(
+            lambda s, half, a=a: parts[a, pl.ds({0: 0, 1: 64, 3: 192}[s] + half.start, half.size)],
+            sc_out.at[a], sc_pass.at[a], sc_got.at[a], s_send.at[a], s_recv.at[a], (Y1,), (Y3,), ROWS,
+        )
+        rings.append(ring)
+        for s in (2, 1, 3, 0):
+            for r in range(4):
+                c = moves[a, s, r]
+                c.wait_recv() if r else c.wait()
+            lhs = jnp.concatenate([g[a, s, r] for r in range(4)], axis=1)
+            value = nt(lhs, weight)
+            if s == 0:
+                parts[a, 0:128] = value
+            elif s == 1:
+                ring.send(1, s, ring.lo, value[:64], 2)
+                parts[a, 128:192] = value[64:]
+            elif s == 3:
+                ring.send(2, s, ring.hi, value[64:], 3)
+                parts[a, 192:256] = value[:64]
+            else:
+                ring.send(0, s, ring.lo, value[:64], 0)
+                ring.send(0, s, ring.hi, value[64:], 1)
+        if a == 0:
+            grid.begin()
+    for ring in rings:
+        ring.relay()
+    grid.relay()
+    for a in range(3):
+        loads[3 + a].wait()
+        turned[...] = rows[...].reshape(512, D).T
+        if a < 2:
+            loads[4 + a].start()
+        grad_w = nn(
+            turned[...], jnp.concatenate([g[a, :, r].reshape(512, HEAD_DIM) for r in range(4)], axis=1)
+        ).astype(BF)
+        for n, r in enumerate((1, 3, 0, 2)):
+            for d in range(8):
+                block = grad_w[d * 256 : (d + 1) * 256, r * HEAD_DIM : (r + 1) * HEAD_DIM]
+                if a < 2:
+                    stage[n, d, 0:256, a * 128 : (a + 1) * 128] = block
+                else:
+                    stage[n, d, 256:384, 0:128] = block[:128]
+                    stage[n, d, 256:384, 128:256] = block[128:]
+        if a == 1:
+            grid.turn()
+    sends = []
+    for n in range(4):
+        if n < 2:
+            c = rcopy(stage.at[n], sib_out.at[n], d_send.at[n], d_recv.at[n], (SIB,))
+        else:
+            c = pltpu.make_async_copy(stage.at[n], keep_out.at[n - 2], d_send.at[n])
+        c.start()
+        sends.append(c)
+    grid.relay2()
+    summed[...] = grid.result()
+    grid.finish()
+    for a, ring in enumerate(rings):
+        ring.arrive()
+        out[a] = ring.total(pl.ds(0, ROWS))
+    for ring in rings:
+        ring.finish()
+    for (a, s, r), c in moves.items():
+        if r:
+            c.wait_send()
+    for c in sends:
+        c.wait()
+
+
+def streams_back(grads, rows, w_all, keep, sib):
+    dma = pltpu.SemaphoreType.DMA
+    vm, hbm = pl.BlockSpec(memory_space=VMEM), pl.BlockSpec(memory_space=ANY)
+    return pl.pallas_call(
+        streams_kernel,
+        in_specs=[vm, hbm, hbm, hbm, hbm],
+        out_specs=[vm, vm, hbm, hbm],
+        out_shape=[
+            jax.ShapeDtypeStruct((3, ROWS, D), F32),
+            jax.ShapeDtypeStruct((512, 256), F32),
+            jax.ShapeDtypeStruct((2, 8, 384, 256), BF),
+            jax.ShapeDtypeStruct((2, 8, 384, 256), BF),
+        ],
+        scratch_shapes=[
+            VMEM((4, ROWS, D), BF),
+            VMEM((3, 4, D, HEAD_DIM), BF),
+            VMEM((3, 4, 4, ROWS, HEAD_DIM), BF),
+            VMEM((D, 512), BF),
+            VMEM((3, 256, D), F32),
+            VMEM((4, 8, 384, 256), BF),
+            VMEM((3, 3, ROWS, D), BF),
+            VMEM((3, ROWS, D), BF),
+            VMEM((3, 2, ROWS, D), BF),
+            dma((3, 6)), dma((3, 6)), dma((3, 4, 4)), dma((3, 4, 4)), dma((4,)), dma((4,)), dma((6,)),
+            *GridSum.scratch(512),
+        ],
+        compiler_params=pltpu.CompilerParams(collective_id=4, has_side_effects=True, vmem_limit_bytes=60 * MIB),
+        cost_estimate=pl.CostEstimate(flops=8 * 10**9, bytes_accessed=20 * MIB, transcendentals=0),
+        name="streams_back",
+    )(grads, rows, w_all, keep, sib)
+
+
+SMALL_ROWS, SMALL_COLS = 80, D + 128
+RING_OF = {
+    "y": ((Y1, 0), (Y2, 0), (Y3, 0)),
+    "x": ((XN, 0), (0, 4), (XN, 4)),
+    "z": ((0, 1), (0, 2), (0, 3)),
+}
+
+
+def finish_kernel(
+    hist_in, gs, grad_middle, n, inv, mix, pre, mix_gain, mix_first, mix_second, gains, gain_mlp,
+    keep_q, sib_q, keep_o, sib_o,
+    grad_hist, summed, small_out,
+    hist, ds, sums, gmix, extra, pack, acc, acc1, acc2, acc3, core_out, core_got, y_out, y_got, x_out, x_got, z_out, z_got,
+    res, hist_sem, out_sem, r_send, r_recv, a_send, a_recv, *grid_scratch,
+):
+    load = pltpu.make_async_copy(hist_in, hist, hist_sem)
+    load.start()
+    enter([(SIB,), *RING_OF["y"], *RING_OF["x"], *RING_OF["z"]])
+    grid = GridSum([(keep_q, sib_q), (keep_o, sib_o)], grid_scratch)
+    grid.load()
+    t, dp = lax.axis_index("tensor"), lax.axis_index("dp")
+    core, y, z = lax.rem(t, 2), lax.rem(lax.div(t, 2), 4), lax.rem(dp, 4)
+    x = 2 * lax.div(dp, 4) + lax.div(t, 8)
+    sums[...] = jnp.zeros(sums.shape, F32)
+    step = 16
+    lane = lax.broadcasted_iota(jnp.int32, (step, 128), 1)
+    grid.begin()
+    load.wait()
+
+    def gradients(tile):
+        at = pl.ds(pl.multiple_of(tile * step, step), step)
+        for k in range(3):
+            g, normal = gs[k, at], n[k, at].astype(F32)
+            gn = g * normal
+            sums[k] += gn[:8] + gn[8:]
+            scaled = g * gains[k : k + 1]
+            mean = jnp.sum(scaled * normal, axis=-1, keepdims=True) * (1.0 / D)
+            ds[k, at] = (scaled - normal * mean) * inv[k, at, 0:1]
+
+        def entry(j, found):
+            h = hist[j, at].astype(F32)
+            for k in range(STREAMS):
+                product = (ds[k, at] if k < 3 else grad_middle[at]) * h
+                total = product[:, :128]
+                for i in range(1, D // 128):
+                    total = total + product[:, i * 128 : (i + 1) * 128]
+                found = jnp.where(lane == k * HISTORY + j, jnp.sum(total, axis=-1, keepdims=True), found)
+            return found
+
+        gmix[at] = lax.fori_loop(0, HISTORY, entry, jnp.zeros((step, 128), F32))
+
+    @pl.loop(0, 4)
+    def _(tile):
+        gradients(tile)
+
+    grid.relay()
+
+    @pl.loop(4, ROWS // step)
+    def _(tile):
+        gradients(tile)
+
+    def exact(a, b, dims):
+        return lax.dot_general(a, b, (dims, ((), ())), precision=PRECISE, preferred_element_type=F32)
+
+    grad_mixing = gmix[:, :MIX]
+    hidden, slope = gelu_parts(pre[...])
+    last = hist[HISTORY - 1].astype(F32)
+    inverse = lax.rsqrt(jnp.mean(last * last, axis=-1, keepdims=True) + NORM_EPS)
+    normal = last * inverse
+    grad_pre = exact(grad_mixing, mix_second[...], ((1,), (1,))) * slope
+    pack[...] = jnp.zeros(pack.shape, F32)
+    pack[0:MIX, 0:D] = exact(grad_pre, normal * mix_gain[...], ((0,), (0,)))
+    pack[0:MIX, D : D + MIX] = exact(hidden, grad_mixing, ((0,), (0,)))
+    grad_latest = exact(grad_pre, mix_first[...], ((1,), (1,)))
+    pack[68:69, 0:D] = jnp.sum(grad_latest * normal, axis=0, keepdims=True)
     for k in range(3):
-        normal = n[k].astype(F32)
-        grads_gain.append(jnp.sum(gs[k] * normal, 0))
-        scaled = gs[k] * gains[k]
-        ds.append(inv[k][:, :1] * (scaled - normal * jnp.mean(scaled * normal, -1, keepdims=True)))
-    ds = jnp.stack(ds + [grad_middle])
-    h = history.astype(F32)
-    gmix = jnp.einsum("ktd,jtd->tkj", ds, h, precision=PRECISE).reshape(ROWS, MIX)
-    hidden, slope = gelu_parts(pre)
-    last = h[HISTORY - 1]
-    inverse = lax.rsqrt(jnp.mean(last * last, -1, keepdims=True) + NORM_EPS)
-    normal = last * inverse
-    latest = normal * mix_gain
-    g_bias = gmix.sum(0)
-    g_second = jnp.dot(hidden.T, gmix, precision=PRECISE)
-    dpre = jnp.dot(gmix, mix_second.T, precision=PRECISE) * slope
-    g_first = jnp.dot(latest.T, dpre, precision=PRECISE)
-    dl = jnp.dot(dpre, mix_first.T, precision=PRECISE)
-    g_gain = jnp.sum(dl * normal, 0)
-    scaled = dl * mix_gain
-    extra = inverse * (scaled - normal * jnp.mean(scaled * normal, -1, keepdims=True))
-    gh = jnp.einsum("tkj,ktd->jtd", mix.reshape(ROWS, STREAMS, HISTORY), ds, precision=PRECISE)
-    gh = gh.at[HISTORY - 1].add(extra).astype(BF)
-    return gh, g_gain, g_first, g_second, g_bias, grads_gain[0], grads_gain[1], grads_gain[2]
+        pack[69 + k : 70 + k, 0:D] = jnp.sum(sums[k], axis=0, keepdims=True)
+    pack[72:73, 0:D] = gain_mlp[...]
+    pack[68:69, D : D + MIX] = jnp.sum(grad_mixing, axis=0, keepdims=True)
+    scaled = grad_latest * mix_gain[...]
+    extra[...] = inverse * (scaled - normal * jnp.mean(scaled * normal, axis=-1, keepdims=True))
+    acc[...] = jnp.zeros(acc.shape, F32)
+    columns = SMALL_COLS // 128
+    for i in range(SMALL_ROWS // 16):
+        for j in range(columns):
+            b = i * columns + j
+            acc[b // 64, b // 16 % 4, b // 4 % 4, b % 4] = pack[i * 16 : (i + 1) * 16, j * 128 : (j + 1) * 128]
+
+    saves = []
+
+    def history_tile(tile):
+        at = pl.ds(tile * step, step)
+        here = mix[at]
+        spread = [jnp.broadcast_to(here[:, i : i + 1], (step, 128)) for i in range(MIX)]
+
+        @pl.loop(0, D // 128)
+        def _(c):
+            cols = pl.ds(pl.multiple_of(c * 128, 128), 128)
+            grad = [ds[k, at, cols] if k < 3 else grad_middle[at, cols] for k in range(STREAMS)]
+            for j in range(HISTORY):
+                value = spread[j] * grad[0]
+                for k in range(1, STREAMS):
+                    value = value + spread[k * HISTORY + j] * grad[k]
+                if j == HISTORY - 1:
+                    value = value + extra[at, cols]
+                hist[j, at, cols] = value.astype(BF)
+
+        c = pltpu.make_async_copy(hist.at[:, at], grad_hist.at[:, at], out_sem.at[tile])
+        c.start()
+        saves.append(c)
+
+    core_out[...] = acc[1 - core].astype(BF)
+    over_core = rcopy(core_out, core_got, r_send.at[0, 0], r_recv.at[0, 0], (SIB,))
+    over_core.start()
+    history_tile(0)
+    over_core.wait()
+    acc1[...] = acc[core] + core_got[...].astype(F32)
+
+    def reduce_over(level, source, out, got, me, axis, between):
+        copies = []
+        for i, target in enumerate(RING_OF[axis]):
+            out[i] = source[flip(me, i + 1)].astype(BF)
+            c = rcopy(out.at[i], got.at[i], r_send.at[level, i], r_recv.at[level, i], target)
+            c.start()
+            copies.append(c)
+        between()
+        for c in copies:
+            c.wait()
+        return source[me] + got[0].astype(F32) + got[1].astype(F32) + got[2].astype(F32)
+
+    acc2[...] = reduce_over(1, acc1, y_out, y_got, y, "y", lambda: history_tile(1))
+    grid.turn()
+    acc3[...] = reduce_over(2, acc2, x_out, x_got, x, "x", lambda: history_tile(2))
+    total = reduce_over(3, acc3, z_out, z_got, z, "z", lambda: history_tile(3))
+    res[core, y, x, z] = total.astype(BF)
+
+    def spread_over(level, ref, axis, between):
+        copies = []
+        for i, target in enumerate(RING_OF[axis] if axis else ((SIB, 0),)):
+            c = rcopy(ref, ref, a_send.at[level, i], a_recv.at[level, i], target)
+            c.start()
+            copies.append(c)
+        between()
+        for c in copies:
+            c.wait()
+
+    spread_over(0, res.at[core, y, x, z], "z", lambda: history_tile(4))
+    grid.relay2()
+    spread_over(1, res.at[core, y, x], "x", lambda: history_tile(5))
+    spread_over(2, res.at[core, y], "y", lambda: history_tile(6))
+    spread_over(3, res.at[core], "", lambda: history_tile(7))
+    for i in range(SMALL_ROWS // 16):
+        for j in range(columns):
+            b = i * columns + j
+            small_out[i * 16 : (i + 1) * 16, j * 128 : (j + 1) * 128] = res[b // 64, b // 16 % 4, b // 4 % 4, b % 4].astype(F32)
+    summed[...] = grid.result()
+    grid.finish()
+    for c in saves:
+        c.wait()
+
+
+def finish(history, gs, grad_middle, n, inv, mix, pre, mix_gain, mix_first, mix_second, gains, gain_mlp, *packs):
+    dma = pltpu.SemaphoreType.DMA
+    vm, hbm = pl.BlockSpec(memory_space=VMEM), pl.BlockSpec(memory_space=ANY)
+    tile = (16, 128)
+    return pl.pallas_call(
+        finish_kernel,
+        in_specs=[hbm] + [vm] * 11 + [hbm] * 4,
+        out_specs=[hbm, vm, vm],
+        out_shape=[
+            jax.ShapeDtypeStruct((HISTORY, ROWS, D), BF),
+            jax.ShapeDtypeStruct((512, 256), F32),
+            jax.ShapeDtypeStruct((SMALL_ROWS, SMALL_COLS), F32),
+        ],
+        scratch_shapes=[
+            VMEM((HISTORY, ROWS, D), BF),
+            VMEM((3, ROWS, D), F32),
+            VMEM((3, 8, D), F32),
+            VMEM((ROWS, 128), F32),
+            VMEM((ROWS, D), F32),
+            VMEM((SMALL_ROWS, SMALL_COLS), F32),
+            VMEM((2, 4, 4, 4, *tile), F32),
+            VMEM((4, 4, 4, *tile), F32),
+            VMEM((4, 4, *tile), F32),
+            VMEM((4, *tile), F32),
+            VMEM((4, 4, 4, *tile), BF),
+            VMEM((4, 4, 4, *tile), BF),
+            VMEM((3, 4, 4, *tile), BF),
+            VMEM((3, 4, 4, *tile), BF),
+            VMEM((3, 4, *tile), BF),
+            VMEM((3, 4, *tile), BF),
+            VMEM((3, *tile), BF),
+            VMEM((3, *tile), BF),
+            VMEM((2, 4, 4, 4, *tile), BF),
+            dma(()), dma((8,)), dma((4, 3)), dma((4, 3)), dma((4, 3)), dma((4, 3)),
+            *GridSum.scratch(512),
+        ],
+        compiler_params=pltpu.CompilerParams(collective_id=5, has_side_effects=True, vmem_limit_bytes=60 * MIB),
+        cost_estimate=pl.CostEstimate(flops=10**9, bytes_accessed=30 * MIB, transcendentals=0),
+        name="finish",
+    )(history, gs, grad_middle, n, inv, mix, pre, mix_gain[None], mix_first, mix_second, gains, gain_mlp, *packs)
 
 
 def on_device(
@@ -565,17 +1228,21 @@
     x, n, inv, resid, mix, pre = front(history, mix_gain, mix_first, mix_second, mix_bias, gains)
     heads, rows, w_all, wo_all, we_two = qkv(x, w_query, w_key, w_value, w_output, w_expand)
     q, k, v = [heads[a].reshape(2048, HEAD_DIM) for a in range(3)]
-    ctx = attend(q, k, v, first[:, None]).reshape(16, ROWS, HEAD_DIM)
-    ctx_rows, middle, reduced, grad_we, grad_wr, g_gain_mlp, grad_middle = mlp_plain(
-        ctx, wo_all, resid, gain_mlp, cotangent, w_expand, we_two, w_reduce)
-    output, gctx, grad_wo = out_back_plain(grad_middle, middle, reduced, ctx_rows, wo_all)
-    dq, dk, dv = attend_back(q, k, v, gctx.reshape(2048, HEAD_DIM), first[None])
-    gs, dw = streams_back_plain([z.reshape(16, ROWS, HEAD_DIM) for z in (dq, dk, dv)], rows, w_all)
-    small = front_back_plain(history, gs, grad_middle, n, inv, mix, pre, mix_gain, mix_first, mix_second, gains)
-    summed = lax.psum(small[1:] + (g_gain_mlp[0],), ("dp", "tensor"))
-    return (output, small[0], *summed,
-        weight_sum_plain(dw[0], 0), weight_sum_plain(dw[1], 0), weight_sum_plain(dw[2], 0),
-        weight_sum_plain(grad_wo, 1), weight_sum_plain(grad_we, 0), weight_sum_plain(grad_wr, 1))
+    ctx_rows, middle, reduced, keep_mlp, sib_mlp, g_gain_mlp, grad_middle, grad_low = mlp(
+        q, k, v, first[:, None], wo_all, resid, gain_mlp, cotangent, w_expand, we_two, w_reduce)
+    output, grads, sum_e, keep_o, sib_o = back(
+        q, k, v, first[None], grad_low, wo_all, ctx_rows, reduced, middle, keep_mlp, sib_mlp)
+    gs, sum_r, keep_q, sib_q = streams_back(grads, rows, w_all, keep_mlp, sib_mlp)
+    grad_history, sum_a, small = finish(
+        history, gs, grad_middle, n, inv, mix, pre, mix_gain, mix_first, mix_second, gains, g_gain_mlp,
+        keep_q, sib_q, keep_o, sib_o)
+    return (
+        output, grad_history,
+        small[68, :D], small[:MIX, :D].T, small[:MIX, D : D + MIX], small[68, D : D + MIX],
+        small[69, :D], small[70, :D], small[71, :D], small[72, :D],
+        sum_a[:256, :128], sum_a[:256, 128:], jnp.concatenate([sum_a[256:384, :128], sum_a[256:384, 128:]], 0),
+        sum_a[384:], jnp.concatenate([sum_e[:256], sum_e[256:]], 1), sum_r,
+    )
 
 
 def solution(mesh):

time: 979 us -> 426 us (0.44)
  waiting for transfers between devices: 448 us -> 0 us
  Pallas kernels: 97.9 us -> 381 us
  matrix products: 115 us -> 0 us
  starting transfers between devices: 78.9 us -> 0 us
  blocking collectives: 69.6 us -> 0 us
  other arithmetic: 65.5 us -> 6.55 us
  local copies, waits for them, and re-layouts: 75.8 us -> 28.7 us
  between operations: 19.9 us -> 3.61 us
    ppermute x64 -> x0, waiting for transfers between devices: 448 us -> none  [moved(): lax.ppermute(x, 'tensor', [(i, i ^ mask) for i in range(16)])]
    pallas_call x2 -> x4, Pallas kernels: 17.2 us -> 300 us  [the longest x1 111 us: mlp(): pl.pallas_call(mlp_kernel, in_specs=[vm] * 8 + [hbm] * 3, out_specs=[vm,...]
    dot_general x21 -> x0, matrix products: 115 us -> none  [the longest x1 24.8 us: front_back_plain(): jnp.einsum('tkj,ktd->jtd', mix.reshape(ROWS, STREAMS, HISTORY), ds, preci...]
    ppermute x64 -> x0, starting transfers between devices: 78.6 us -> none  [moved(): lax.ppermute(x, 'tensor', [(i, i ^ mask) for i in range(16)])]
    psum x1 -> x0, blocking collectives: 69.6 us -> none  [on_device(): summed = lax.psum(small[1:] + (g_gain_mlp[0],), ('dp', 'tensor'))]
    add x7 -> x0, other arithmetic: 24.4 us -> none  [the longest x6 22.3 us: weight_sum_plain(): own = y = sum((moved(dw[r], A_MASKS[r]).astype(F32) for r in range(4)))]
    unnamed x201 -> x42, local copies, waits for them, and re-layouts: 39.8 us -> 18.3 us
    scatter-add x1 -> x0, local copies, waits for them, and re-layouts: 20.6 us -> none  [front_back_plain(): gh = gh.at[HISTORY - 1].add(extra).astype(BF)]
  transfers between devices with their start and end apart: 71 -> 0, of which waited for: 35 -> 0; matrix products, arithmetic and copies ran while one was open for 21% -> 0% of each run, Pallas kernels for 0% -> 0%
where the time goes in v2:
time: 426 us; the launch traced here: 420 us
  Pallas kernels  381 us (89%)
  local copies, waits for them, and re-layouts  28.7 us (7%)
  other arithmetic  6.55 us (2%)
    pallas_call x1, Pallas kernels, mlp(): pl.pallas_call(mlp_kernel, in_specs=[vm] * 8 + [hbm] * 3, out_specs=[vm,...  111 us
    pallas_call x1, Pallas kernels, streams_back(): pl.pallas_call(streams_kernel, in_specs=[vm, hbm, hbm, hbm, hbm], out_spe...  69.3 us
    pallas_call x1, Pallas kernels, qkv(): pl.pallas_call(qkv_kernel, in_specs=[pl.BlockSpec(memory_space=VMEM)] + [...  69.3 us
    pallas_call x1, Pallas kernels, finish(): pl.pallas_call(finish_kernel, in_specs=[hbm] + [vm] * 11 + [hbm] * 4, out...  65.2 us
    pallas_call x1, Pallas kernels, back(): pl.pallas_call(back_kernel, in_specs=[vm] * 9 + [hbm] * 2, out_specs=[vm,...  53.9 us
    unnamed x42, local copies, waits for them, and re-layouts  18.3 us
    pallas_call x1, Pallas kernels, front(): pl.pallas_call(front_kernel, grid=(ROWS // rows,), in_specs=[pl.BlockSpec...  11.6 us

profile of v2, /device:TPU:1, one launch (start us, length us, event | category | flops | bytes accessed | tf_op | source)
XLA Modules:
  0.0 419.7 jit_solution(14481927717431602171)
XLA Ops:
  0.6 0.0 copy-start
  0.7 0.7 copy-done
  1.3 0.1 constant_dynamic-slice_fusion
  1.4 0.5 fusion.5
  4.5 1.3 compare_select_fusion.3.first_place
  5.8 0.8 pad_maximum_fusion.2.gains
  6.6 0.0 copy-start.4
  6.6 1.9 select_select_fusion.first_place
  8.5 1.4 copy.33.mix_first
  9.9 0.0 copy-start.6
  10.0 0.8 copy-done.6
  10.7 0.0 copy-start.9
  10.7 0.7 copy-done.9
  11.4 0.0 copy-start.10
  11.4 0.7 copy-done.10
  12.1 0.0 copy-start.2
  12.1 0.0 copy-start.12
  12.1 0.0 copy-start.13
  12.1 0.0 copy-start.14
  12.1 0.0 copy-start.15
  12.1 11.6 %front.1 = (bf16[3,128,2048]{2,1,0:T(8,128)(2,1)S(1)}, bf16[3,128,2048]{2,1,0:T(8,128)(2,1)S(1)}, f32[3,128,128]{2,1,0:T(8,128)S(1)}, f32[128,2048]{1,0:T(8,128)...) custom-call(bf16[17,128,2048]{2,1,0:T(8,128)(2,1)} %hist_in.1, bf16[17,128,2048]{2,1,0:T(8,128)(2,1)} %hist_in.1, ...), custom_call_target="tpu_custom_call" | custom-call | tf_op jit(solution)/shard_map/front/pallas_call | solution.py:201
  23.7 0.0 copy-done.4
  23.7 0.0 copy-done.2
  23.7 0.0 copy-start.3
  23.8 1.1 copy-done.3
  24.9 0.0 copy-start.5
  24.9 0.7 copy-done.5
  25.6 0.0 copy-start.8
  25.6 0.6 copy-done.8
  26.2 0.0 copy-start.11
  26.2 1.0 copy-done.11
  27.2 0.0 copy-start.7
  27.2 0.0 copy-done.12
  27.2 0.0 copy-done.13
  27.2 0.0 copy-done.14
  27.2 0.0 copy-done.15
  27.3 69.3 %qkv.1 = (bf16[3,16,128,128]{3,2,1,0:T(8,128)(2,1)S(1)}, bf16[3,4,128,2048]{3,2,1,0:T(8,128)(2,1)}, bf16[3,4,2048,128]{3,2,1,0:T(8,128)(2,1)}, bf16[4,128,2048]{2,1,0:T(8,128)(2,1)}, bf16[2,2048,512]{2,1,0:T(8,128)(2,1)}) custom-call(bf16[3,128,2048]{2,1,0:T(8,128)(2,1)S(1)} %get-tuple-element.47.x, bf16[2048,128]{1,0:T(8,128)(2,1)S(1)} %copy-done.12, ...), custom_call_target="tpu_custom_call" | custom-call | flops 3221225472 | bytes 31457280 | tf_op jit(solution)/shard_map/qkv/pallas_call | solution.py:349
  96.6 0.0 copy-done.7
  96.6 1.2 fusion
  97.8 111.5 %mlp.1 = (bf16[4,4,128,128]{3,2,1,0:T(8,128)(2,1)}, f32[128,2048]{1,0:T(8,128)}, bf16[4,128,2048]{2,1,0:T(8,128)(2,1)}, bf16[2,8,1024,256]{3,2,1,0:T(8,128)(2,1)...) custom-call(bf16[2048,128]{1,0:T(8,128)(2,1)} %bitcast.29, ...), custom_call_target="tpu_custom_call" | custom-call | flops 30000001024 | bytes 52428800 | tf_op jit(solution)/shard_map/mlp/pallas_call | solution.py:581
  209.3 53.9 %back.1 = (bf16[128,2048]{1,0:T(8,128)(2,1)}, bf16[3,2048,128]{2,1,0:T(8,128)(2,1)}, f32[512,256]{1,0:T(8,128)}, bf16[2,8,128,256]{3,2,1,0:T(8,128)(2,1)}, bf16[2,8,128,256]{3,2,1,0:T(8,128)(2,1)}) custom-call(bf16[2048,128]{1,0:T(8,128)(2,1)} %bitcast.30, bf16[2048,128]{1,0:T(8,128)(2,1)} %bitcast.28, bf16[2048,128]{1,0:T(8,128)(2,1)} %bitcast.26, ...), custom_call_target="tpu_custom_call" | custom-call | flops 8000000000 | bytes 20971520 | tf_op jit(solution)/shard_map/back/pallas_call | solution.py:848
  263.1 69.3 %streams_back.1 = (f32[3,128,2048]{2,1,0:T(8,128)}, f32[512,256]{1,0:T(8,128)}, bf16[2,8,384,256]{3,2,1,0:T(8,128)(2,1)}, bf16[2,8,384,256]{3,2,1,0:T(8,128)(2,1)}) custom-call(bf16[3,2048,128]{2,1,0:T(8,128)(2,1)} %get-tuple-element.59.grads, bf16[3,4,128,2048]{3,2,1,0:T(8,128)(2,1)} %get-tuple-element.60.rows_in, ...), custom_call_target="tpu_custom_call" | custom-call | flops 8000000000 | bytes 20971520 | tf_op jit(solution)/shard_map/streams_back/pallas_call | solution.py:984
  332.4 0.0 copy-start.17
  332.5 65.2 %finish.1 = (bf16[17,128,2048]{2,1,0:T(8,128)(2,1)}, f32[512,256]{1,0:T(8,128)}, f32[80,2176]{1,0:T(8,128)}) custom-call(bf16[17,128,2048]{2,1,0:T(8,128)(2,1)} %hist_in.1, f32[3,128,2048]{2,1,0:T(8,128)} %get-tuple-element.62.gs, f32[128,2048]{1,0:T(8,128)} %get-tuple-element.63.grad_middle, bf16[3,128,2048]{2,1,0:T(8,128)(2,1)} %copy-done.3, ...), custom_call_target="tpu_custom_call" | custom-call | flops 1000000000 | bytes 31457280 | tf_op jit(solution)/shard_map/finish/pallas_call | solution.py:1178
  397.7 0.0 copy-start.16
  397.7 1.2 slice_bitcast_fusion.1
  398.9 1.4 slice.79
  400.3 1.7 fusion.1
  402.0 1.9 slice_bitcast_fusion
  403.9 1.6 slice.89
  405.4 0.9 fusion.3
  406.3 1.7 fusion.4
  408.0 0.0 copy-done.17
  408.1 0.9 pad_maximum_fusion
  408.9 0.0 copy-done.16
  408.9 0.8 copy.38
  409.7 0.0 copy-start.18
  409.7 0.0 copy-start.1
  409.7 9.0 %copy.39 = bf16[17,128,2048]{2,1,0:T(8,128)(2,1)} copy(bf16[17,128,2048]{2,1,0:T(8,128)(2,1)} %get-tuple-element.114) | data formatting | bytes 17825792
  418.7 0.0 copy-done.18
  418.7 0.8 copy.40
  419.5 0.0 copy-done.1
  (1 shorter events, 0.0 us)
Async XLA Ops:
  0.6 0.7 copy-start
  6.6 17.2 %copy-start.4 = (f32[3,2048]{1,0:T(4,128)}, f32[3,2048]{1,0:T(4,128)S(1)}, u32[]{:S(2)}) copy-start(f32[3,2048]{1,0:T(4,128)S(1)} %pad_maximum_fusion.2.gains) | copy-start | bytes 73732
  9.9 0.8 copy-start.6
  10.7 0.7 copy-start.9
  11.4 0.7 copy-start.10
  12.1 11.7 %copy-start.2 = (f32[2048,68]{1,0:T(8,128)}, f32[2048,68]{1,0:T(8,128)S(1)}, u32[]{:S(2)}) copy-start(f32[2048,68]{1,0:T(8,128)S(1)} %copy.33.mix_first) | copy-start | bytes 1671172
  12.1 15.2 %copy-start.12 = (bf16[2048,128]{1,0:T(8,128)(2,1)S(1)}, bf16[2048,128]{1,0:T(8,128)(2,1)}, u32[]{:S(2)}) copy-start(bf16[2048,128]{1,0:T(8,128)(2,1)} %w_query.1) | copy-start | bytes 1572868
  12.1 15.2 %copy-start.13 = (bf16[2048,128]{1,0:T(8,128)(2,1)S(1)}, bf16[2048,128]{1,0:T(8,128)(2,1)}, u32[]{:S(2)}) copy-start(bf16[2048,128]{1,0:T(8,128)(2,1)} %w_key.1) | copy-start | bytes 1572868
  12.1 15.2 %copy-start.14 = (bf16[2048,128]{1,0:T(8,128)(2,1)S(1)}, bf16[2048,128]{1,0:T(8,128)(2,1)}, u32[]{:S(2)}) copy-start(bf16[2048,128]{1,0:T(8,128)(2,1)} %w_value.1) | copy-start | bytes 1572868
  12.1 15.2 %copy-start.15 = (bf16[128,2048]{1,0:T(8,128)(2,1)S(1)}, bf16[128,2048]{1,0:T(8,128)(2,1)}, u32[]{:S(2)}) copy-start(bf16[128,2048]{1,0:T(8,128)(2,1)} %w_output.1) | copy-start | bytes 1572868
  23.7 1.1 copy-start.3
  24.9 0.7 copy-start.5
  25.6 0.6 copy-start.8
  26.2 1.0 copy-start.11
  27.2 69.3 %copy-start.7 = (f32[128,68]{1,0:T(8,128)}, f32[128,68]{1,0:T(8,128)S(1)}, u32[]{:S(2)}) copy-start(f32[128,68]{1,0:T(8,128)S(1)} %get-tuple-element.66.mix) | copy-start | bytes 104452
  332.4 75.6 %copy-start.17 = (f32[512,256]{1,0:T(8,128)S(1)}, f32[512,256]{1,0:T(8,128)}, u32[]{:S(2)}) copy-start(f32[512,256]{1,0:T(8,128)} %get-tuple-element.76) | copy-start | bytes 1572868
  397.7 11.3 %copy-start.16 = (bf16[128,2048]{1,0:T(8,128)(2,1)S(1)}, bf16[128,2048]{1,0:T(8,128)(2,1)}, u32[]{:S(2)}) copy-start(bf16[128,2048]{1,0:T(8,128)(2,1)} %get-tuple-element.113) | copy-start | bytes 1572868
  409.7 9.0 %copy-start.18 = (f32[512,256]{1,0:T(8,128)S(1)}, f32[512,256]{1,0:T(8,128)}, u32[]{:S(2)}) copy-start(f32[512,256]{1,0:T(8,128)} %get-tuple-element.128) | copy-start | bytes 1572868
  409.7 9.8 %copy-start.1 = (s32[8,4]{0,1:T(4,128)S(1)}, s32[8,4]{0,1:T(4,128)}, u32[]{:S(2)}) copy-start(s32[8,4]{0,1:T(4,128)} %param.19) | copy-start | bytes 388
